TPU v7x, 256 devices: a whole 4x4x8 slice. The times are simulated.
256 devices in a mesh: adapter: 32 (over x, z), seq: 8 (over y, core).
Axes of the slice: x: 4, y: 4, z: 8, core: 2. Of those that a mesh axis runs over, the one named last changes fastest.
Arguments:
- tokens: bfloat16 [32768, 8192], P('adapter', 'seq'), may hold values from -6 to 6
- frozen_weight: bfloat16 [8192, 1024], P('seq'), may hold values from -0.0625 to 0.0625
- saved_mid: bfloat16 [32768, 128], P(('adapter', 'seq')), may hold values from -6 to 6
- cotangent: bfloat16 [32768, 1024], P('adapter', 'seq'), may hold values from -0.059814453 to 0.059814453
- up_stack: bfloat16 [32, 128, 1024], P(None, None, 'seq'), may hold values from -0.5 to 0.5
- block_job: int32 [256, 1], P('adapter'), may hold values from 0 to 31; in each aligned block of 8 rows (0 to 7, 8 to 15, ...) no two rows name the same one
- block_fill: int32 [256], P('adapter'), may hold values from 1 to 128
- slot_of: int32 [32], replicated, may hold values from 0 to 31, each once
Outputs:
- keys: bfloat16 [32768, 1024], P(('adapter', 'seq'))
- grad_down: float32 [32, 8192, 128], P('adapter', 'seq')
- grad_up: float32 [32, 128, 1024], P('adapter', None, 'seq')
Inputs may be any that keep to these rules, and one draw needn't show every extreme that they name: `block_job`: within each aligned run of 8 blocks no adapter id appears twice. `slot_of`: each slot holds exactly one adapter.
All inputs are finite; a program needn't handle non-finite values.
Results may differ from a plain program's by a relative error of at most 0.0029.
Values may be sent and summed in bfloat16 or wider, within the bound.
No kernel may reach another device: no remote copies, remote signals or barrier semaphores. Data moves between devices by JAX's collectives and lax.ppermute only.
A program may use at most 128 MiB of HBM per device.

v0:
```python
import jax
import jax.numpy as jnp
from jax import lax
from jax.sharding import PartitionSpec as P

BLK = 128


ADAPTER_SCALE = 2.0


def per_device(
    tokens, frozen_weight, saved_mid, cotangent, up_stack, block_job, block_fill, slot_of
):
    group_token_rows, width_part = tokens.shape
    feature_slice_part = cotangent.shape[1]
    rank_width = saved_mid.shape[1]
    nblocks = block_job.shape[0]
    adapter_count = slot_of.shape[0]
    jobs = block_job[:, 0]
    picked_adapter = jnp.take(up_stack, jobs, axis=0)
    position = lax.broadcasted_iota(jnp.int32, (nblocks, BLK), 1)
    validity = (position < block_fill[:, None]).astype(jnp.bfloat16)
    grad_blocks = cotangent.reshape(nblocks, BLK, feature_slice_part) * validity[:, :, None]
    mid_partial = jnp.einsum(
        "nbc,nrc->nbr", grad_blocks, picked_adapter, preferred_element_type=jnp.float32
    )
    mid_partial = mid_partial.reshape(group_token_rows, rank_width)
    mid_rows = lax.all_gather(saved_mid, "seq", axis=0, tiled=True)
    mid_grad = lax.psum(mid_partial, "seq").astype(jnp.bfloat16)
    middle_blocks = mid_rows.reshape(nblocks, BLK, rank_width)
    adapter_output = ADAPTER_SCALE * jnp.einsum(
        "axk,aky->axy", middle_blocks, picked_adapter, preferred_element_type=jnp.float32
    )
    adapter_output = adapter_output.reshape(group_token_rows, feature_slice_part)
    column_offset = lax.axis_index("seq") * feature_slice_part
    frozen_output = jnp.dot(tokens, frozen_weight, preferred_element_type=jnp.float32)
    middle_product = (
        lax.dynamic_slice_in_dim(frozen_output, column_offset, feature_slice_part, 1)
        + adapter_output
    )
    keys = lax.psum_scatter(
        lax.dynamic_update_slice_in_dim(frozen_output, middle_product, column_offset, 1),
        "seq",
        scatter_dimension=0,
        tiled=True,
    ).astype(jnp.bfloat16)
    token_blocks = tokens.reshape(nblocks, BLK, width_part)
    grad_mid_blocks = mid_grad.reshape(nblocks, BLK, rank_width)
    slot_blocks = jnp.take(slot_of, jobs)
    owned = adapter_count // lax.axis_size("adapter")
    selector = lax.broadcasted_iota(jnp.int32, (adapter_count, nblocks), 0) == slot_blocks[None, :]
    selector_half = selector.astype(jnp.bfloat16)
    send_tokens = jnp.einsum(
        "kn,nbd->kbd", selector_half, token_blocks, preferred_element_type=jnp.float32
    ).astype(jnp.bfloat16)
    send_grad = jnp.einsum(
        "kn,nbr->kbr", selector_half, grad_mid_blocks, preferred_element_type=jnp.float32
    ).astype(jnp.bfloat16)
    send_saved = jnp.einsum(
        "kn,nbr->kbr", selector_half, middle_blocks, preferred_element_type=jnp.float32
    ).astype(jnp.bfloat16)
    send_cotangent = jnp.einsum(
        "kn,nbc->kbc", selector_half, grad_blocks, preferred_element_type=jnp.float32
    ).astype(jnp.bfloat16)
    got_tokens, got_grad, got_saved, got_cotangent = (
        lax.all_to_all(send_tokens, "adapter", split_axis=0, concat_axis=0, tiled=True),
        lax.all_to_all(send_grad, "adapter", split_axis=0, concat_axis=0, tiled=True),
        lax.all_to_all(send_saved, "adapter", split_axis=0, concat_axis=0, tiled=True),
        lax.all_to_all(send_cotangent, "adapter", split_axis=0, concat_axis=0, tiled=True),
    )
    sources = got_tokens.shape[0] // owned
    got_tokens = got_tokens.reshape(sources, owned, BLK, width_part)
    got_grad = got_grad.reshape(sources, owned, BLK, rank_width)
    got_saved = got_saved.reshape(sources, owned, BLK, rank_width)
    got_cotangent = got_cotangent.reshape(sources, owned, BLK, feature_slice_part)
    grad_down = ADAPTER_SCALE * jnp.einsum(
        "skbd,skbr->kdr", got_tokens, got_grad, preferred_element_type=jnp.float32
    )
    grad_up = ADAPTER_SCALE * jnp.einsum(
        "skbr,skbc->krc", got_saved, got_cotangent, preferred_element_type=jnp.float32
    )
    return (keys, grad_down, grad_up)


def solution(mesh):
    placed = (
        P("adapter", "seq"),
        P("seq", None),
        P(("adapter", "seq"), None),
        P("adapter", "seq"),
        P(None, None, "seq"),
        P("adapter", None),
        P("adapter"),
        P(),
    )
    return jax.shard_map(
        per_device,
        mesh=mesh,
        in_specs=placed,
        out_specs=(
            P(("adapter", "seq"), None),
            P("adapter", "seq", None),
            P("adapter", None, "seq"),
        ),
        check_vma=False,
    )
```

profile of v0, /device:TPU:28, one launch (start us, length us, event | category | flops | bytes accessed | tf_op | source)
XLA Modules:
  0.0 358.3 jit_solution(18002397302381472165)
XLA Ops:
  7.2 0.8 fusion.25
  8.0 1.8 gather_fusion
  9.8 1.4 gather_fusion.1
  11.2 0.7 broadcast_select_fusion.3
  11.9 0.7 fusion.22
  12.6 1.1 broadcast_multiply_fusion
  13.8 0.7 copy-done.1
  14.9 28.1 %all-reduce.1 = bf16[1024,128]{1,0:T(8,128)(2,1)S(1)} all-reduce(f32[1024,128]{1,0:T(8,128)S(1)} %bitcast.47), channel_id=1, replica_groups=mesh['adapter'=32,'seq'=8] {'seq'}, use_global_device_ids=true, to_apply=%region_1.2 | all-reduce | flops 131072 | bytes 786432 | tf_op jit(solution)/shard_map/psum | solution.py:30
  42.9 0.4 fusion.10
  43.4 1.4 copy.30
  44.7 11.6 %all-to-all-start.1 = ((bf16[32,128,128]{2,1,0:T(8,128)(2,1)}), bf16[32,128,128]{2,1,0:T(8,128)(2,1)}, u32[]{:S(2)}, u32[]{:S(2)}) async-start(bf16[32,128,128]{2,1,0:T(8,128)(2,1)} %copy.30), calls=%async_computation.2 | async-start | bytes 2097152 | tf_op jit(solution)/shard_map/all_to_all | solution.py:68
  56.4 13.4 %all_gather.3 = bf16[1024,128]{1,0:T(8,128)(2,1)S(1)} all-gather(bf16[128,128]{1,0:T(8,128)(2,1)S(1)} %copy-done.3), channel_id=1, replica_groups=mesh['adapter'=32,'seq'=8] {'seq'}, dimensions={0}, use_global_device_ids=true | all-gather | bytes 294912 | tf_op jit(solution)/shard_map/all_gather | solution.py:29
  69.8 0.4 fusion.8
  70.2 1.7 copy.16
  71.9 11.4 %all-to-all-done.1 = bf16[32,128,128]{2,1,0:T(8,128)(2,1)} async-done(((bf16[32,128,128]{2,1,0:T(8,128)(2,1)}), bf16[32,128,128]{2,1,0:T(8,128)(2,1)}, u32[]{:S(2)}, u32[]{:S(2)}) %all-to-all-start.1) | async-done | bytes 1048608 | tf_op jit(solution)/shard_map/all_to_all | solution.py:68
  83.3 7.9 %all-to-all-start.2 = ((bf16[32,128,128]{1,2,0:T(8,128)(2,1)}), bf16[32,128,128]{1,2,0:T(8,128)(2,1)S(1)}, u32[]{:S(2)}, u32[]{:S(2)}) async-start(bf16[32,128,128]{1,2,0:T(8,128)(2,1)} %copy.16), calls=%async_computation.3 | async-start | bytes 2097152 | tf_op jit(solution)/shard_map/all_to_all | solution.py:69
  91.2 1.4 fusion.6
  92.6 1.4 copy.29
  94.0 23.5 %all-to-all-done.2 = bf16[32,128,128]{1,2,0:T(8,128)(2,1)S(1)} async-done(((bf16[32,128,128]{1,2,0:T(8,128)(2,1)}), bf16[32,128,128]{1,2,0:T(8,128)(2,1)S(1)}, u32[]{:S(2)}, u32[]{:S(2)}) %all-to-all-start.2) | async-done | bytes 1048608 | tf_op jit(solution)/shard_map/all_to_all | solution.py:69
  117.5 7.7 %all-to-all-start.3 = ((bf16[32,128,128]{2,1,0:T(8,128)(2,1)}), bf16[32,128,128]{2,1,0:T(8,128)(2,1)}, u32[]{:S(2)}, u32[]{:S(2)}) async-start(bf16[32,128,128]{2,1,0:T(8,128)(2,1)} %copy.29), calls=%async_computation.4 | async-start | bytes 2097152 | tf_op jit(solution)/shard_map/all_to_all | solution.py:70
  125.2 5.6 %fusion = bf16[32,128,1024]{2,0,1:T(8,128)(2,1)} fusion(bf16[8,128,1024]{2,1,0:T(8,128)(2,1)S(1)} %bitcast.44, s32[8]{0:T(128)S(1)} %get-tuple-element.3), kind=kOutput, calls=%fused_computation.4 | convolution fusion | flops 67109120 | bytes 10485792 | tf_op jit(solution)/shard_map/kn,nbd->kbd/dot_general | solution.py:54
  130.8 12.1 %copy.12 = bf16[32,128,1024]{1,2,0:T(8,128)(2,1)} copy(bf16[32,128,1024]{2,0,1:T(8,128)(2,1)} %fusion) | data formatting | bytes 16777216 | tf_op jit(solution)/shard_map/kn,nbd->kbd/dot_general | solution.py:54
  142.8 8.2 %all-to-all-done.3 = bf16[32,128,128]{2,1,0:T(8,128)(2,1)} async-done(((bf16[32,128,128]{2,1,0:T(8,128)(2,1)}), bf16[32,128,128]{2,1,0:T(8,128)(2,1)}, u32[]{:S(2)}, u32[]{:S(2)}) %all-to-all-start.3) | async-done | bytes 1048608 | tf_op jit(solution)/shard_map/all_to_all | solution.py:70
  151.0 7.5 %all-to-all-start = ((bf16[32,128,1024]{1,2,0:T(8,128)(2,1)}), bf16[32,128,1024]{1,2,0:T(8,128)(2,1)}, u32[]{:S(2)}, u32[]{:S(2)}) async-start(bf16[32,128,1024]{1,2,0:T(8,128)(2,1)} %copy.12), calls=%async_computation.1 | async-start | bytes 16777216 | tf_op jit(solution)/shard_map/all_to_all | solution.py:67
  158.7 1.2 convolution_multiply_fusion
  160.0 5.9 %fusion.26 = f32[1024,1024]{1,0:T(8,128)} fusion(bf16[1024,1024]{1,0:T(8,128)(2,1)S(1)} %copy-done, bf16[1024,1024]{1,0:T(8,128)(2,1)} %param.9), kind=kOutput, calls=%fused_computation.39 | convolution fusion | flops 2147483648 | bytes 8388608 | tf_op jit(solution)/shard_map/dot_general | solution.py:37
  165.9 1.9 constant_dynamic-update-slice_fusion
  167.8 2.3 fusion.5
  170.1 36.2 %reduce-scatter.2.cloned.1.call-done = f32[128,1024]{1,0:T(8,128)} async-done(((f32[1024,1024]{1,0:T(8,128)}), f32[128,1024]{1,0:T(8,128)}) %reduce-scatter.2.cloned.1.call-update) | async-done | bytes 524304 | tf_op jit(solution)/shard_map/reduce_scatter | solution.py:42
  206.3 1.8 convert_element_type.26
  208.1 136.6 %all-to-all-done = bf16[32,128,1024]{1,2,0:T(8,128)(2,1)} async-done(((bf16[32,128,1024]{1,2,0:T(8,128)(2,1)}), bf16[32,128,1024]{1,2,0:T(8,128)(2,1)}, u32[]{:S(2)}, u32[]{:S(2)}) %all-to-all-start) | async-done | bytes 8388640 | tf_op jit(solution)/shard_map/all_to_all | solution.py:67
  344.7 6.7 %fusion.3 = f32[1,1024,128]{2,1,0:T(8,128)} fusion(bf16[32,128,1024]{1,2,0:T(8,128)(2,1)} %all-to-all-done, bf16[32,128,128]{2,1,0:T(8,128)(2,1)} %all-to-all-done.1), kind=kOutput, calls=%fused_computation.8 | convolution fusion | flops 1073872896 | bytes 9961472 | tf_op jit(solution)/shard_map/skbd,skbr->kdr/dot_general | solution.py:77
  (11 shorter events, 0.6 us)
Async XLA Ops:
  7.2 118.0 %copy-start = (bf16[1024,1024]{1,0:T(8,128)(2,1)S(1)}, bf16[1024,1024]{1,0:T(8,128)(2,1)}, u32[]{:S(2)}) copy-start(bf16[1024,1024]{1,0:T(8,128)(2,1)} %param.8) | copy-start | bytes 6291460
  9.8 34.9 %copy-start.2 = (bf16[8,128,128]{2,1,0:T(8,128)(2,1)}, bf16[8,128,128]{2,1,0:T(8,128)(2,1)S(1)}, u32[]{:S(2)}) copy-start(bf16[8,128,128]{2,1,0:T(8,128)(2,1)S(1)} %gather_fusion) | copy-start | bytes 786436
  9.8 46.6 %copy-start.3 = (bf16[128,128]{1,0:T(8,128)(2,1)S(1)}, bf16[128,128]{1,0:T(8,128)(2,1)}, u32[]{:S(2)}) copy-start(bf16[128,128]{1,0:T(8,128)(2,1)} %param.10) | copy-start | bytes 98308
  13.8 0.7 copy-start.1
  44.7 38.5 %all-to-all-start.1 = ((bf16[32,128,128]{2,1,0:T(8,128)(2,1)}), bf16[32,128,128]{2,1,0:T(8,128)(2,1)}, u32[]{:S(2)}, u32[]{:S(2)}) async-start(bf16[32,128,128]{2,1,0:T(8,128)(2,1)} %copy.30), calls=%async_computation.2 | async-start | bytes 2097152 | tf_op jit(solution)/shard_map/all_to_all | solution.py:68
  83.3 34.2 %all-to-all-start.2 = ((bf16[32,128,128]{1,2,0:T(8,128)(2,1)}), bf16[32,128,128]{1,2,0:T(8,128)(2,1)S(1)}, u32[]{:S(2)}, u32[]{:S(2)}) async-start(bf16[32,128,128]{1,2,0:T(8,128)(2,1)} %copy.16), calls=%async_computation.3 | async-start | bytes 2097152 | tf_op jit(solution)/shard_map/all_to_all | solution.py:69
  117.5 33.5 %all-to-all-start.3 = ((bf16[32,128,128]{2,1,0:T(8,128)(2,1)}), bf16[32,128,128]{2,1,0:T(8,128)(2,1)}, u32[]{:S(2)}, u32[]{:S(2)}) async-start(bf16[32,128,128]{2,1,0:T(8,128)(2,1)} %copy.29), calls=%async_computation.4 | async-start | bytes 2097152 | tf_op jit(solution)/shard_map/all_to_all | solution.py:70
  151.0 193.7 %all-to-all-start = ((bf16[32,128,1024]{1,2,0:T(8,128)(2,1)}), bf16[32,128,1024]{1,2,0:T(8,128)(2,1)}, u32[]{:S(2)}, u32[]{:S(2)}) async-start(bf16[32,128,1024]{1,2,0:T(8,128)(2,1)} %copy.12), calls=%async_computation.1 | async-start | bytes 16777216 | tf_op jit(solution)/shard_map/all_to_all | solution.py:67
  158.5 47.8 %reduce-scatter.2.cloned.1.call-start = ((), (), s32[]{:S(2)}) async-start(), calls=%async_computation.5 | async-start | bytes 4718592 | tf_op jit(solution)/shard_map/reduce_scatter | solution.py:42
Sparse Core Ops, SparseCore 0:
  167.9 38.3 reduce-scatter.1
where the time goes:
time: 359 us; the launch traced here: 358 us
  waiting for transfers between devices  216 us (60%)
  blocking collectives  41.5 us (12%)
  starting transfers between devices  34.9 us (10%)
  matrix products  24.3 us (7%)
  local copies, waits for them, and re-layouts  20.5 us (6%)
  between operations  14.2 us (4%)
  other arithmetic  7.06 us (2%)
    all_to_all x1, waiting for transfers between devices, per_device(): lax.all_to_all(send_tokens, 'adapter', split_axis=0, concat_axis=0, tiled...  137 us
    reduce_scatter x1, waiting for transfers between devices, per_device(): lax.psum_scatter(lax.dynamic_update_slice_in_dim(frozen_output, middle_pr...  36.2 us
    psum x1, blocking collectives, per_device(): mid_grad = lax.psum(mid_partial, 'seq').astype(jnp.bfloat16)  28.1 us
    all_to_all x1, waiting for transfers between devices, per_device(): lax.all_to_all(send_saved, 'adapter', split_axis=0, concat_axis=0, tiled=...  23.5 us
    all_gather x1, blocking collectives, per_device(): mid_rows = lax.all_gather(saved_mid, 'seq', axis=0, tiled=True)  13.4 us
    dot_general x1, local copies, waits for them, and re-layouts, per_device(): jnp.einsum('kn,nbd->kbd', selector_half, token_blocks, preferred_element_...  12.1 us
    all_to_all x1, starting transfers between devices, per_device(): lax.all_to_all(send_grad, 'adapter', split_axis=0, concat_axis=0, tiled=T...  11.6 us
    all_to_all x1, waiting for transfers between devices, per_device(): lax.all_to_all(send_grad, 'adapter', split_axis=0, concat_axis=0, tiled=T...  11.4 us
  transfers between devices with their start and end apart: 5, of which 5 were waited for; matrix products, arithmetic and copies ran while one was open for 10% of the time, Pallas kernels for 0%

commit v1 on v0

v1 whole, which is shorter than its diff:
```python
import jax
import jax.numpy as jnp
from jax import lax
from jax.experimental import pallas as pl
from jax.experimental.pallas import tpu as pltpu
from jax.sharding import Mesh, PartitionSpec as P

BLK = 128
ADAPTER_SCALE = 2.0
SEQ = ("y", "core")


def slot_sums(slots, token_parts, mids, up_parts, slot_count):
    groups, blocks, rows, width = token_parts.shape
    rank = mids.shape[-1]
    up_rows = up_parts.shape[2]

    def kernel(slots_ref, tokens_ref, mids_ref, up_ref, out_ref, acc):
        acc[...] = jnp.zeros_like(acc)
        for g in range(groups):
            for b in range(blocks):
                slot = slots_ref[g, b]
                acc[slot, :width] += lax.dot_general(
                    tokens_ref[g, b],
                    mids_ref[b, g],
                    (((0,), (0,)), ((), ())),
                    preferred_element_type=jnp.float32,
                )
                acc[slot, width:] += up_ref[g, b].astype(jnp.float32)
        out_ref[...] = acc[...].astype(out_ref.dtype)

    vmem = pl.BlockSpec(memory_space=pltpu.VMEM)
    return pl.pallas_call(
        kernel,
        out_shape=jax.ShapeDtypeStruct((slot_count, width + up_rows, rank), jnp.bfloat16),
        in_specs=[pl.BlockSpec(memory_space=pltpu.SMEM), vmem, vmem, vmem],
        out_specs=vmem,
        scratch_shapes=[pltpu.VMEM((slot_count, width + up_rows, rank), jnp.float32)],
        compiler_params=pltpu.CompilerParams(vmem_limit_bytes=32 * 1024 * 1024),
    )(slots, token_parts, mids, up_parts)


def per_device(
    tokens, frozen_weight, saved_mid, cotangent, up_stack, block_job, block_fill, slot_of
):
    rows, width = tokens.shape
    features = cotangent.shape[1]
    rank = saved_mid.shape[1]
    nblocks = block_job.shape[0]
    slot_count = slot_of.shape[0]
    nx, nz = lax.axis_size("x"), lax.axis_size("z")
    bf16, f32 = jnp.bfloat16, jnp.float32
    jobs = block_job[:, 0]

    with jax.named_scope("tokens_over_z"):
        token_parts = lax.all_to_all(tokens, "z", split_axis=1, concat_axis=0, tiled=True)
        token_parts = token_parts.reshape(nz, nblocks, BLK, width // nz)

    with jax.named_scope("mid_sums"):
        picked = jnp.take(up_stack, jobs, axis=0)
        position = lax.broadcasted_iota(jnp.int32, (nblocks, BLK), 1)
        validity = (position < block_fill[:, None]).astype(bf16)
        grad_blocks = cotangent.reshape(nblocks, BLK, features) * validity[:, :, None]
        mid_partial = jnp.einsum("nbc,nrc->nbr", grad_blocks, picked, preferred_element_type=f32)
        high = lax.reduce_precision(mid_partial, exponent_bits=8, mantissa_bits=7)
        low = (mid_partial - high).astype(bf16)
        own_saved = jnp.broadcast_to(saved_mid[None], (nblocks, BLK, rank))
        sent = jnp.concatenate([high.astype(bf16), low, own_saved], axis=1)
        got = lax.all_to_all(sent, SEQ, split_axis=0, concat_axis=0, tiled=True)
        mid_grad = jnp.sum(got[:, : 2 * BLK].astype(f32).reshape(-1, BLK, rank), axis=0).astype(bf16)
        saved_blocks = got[:, 2 * BLK :]

    with jax.named_scope("mid_gather"):
        slots = jnp.take(slot_of, jobs)
        slot_rows = jnp.broadcast_to(
            jnp.pad(slots.astype(bf16), (0, rank - nblocks))[None], (16, rank)
        )
        column = lax.all_gather(jnp.concatenate([mid_grad, slot_rows], axis=0), "z", axis=0)
        column_slots = column[:, BLK, :nblocks].astype(jnp.int32)
        mids = lax.all_gather(column[:, :BLK], SEQ, axis=0)

    with jax.named_scope("up_over_z"):
        up_terms = jnp.einsum("nbr,nbc->nrc", saved_blocks, grad_blocks, preferred_element_type=f32)
        up_parts = lax.all_to_all(up_terms.astype(bf16), "z", split_axis=1, concat_axis=0, tiled=True)
        up_parts = up_parts.reshape(nz, nblocks, rank // nz, features)

    with jax.named_scope("keys"):
        adapter_output = ADAPTER_SCALE * jnp.einsum(
            "axk,aky->axy", saved_blocks, picked, preferred_element_type=f32
        ).reshape(rows, features)
        column_offset = lax.axis_index(SEQ) * features
        frozen_output = jnp.dot(tokens, frozen_weight, preferred_element_type=f32)
        middle = lax.dynamic_slice_in_dim(frozen_output, column_offset, features, 1) + adapter_output
        keys = lax.psum_scatter(
            lax.dynamic_update_slice_in_dim(frozen_output, middle, column_offset, 1),
            SEQ,
            scatter_dimension=0,
            tiled=True,
        ).astype(bf16)

    with jax.named_scope("slot_sums"):
        sums = slot_sums(column_slots, token_parts, mids, up_parts, slot_count)

    with jax.named_scope("sums_over_x"):
        over_x = lax.all_to_all(sums, "x", split_axis=0, concat_axis=0, tiled=True)
        over_x = over_x.reshape(nx, nz, -1, rank)
        totals = ADAPTER_SCALE * jnp.sum(over_x.astype(f32), axis=0)
    with jax.named_scope("totals_over_z"):
        owned = lax.all_to_all(totals, "z", split_axis=0, concat_axis=0, tiled=True)
        split = width // nz
        grad_down = owned[:, :split].reshape(1, width, rank)
        grad_up = owned[:, split:].reshape(1, rank, features)
    return (keys, grad_down, grad_up)


def solution(mesh):
    chips = Mesh(mesh.devices.reshape(4, 8, 4, 2), ("x", "z", "y", "core"))
    adapter = ("x", "z")
    return jax.shard_map(
        per_device,
        mesh=chips,
        in_specs=(
            P(adapter, SEQ),
            P(SEQ, None),
            P(adapter + SEQ, None),
            P(adapter, SEQ),
            P(None, None, SEQ),
            P(adapter, None),
            P(adapter),
            P(),
        ),
        out_specs=(
            P(adapter + SEQ, None),
            P(adapter, SEQ, None),
            P(adapter, None, SEQ),
        ),
        check_vma=False,
    )
```

time: 359 us -> 183 us (0.51)
  the two profiles are of different devices: /device:TPU:28 before, /device:TPU:32 now
where the time goes in v1:
time: 183 us; the launch traced here: 182 us
  waiting for transfers between devices  62.9 us (34%)
  blocking collectives  59.7 us (33%)
  starting transfers between devices  16.1 us (9%)
  between operations  14.2 us (8%)
  local copies, waits for them, and re-layouts  10.6 us (6%)
  matrix products  8.06 us (4%)
  other arithmetic  7.22 us (4%)
  Pallas kernels  2.75 us (2%)
    all_to_all x1, waiting for transfers between devices, per_device(): lax.all_to_all(tokens, 'z', split_axis=1, concat_axis=0, tiled=True)  42.5 us
    all_gather x1, blocking collectives, per_device(): lax.all_gather(jnp.concatenate([mid_grad, slot_rows], axis=0), 'z', axis=0)  27.6 us
    all_to_all x1, blocking collectives, per_device(): owned = lax.all_to_all(totals, 'z', split_axis=0, concat_axis=0, tiled=True)  16.5 us
    all_to_all x1, blocking collectives, per_device(): over_x = lax.all_to_all(sums, 'x', split_axis=0, concat_axis=0, tiled=True)  15.7 us
    all_to_all x1, waiting for transfers between devices, per_device(): got = lax.all_to_all(sent, SEQ, split_axis=0, concat_axis=0, tiled=True)  13.1 us
    all_to_all x1, waiting for transfers between devices, per_device(): lax.all_to_all(up_terms.astype(bf16), 'z', split_axis=1, concat_axis=0, t...  7.27 us
    dot_general x1, matrix products, per_device(): frozen_output = jnp.dot(tokens, frozen_weight, preferred_element_type=f32)  5.92 us
    all_to_all x1, starting transfers between devices, per_device(): lax.all_to_all(up_terms.astype(bf16), 'z', split_axis=1, concat_axis=0, t...  5.83 us
  transfers between devices with their start and end apart: 5, of which 3 were waited for; matrix products, arithmetic and copies ran while one was open for 7% of the time, Pallas kernels for 2%

profile of v1, /device:TPU:32, one launch (start us, length us, event | category | flops | bytes accessed | tf_op | source)
XLA Modules:
  0.0 181.5 jit_solution(13752900202059481084)
XLA Ops:
  7.2 0.8 fusion.11
  8.0 0.7 fusion.8
  8.7 1.3 gather_fusion.1
  10.0 0.7 select_convert_fusion
  10.7 1.8 %gather_fusion = bf16[8,128,128]{2,1,0:T(8,128)(2,1)S(1)} fusion(bf16[32,128,128]{2,1,0:T(8,128)(2,1)} %param.12, s32[1024]{0:T(1024)S(1)} %pad_clamp_fusion), kind=kCustom, calls=%fused_computation | custom fusion | bytes 524320 | tf_op jit(solution)/shard_map/mid_sums/jit(_take)/gather | solution.py:60
  12.5 1.4 reduce-precision_convert_fusion
  14.0 0.9 pad_maximum_fusion
  15.0 4.5 %all-to-all-start = ((bf16[8,384,128]{2,1,0:T(8,128)(2,1)}), bf16[8,384,128]{2,1,0:T(8,128)(2,1)S(1)}, u32[]{:S(2)}, u32[]{:S(2)}) async-start(bf16[8,384,128]{2,1,0:T(8,128)(2,1)} %pad_maximum_fusion), calls=%async_computation | async-start | bytes 1572864 | tf_op jit(solution)/shard_map/mid_sums/all_to_all | solution.py:69
  19.5 13.1 %all-to-all-done = bf16[8,384,128]{2,1,0:T(8,128)(2,1)S(1)} async-done(((bf16[8,384,128]{2,1,0:T(8,128)(2,1)}), bf16[8,384,128]{2,1,0:T(8,128)(2,1)S(1)}, u32[]{:S(2)}, u32[]{:S(2)}) %all-to-all-start) | async-done | bytes 786464 | tf_op jit(solution)/shard_map/mid_sums/all_to_all | solution.py:69
  32.6 0.1 reduce
  32.7 27.6 %all-gather = bf16[1152,128]{1,0:T(8,128)(2,1)S(1)} all-gather(bf16[144,128]{1,0:T(8,128)(2,1)S(1)} %pad_maximum_fusion.1), channel_id=2, replica_groups=mesh['x'=4,'z'=8,'y'=4,'core'=2] {'z'}, dimensions={0}, use_global_device_ids=true | all-gather | bytes 331776 | tf_op jit(solution)/shard_map/mid_gather/all_gather | solution.py:78
  60.3 0.7 slice.31
  61.1 0.0 reduce-scatter.2.cloned.1.call-start
  61.1 5.9 %fusion.12 = f32[1024,1024]{1,0:T(8,128)} fusion(bf16[1024,1024]{1,0:T(8,128)(2,1)S(1)} %copy-done, bf16[1024,1024]{1,0:T(8,128)(2,1)} %param.9), kind=kOutput, calls=%fused_computation.33 | convolution fusion | flops 2147483648 | bytes 8388608 | tf_op jit(solution)/shard_map/keys/dot_general | solution.py:92
  67.1 0.3 convolution_multiply_fusion
  67.4 2.0 %constant_dynamic-update-slice_fusion = f32[1024,1024]{1,0:T(8,128)} fusion(f32[1024,1024]{1,0:T(8,128)} %fusion.12, s32[]{:T(128)S(6)} %select_n.21, f32[8,128,128]{2,1,0:T(8,128)S(1)} %convolution_multiply_fusion), kind=kLoop, calls=%fused_computation.29 | loop fusion | flops 131072 | bytes 1572868 | tf_op jit(solution)/shard_map/keys/dynamic_update_slice | solution.py:95
  69.4 0.9 copy-done.4
  70.3 0.4 convolution_convert_fusion
  70.7 0.9 copy.19
  71.6 5.8 %all-to-all-start.2 = ((bf16[8,128,128]{2,0,1:T(8,128)(2,1)}), bf16[8,128,128]{2,0,1:T(8,128)(2,1)S(1)}, u32[]{:S(2)}, u32[]{:S(2)}) async-start(bf16[8,128,128]{2,0,1:T(8,128)(2,1)} %copy.19), calls=%async_computation.3 | async-start | bytes 524288 | tf_op jit(solution)/shard_map/up_over_z/all_to_all | solution.py:84
  77.4 1.8 copy_bitcast_fusion
  79.2 7.3 %all-to-all-done.2 = bf16[8,128,128]{2,0,1:T(8,128)(2,1)S(1)} async-done(((bf16[8,128,128]{2,0,1:T(8,128)(2,1)}), bf16[8,128,128]{2,0,1:T(8,128)(2,1)S(1)}, u32[]{:S(2)}, u32[]{:S(2)}) %all-to-all-start.2) | async-done | bytes 262176 | tf_op jit(solution)/shard_map/up_over_z/all_to_all | solution.py:84
  86.5 5.7 %all-to-all-start.1 = ((bf16[1024,8,128]{2,0,1:T(8,128)(2,1)}), bf16[1024,8,128]{2,0,1:T(8,128)(2,1)}, u32[]{:S(2)}, u32[]{:S(2)}) async-start(bf16[1024,8,128]{2,0,1:T(8,128)(2,1)} %copy_bitcast_fusion), calls=%async_computation.2 | async-start | bytes 4194304 | tf_op jit(solution)/shard_map/tokens_over_z/all_to_all | solution.py:56
  92.2 42.5 %all-to-all-done.1 = bf16[1024,8,128]{2,0,1:T(8,128)(2,1)} async-done(((bf16[1024,8,128]{2,0,1:T(8,128)(2,1)}), bf16[1024,8,128]{2,0,1:T(8,128)(2,1)}, u32[]{:S(2)}, u32[]{:S(2)}) %all-to-all-start.1) | async-done | bytes 2097184 | tf_op jit(solution)/shard_map/tokens_over_z/all_to_all | solution.py:56
  134.7 1.6 copy-done.1
  136.3 2.8 %slot_sums.1 = bf16[32,144,128]{2,1,0:T(8,128)(2,1)S(1)} custom-call(s32[8,8]{1,0:T(8,128)S(1)} %bitcast.32, bf16[8,8,128,128]{3,2,1,0:T(8,128)(2,1)} %bitcast.8.tokens_ref, bf16[8,8,128,128]{3,2,1,0:T(8,128)(2,1)S(1)} %bitcast.30, bf16[8,8,16,128]{3,2,1,0:T(8,128)(2,1)S(1)} %bitcast.31), custom_call_target="tpu_custom_call" | custom-call | tf_op jit(solution)/shard_map/slot_sums/pallas_call | solution.py:33
  139.1 15.7 %all_to_all.46 = bf16[32,144,128]{2,1,0:T(8,128)(2,1)S(1)} all-to-all(bf16[32,144,128]{2,1,0:T(8,128)(2,1)S(1)} %slot_sums.1), channel_id=1, replica_groups=mesh['x'=4,'z'=8,'y'=4,'core'=2] {'x'}, dimensions={0} | all-to-all | bytes 2359296 | tf_op jit(solution)/shard_map/sums_over_x/all_to_all | solution.py:105
  154.8 0.2 convert_reduce_fusion
  155.0 16.5 %all_to_all.47 = f32[8,144,128]{2,1,0:T(8,128)S(1)} all-to-all(f32[8,144,128]{2,1,0:T(8,128)S(1)} %broadcast_multiply_fusion), channel_id=1, replica_groups=mesh['x'=4,'z'=8,'y'=4,'core'=2] {'z'}, dimensions={0} | all-to-all | bytes 1179648 | tf_op jit(solution)/shard_map/totals_over_z/all_to_all | solution.py:109
  171.4 0.6 slice.33
  172.1 0.8 slice.32
  172.9 1.8 convert_element_type.42
  (24 shorter events, 0.3 us)
Async XLA Ops:
  7.2 54.0 %copy-start = (bf16[1024,1024]{1,0:T(8,128)(2,1)S(1)}, bf16[1024,1024]{1,0:T(8,128)(2,1)}, u32[]{:S(2)}) copy-start(bf16[1024,1024]{1,0:T(8,128)(2,1)} %param.8) | copy-start | bytes 6291460
  7.2 6.8 %copy-start.5 = (bf16[128,128]{1,0:T(8,128)(2,1)S(1)}, bf16[128,128]{1,0:T(8,128)(2,1)}, u32[]{:S(2)}) copy-start(bf16[128,128]{1,0:T(8,128)(2,1)} %param.10) | copy-start | bytes 98308
  12.5 2.4 %copy-start.2 = (bf16[8,128,128]{2,1,0:T(8,128)(2,1)}, bf16[8,128,128]{2,1,0:T(8,128)(2,1)S(1)}, u32[]{:S(2)}) copy-start(bf16[8,128,128]{2,1,0:T(8,128)(2,1)S(1)} %gather_fusion) | copy-start | bytes 786436
  15.0 17.6 %all-to-all-start = ((bf16[8,384,128]{2,1,0:T(8,128)(2,1)}), bf16[8,384,128]{2,1,0:T(8,128)(2,1)S(1)}, u32[]{:S(2)}, u32[]{:S(2)}) async-start(bf16[8,384,128]{2,1,0:T(8,128)(2,1)} %pad_maximum_fusion), calls=%async_computation | async-start | bytes 1572864 | tf_op jit(solution)/shard_map/mid_sums/all_to_all | solution.py:69
  19.4 115.3 %all-gather.4.cloned.1.call-start = ((), (), s32[]{:S(2)}) async-start(), calls=%async_computation.7 | async-start | bytes 2359296 | tf_op jit(solution)/shard_map/mid_gather/all_gather | solution.py:80
  61.1 111.8 %reduce-scatter.2.cloned.1.call-start = ((), (), s32[]{:S(2)}) async-start(), calls=%async_computation.6 | async-start | bytes 4718592 | tf_op jit(solution)/shard_map/keys/reduce_scatter | solution.py:94
  61.1 5.9 %copy-start.3 = (bf16[8,128,128]{2,1,0:T(8,128)(2,1)S(1)}, bf16[8,128,128]{2,1,0:T(8,128)(2,1)}, u32[]{:S(2)}) copy-start(bf16[8,128,128]{2,1,0:T(8,128)(2,1)} %copy-done.2) | copy-start | bytes 786436
  69.4 1.0 copy-start.4
  71.6 14.9 %all-to-all-start.2 = ((bf16[8,128,128]{2,0,1:T(8,128)(2,1)}), bf16[8,128,128]{2,0,1:T(8,128)(2,1)S(1)}, u32[]{:S(2)}, u32[]{:S(2)}) async-start(bf16[8,128,128]{2,0,1:T(8,128)(2,1)} %copy.19), calls=%async_computation.3 | async-start | bytes 524288 | tf_op jit(solution)/shard_map/up_over_z/all_to_all | solution.py:84
  86.5 48.2 %all-to-all-start.1 = ((bf16[1024,8,128]{2,0,1:T(8,128)(2,1)}), bf16[1024,8,128]{2,0,1:T(8,128)(2,1)}, u32[]{:S(2)}, u32[]{:S(2)}) async-start(bf16[1024,8,128]{2,0,1:T(8,128)(2,1)} %copy_bitcast_fusion), calls=%async_computation.2 | async-start | bytes 4194304 | tf_op jit(solution)/shard_map/tokens_over_z/all_to_all | solution.py:56
  134.7 1.6 copy-start.1
Sparse Core Ops, SparseCore 0:
  61.2 25.5 all-gather.3
  89.4 41.5 reduce-scatter.1

commit v2 on v1

v2 whole, which is shorter than its diff:
```python
import jax
import jax.numpy as jnp
from jax import lax
from jax.experimental import pallas as pl
from jax.experimental.pallas import tpu as pltpu
from jax.sharding import Mesh, PartitionSpec as P

BLK = 128
ADAPTER_SCALE = 2.0
SEQ = ("y", "core")
FIRST = ("x", "zp")
ADAPTER = ("x", "zq", "zp")
SLOT_ROWS = 16
LIMIT = pltpu.CompilerParams(vmem_limit_bytes=16 * 1024 * 1024)
WHOLE = pltpu.CompilerParams(vmem_limit_bytes=60 * 1024 * 1024)
VMEM = pl.BlockSpec(memory_space=pltpu.VMEM)
SMEM = pl.BlockSpec(memory_space=pltpu.SMEM)
HBM = pl.BlockSpec(memory_space=pltpu.HBM)
BF16 = jnp.bfloat16
F32 = jnp.float32


def shift(value, axis, distance):
    size = lax.axis_size(axis)
    return lax.ppermute(value, axis, [(i, (i + distance) % size) for i in range(size)])


def contract(left, right, left_dim, right_dim):
    return lax.dot_general(
        left, right, (((left_dim,), (right_dim,)), ((), ())), preferred_element_type=F32
    )


def masked(cot_ref, fill_ref, b):
    block = cot_ref[b * BLK : (b + 1) * BLK, :]
    position = lax.broadcasted_iota(jnp.int32, block.shape, 0)
    return jnp.where(position < fill_ref[b], block, jnp.zeros_like(block))


def mid_partials(place, jobs, fills, up_stack, cotangent):
    nblocks = jobs.shape[0]
    rank, features = up_stack.shape[1:]

    def kernel(place_ref, jobs_ref, fill_ref, up_ref, cot_ref, own_ref, other_ref, picked_ref, sems):
        copies = [
            pltpu.make_async_copy(up_ref.at[jobs_ref[b]], picked_ref.at[b], sems.at[b])
            for b in range(nblocks)
        ]
        for copy in copies:
            copy.start()
        core = place_ref[1]
        for pair in range(nblocks // 2):
            partials = []
            for b in (2 * pair, 2 * pair + 1):
                copies[b].wait()
                partials.append(contract(masked(cot_ref, fill_ref, b), picked_ref[b], 1, 1))
            own_ref[pair] = jnp.where(core == 0, partials[0], partials[1])
            other_ref[pair] = jnp.where(core == 0, partials[1], partials[0])

    half = jax.ShapeDtypeStruct((nblocks // 2, BLK, rank), F32)
    return pl.pallas_call(
        kernel,
        out_shape=[half, half, jax.ShapeDtypeStruct((nblocks, rank, features), BF16)],
        in_specs=[SMEM, SMEM, SMEM, HBM, VMEM],
        out_specs=[VMEM, VMEM, VMEM],
        scratch_shapes=[pltpu.SemaphoreType.DMA((nblocks,))],
        compiler_params=WHOLE,
        name="mid_partials",
    )(place, jobs, fills, up_stack, cotangent)


def y_payload(place, own, received, saved, saved_other):
    half, _, rank = own.shape

    def kernel(place_ref, own_ref, received_ref, saved_ref, saved_other_ref, keep_ref, out_ref):
        core = place_ref[1]
        first, second = saved_ref[...], saved_other_ref[...]
        out_ref[2 * half] = jnp.where(core == 0, first, second)
        out_ref[2 * half + 1] = jnp.where(core == 0, second, first)
        total = own_ref[...] + received_ref[...]
        keep_ref[...] = total
        high = total.astype(BF16)
        out_ref[:half] = high
        out_ref[half : 2 * half] = (total - high.astype(F32)).astype(BF16)

    return pl.pallas_call(
        kernel,
        out_shape=[
            jax.ShapeDtypeStruct((half, BLK, rank), F32),
            jax.ShapeDtypeStruct((2 * half + 2, BLK, rank), BF16),
        ],
        in_specs=[SMEM] + [VMEM] * 4,
        out_specs=[VMEM] * 2,
        compiler_params=LIMIT,
        name="y_payload",
    )(place, own, received, saved, saved_other)


def mid_grads(place, keep, sent, received):
    half, _, rank = keep.shape
    ny = len(received) + 1

    def kernel(place_ref, keep_ref, sent_ref, *refs):
        got = refs[: ny - 1]
        mids_ref, rows_ref = refs[ny - 1 :]
        y = place_ref[0]
        total = keep_ref[...]
        for ref in got:
            total += ref[:half].astype(F32) + ref[half : 2 * half].astype(F32)
        mids_ref[...] = total.astype(BF16)
        for d, ref in enumerate((sent_ref,) + got):
            source = lax.rem(y + ny - d, ny)
            rows_ref[2 * source] = ref[2 * half]
            rows_ref[2 * source + 1] = ref[2 * half + 1]

    return pl.pallas_call(
        kernel,
        out_shape=[
            jax.ShapeDtypeStruct((half, BLK, rank), BF16),
            jax.ShapeDtypeStruct((2 * half, BLK, rank), BF16),
        ],
        in_specs=[SMEM] + [VMEM] * (ny + 1),
        out_specs=[VMEM] * 2,
        compiler_params=LIMIT,
        name="mid_grads",
    )(place, keep, sent, *received)


def products(place, jobs, fills, slot_of, tokens, mids, mids_other, saved_rows, cotangent, parts):
    width = tokens.shape[1]
    nblocks, _, rank = saved_rows.shape
    part, split = width // parts, rank // parts
    height = part + split

    def kernel(
        place_ref, jobs_ref, fill_ref, slot_ref, tokens_ref, mids_ref, other_ref, saved_ref, cot_ref, out_ref
    ):
        core = place_ref[1]
        row = lax.broadcasted_iota(jnp.int32, (SLOT_ROWS, rank), 0)
        slots = jnp.zeros((SLOT_ROWS, rank), jnp.int32)
        for b in range(nblocks):
            slots = jnp.where(row == b, slot_ref[jobs_ref[b]], slots)
        slots = slots.astype(F32).astype(BF16)
        for i in range(parts):
            out_ref[i, nblocks * height :, :] = slots
        for b in range(nblocks):
            mine, other = mids_ref[b // 2], other_ref[b // 2]
            mid = jnp.where(core == b % 2, mine, other)
            up = contract(saved_ref[b], masked(cot_ref, fill_ref, b), 0, 0).astype(BF16)
            first = b * height
            for i in range(parts):
                block = tokens_ref[b * BLK : (b + 1) * BLK, i * part : (i + 1) * part]
                out_ref[i, first : first + part, :] = contract(block, mid, 0, 0).astype(BF16)
                out_ref[i, first + part : first + height, :] = up[i * split : (i + 1) * split]

    return pl.pallas_call(
        kernel,
        out_shape=jax.ShapeDtypeStruct((parts, nblocks * height + SLOT_ROWS, rank), BF16),
        in_specs=[SMEM] * 4 + [VMEM] * 5,
        out_specs=VMEM,
        compiler_params=LIMIT,
        name="products",
    )(place, jobs, fills, slot_of, tokens, mids, mids_other, saved_rows, cotangent)


def slot_sums(slots, terms, slot_count):
    groups, nblocks = slots.shape
    rank = terms.shape[2]
    height = (terms.shape[1] - SLOT_ROWS) // nblocks

    def kernel(slots_ref, terms_ref, out_ref, acc):
        acc[...] = jnp.zeros_like(acc)
        for g in range(groups):
            for b in range(nblocks):
                acc[slots_ref[g, b]] += terms_ref[g, b * height : (b + 1) * height, :].astype(F32)
        out_ref[...] = acc[...].astype(BF16)

    return pl.pallas_call(
        kernel,
        out_shape=jax.ShapeDtypeStruct((slot_count, height, rank), BF16),
        in_specs=[SMEM, VMEM],
        out_specs=VMEM,
        scratch_shapes=[pltpu.VMEM((slot_count, height, rank), F32)],
        compiler_params=LIMIT,
        name="slot_sums",
    )(slots, terms)


def finish(owned, part):
    nx, nq, npair, height, rank = owned.shape
    parts, split = nx * npair, height - part

    def kernel(owned_ref, down_ref, up_ref):
        for x in range(nx):
            for p in range(npair):
                total = owned_ref[x, 0, p].astype(F32)
                for q in range(1, nq):
                    total += owned_ref[x, q, p].astype(F32)
                total = ADAPTER_SCALE * total
                down_ref[x * npair + p] = total[:part]
                up_ref[x * npair + p] = total[part:]

    return pl.pallas_call(
        kernel,
        out_shape=[
            jax.ShapeDtypeStruct((parts, part, rank), F32),
            jax.ShapeDtypeStruct((parts, split, rank), F32),
        ],
        in_specs=[VMEM],
        out_specs=[VMEM, VMEM],
        compiler_params=LIMIT,
        name="finish",
    )(owned)


def keys_partials(place, tokens, frozen_weight, saved_rows, picked):
    rows, width = tokens.shape
    nblocks, rank, features = picked.shape
    half = nblocks // 2
    total = frozen_weight.shape[1]

    def block_of(i, j, place_ref):
        return 2 * j + lax.rem(place_ref[1] + i, 2)

    def kernel(place_ref, tokens_ref, weight_ref, saved_ref, picked_ref, own_ref, other_ref):
        columns = pl.ds(pl.multiple_of((2 * place_ref[0] + place_ref[1]) * features, features), features)
        for i, out_ref in enumerate((own_ref, other_ref)):

            @pl.when(pl.program_id(0) == i)
            def _():
                out_ref[0] = jnp.dot(tokens_ref[...], weight_ref[...], preferred_element_type=F32)
                out_ref[0, :, columns] += ADAPTER_SCALE * jnp.dot(
                    saved_ref[0], picked_ref[0], preferred_element_type=F32
                )

    shape = jax.ShapeDtypeStruct((half, BLK, total), F32)
    return pl.pallas_call(
        kernel,
        grid_spec=pltpu.PrefetchScalarGridSpec(
            num_scalar_prefetch=1,
            grid=(2, half),
            in_specs=[
                pl.BlockSpec((BLK, width), lambda i, j, place: (block_of(i, j, place), 0)),
                pl.BlockSpec((width, total), lambda i, j, place: (0, 0)),
                pl.BlockSpec((1, BLK, rank), lambda i, j, place: (block_of(i, j, place), 0, 0)),
                pl.BlockSpec((1, rank, features), lambda i, j, place: (block_of(i, j, place), 0, 0)),
            ],
            out_specs=[
                pl.BlockSpec((1, BLK, total), lambda i, j, place: (jnp.where(i == 0, j, half - 1), 0, 0)),
                pl.BlockSpec((1, BLK, total), lambda i, j, place: (jnp.where(i == 0, 0, j), 0, 0)),
            ],
        ),
        out_shape=[shape, shape],
        compiler_params=LIMIT,
        name="keys_partials",
    )(place, tokens, frozen_weight, saved_rows, picked)


def keys_chip_sums(place, own, received):
    ny, block, total = own.shape

    def kernel(place_ref, own_ref, received_ref, *outs):
        for d in range(ny):
            to = lax.rem(place_ref[0] + d, ny)
            outs[d][...] = own_ref[to] + received_ref[to]

    return pl.pallas_call(
        kernel,
        out_shape=[jax.ShapeDtypeStruct((block, total), F32)] * ny,
        in_specs=[SMEM, VMEM, VMEM],
        out_specs=[VMEM] * ny,
        compiler_params=LIMIT,
        name="keys_chip_sums",
    )(place, own, received)


def per_device(
    tokens, frozen_weight, saved_mid, cotangent, up_stack, block_job, block_fill, slot_of
):
    width = tokens.shape[1]
    features = cotangent.shape[1]
    rank = saved_mid.shape[1]
    nblocks = block_job.shape[0]
    slot_count = slot_of.shape[0]
    nx, nq, npair, ny = (lax.axis_size(name) for name in ADAPTER + ("y",))
    parts = nx * npair
    part, split = width // parts, rank // parts
    jobs = block_job.reshape(nblocks)
    place = jnp.stack([lax.axis_index(name) for name in SEQ]).astype(jnp.int32)

    with jax.named_scope("mid_sums"):
        saved_other = shift(saved_mid, "core", 1)
        own, other, picked = mid_partials(place, jobs, block_fill, up_stack, cotangent)
        keep, sent = y_payload(place, own, shift(other, "core", 1), saved_mid, saved_other)
        received = [shift(sent, "y", d) for d in range(1, ny)]
        mids, saved_rows = mid_grads(place, keep, sent, received)
        mids_other = shift(mids, "core", 1)
    with jax.named_scope("terms_over_first"):
        terms = products(
            place, jobs, block_fill, slot_of, tokens, mids, mids_other, saved_rows, cotangent, parts
        )
        terms = lax.all_to_all(terms, FIRST, split_axis=0, concat_axis=0, tiled=True)
        tail = nblocks * (part + split)
        slots = terms[:, tail : tail + nblocks, 0].astype(jnp.int32)
    with jax.named_scope("keys_core"):
        keys_own, keys_other = keys_partials(place, tokens, frozen_weight, saved_rows, picked)
        keys_parts = keys_chip_sums(place, keys_own, shift(keys_other, "core", 1))
    with jax.named_scope("keys_y"):
        keys = keys_parts[0]
        for d in range(1, ny):
            keys = keys + shift(keys_parts[d], "y", d)
        keys = keys.astype(BF16)
    with jax.named_scope("sums_over_adapter"):
        sums = slot_sums(slots, terms, slot_count)
        owned = lax.all_to_all(sums, ADAPTER, split_axis=0, concat_axis=0, tiled=True)
    grad_down, grad_up = finish(owned.reshape((nx, nq, npair) + owned.shape[1:]), part)
    return (keys, grad_down.reshape(1, width, rank), grad_up.reshape(1, rank, features))


def solution(mesh):
    chips = Mesh(mesh.devices.reshape(4, 4, 2, 4, 2), ("x", "zq", "zp", "y", "core"))
    return jax.shard_map(
        per_device,
        mesh=chips,
        in_specs=(
            P(ADAPTER, SEQ),
            P(SEQ, None),
            P(ADAPTER + SEQ, None),
            P(ADAPTER, SEQ),
            P(None, None, SEQ),
            P(ADAPTER, None),
            P(ADAPTER),
            P(),
        ),
        out_specs=(
            P(ADAPTER + SEQ, None),
            P(ADAPTER, SEQ, None),
            P(ADAPTER, None, SEQ),
        ),
        check_vma=False,
    )
```

time: 183 us -> 115 us (0.63)
  blocking collectives: 59.7 us -> 0 us
  Pallas kernels: 2.75 us -> 16.5 us
  between operations: 14.2 us -> 0.8 us
  starting transfers between devices: 16.1 us -> 26.5 us
  matrix products: 8.06 us -> 0 us
  other arithmetic: 7.22 us -> 1.7 us
  waiting for transfers between devices: 62.9 us -> 58.8 us
    all_to_all x3 -> x2, waiting for transfers between devices: 62.9 us -> 19.8 us  [the longest x1 19.1 us: per_device(): lax.all_to_all(terms, FIRST, split_axis=0, concat_axis=0, tiled=True)]
    ppermute x0 -> x10, waiting for transfers between devices: none -> 39 us  [shift(): lax.ppermute(value, axis, [(i, (i + distance) % size) for i in range(size)])]
    all_to_all x2 -> x0, blocking collectives: 32.2 us -> none  [the longest x1 16.5 us: per_device(): owned = lax.all_to_all(totals, 'z', split_axis=0, concat_axis=0, tiled=True)]
    all_gather x1 -> x0, blocking collectives: 27.6 us -> none  [per_device(): lax.all_gather(jnp.concatenate([mid_grad, slot_rows], axis=0), 'z', axis=0)]
    pallas_call x1 -> x8, Pallas kernels: 2.75 us -> 16.5 us  [the longest x1 5.59 us: keys_partials(): pl.pallas_call(kernel, grid_spec=pltpu.PrefetchScalarGridSpec(num_scalar_...]
    ppermute x0 -> x10, starting transfers between devices: none -> 10.7 us  [shift(): lax.ppermute(value, axis, [(i, (i + distance) % size) for i in range(size)])]
    dot_general x4 -> x0, matrix products: 8.06 us -> none  [the longest x1 5.92 us: per_device(): frozen_output = jnp.dot(tokens, frozen_weight, preferred_element_type=f32)]
    unnamed x12 -> x32, local copies, waits for them, and re-layouts: 2.55 us -> 9.4 us
  transfers between devices with their start and end apart: 5 -> 12, of which waited for: 3 -> 8; matrix products, arithmetic and copies ran while one was open for 7% -> 1% of each run, Pallas kernels for 2% -> 8%
where the time goes in v2:
time: 115 us; the launch traced here: 114 us
  waiting for transfers between devices  58.8 us (51%)
  starting transfers between devices  26.5 us (23%)
  Pallas kernels  16.5 us (14%)
  local copies, waits for them, and re-layouts  9.4 us (8%)
  other arithmetic  1.7 us (1%)
    ppermute x10, waiting for transfers between devices, shift(): lax.ppermute(value, axis, [(i, (i + distance) % size) for i in range(size)])  39 us
    all_to_all x1, waiting for transfers between devices, per_device(): lax.all_to_all(terms, FIRST, split_axis=0, concat_axis=0, tiled=True)  19.1 us
    ppermute x10, starting transfers between devices, shift(): lax.ppermute(value, axis, [(i, (i + distance) % size) for i in range(size)])  10.7 us
    all_to_all x1, starting transfers between devices, per_device(): lax.all_to_all(sums, ADAPTER, split_axis=0, concat_axis=0, tiled=True)  9.96 us
    unnamed x32, local copies, waits for them, and re-layouts  9.4 us
    all_to_all x1, starting transfers between devices, per_device(): lax.all_to_all(terms, FIRST, split_axis=0, concat_axis=0, tiled=True)  5.89 us
    pallas_call x1, Pallas kernels, keys_partials(): pl.pallas_call(kernel, grid_spec=pltpu.PrefetchScalarGridSpec(num_scalar_...  5.59 us
    pallas_call x1, Pallas kernels, mid_partials(): pl.pallas_call(kernel, out_shape=[half, half, jax.ShapeDtypeStruct((nbloc...  4.03 us
  transfers between devices with their start and end apart: 12, of which 8 were waited for; matrix products, arithmetic and copies ran while one was open for 1% of the time, Pallas kernels for 8%

profile of v2, /device:TPU:32, one launch (start us, length us, event | category | flops | bytes accessed | tf_op | source)
XLA Modules:
  0.0 113.7 jit_solution(1479919264706360223)
XLA Ops:
  1.3 4.0 %mid_partials.1 = (f32[4,128,128]{2,1,0:T(8,128)}, f32[4,128,128]{2,1,0:T(8,128)}, bf16[8,128,128]{2,1,0:T(8,128)(2,1)}) custom-call(s32[2]{0:T(128)} %pad_add_fusion.place_ref, s32[8]{0:T(128)} %bitcast.7, s32[8]{0:T(128)} %fill_ref.3, bf16[32,128,128]{2,1,0:T(8,128)(2,1)} %up_ref.1, bf16[1024,128]{1,0:T(8,128)(2,1)} %cot_ref.3), custom_call_target="tpu_custom_call" | custom-call | tf_op jit(solution)/shard_map/mid_sums/mid_partials/pallas_call | solution.py:61
  5.9 1.3 %collective-permute-done.1.saved_other_ref = bf16[128,128]{1,0:T(8,128)(2,1)S(1)} collective-permute-done((bf16[128,128]{1,0:T(8,128)(2,1)}, bf16[128,128]{1,0:T(8,128)(2,1)S(1)}, u32[]{:S(2)}, u32[]{:S(2)}) %collective-permute-start.1) | collective-permute-done | bytes 32800 | tf_op jit(solution)/shard_map/mid_sums/ppermute | solution.py:25
  7.2 0.9 copy-done.9
  8.2 0.8 copy-done.10
  8.9 0.7 copy-done.11
  10.2 1.7 %collective-permute-start.2 = (bf16[10,128,128]{2,1,0:T(8,128)(2,1)S(1)}, bf16[10,128,128]{2,1,0:T(8,128)(2,1)S(1)}, u32[]{:S(2)}, u32[]{:S(2)}) collective-permute-start(bf16[10,128,128]{2,1,0:T(8,128)(2,1)S(1)} %get-tuple-element.21.sent_ref), channel_id=1, source_target_pairs={{0,2},{2,4},{4,6},{6,0},{1,3},{3,5},{5,7},{7,1},{8,10},{10,12},{12... | collective-permute-start | bytes 983048 | tf_op jit(solution)/shard_map/mid_sums/ppermute | solution.py:25
  11.9 2.9 %collective-permute-start.3 = (bf16[10,128,128]{2,1,0:T(8,128)(2,1)S(1)}, bf16[10,128,128]{2,1,0:T(8,128)(2,1)S(1)}, u32[]{:S(2)}, u32[]{:S(2)}) collective-permute-start(bf16[10,128,128]{2,1,0:T(8,128)(2,1)S(1)} %get-tuple-element.21.sent_ref), channel_id=1, source_target_pairs={{0,4},{2,6},{4,0},{6,2},{1,5},{3,7},{5,1},{7,3},{8,12},{10,14},{12... | collective-permute-start | bytes 983048 | tf_op jit(solution)/shard_map/mid_sums/ppermute | solution.py:25
  14.8 1.3 %collective-permute-start.4 = (bf16[10,128,128]{2,1,0:T(8,128)(2,1)S(1)}, bf16[10,128,128]{2,1,0:T(8,128)(2,1)S(1)}, u32[]{:S(2)}, u32[]{:S(2)}) collective-permute-start(bf16[10,128,128]{2,1,0:T(8,128)(2,1)S(1)} %get-tuple-element.21.sent_ref), channel_id=1, source_target_pairs={{0,6},{2,0},{4,2},{6,4},{1,7},{3,1},{5,3},{7,5},{8,14},{10,8},{12,... | collective-permute-start | bytes 983048 | tf_op jit(solution)/shard_map/mid_sums/ppermute | solution.py:25
  16.1 5.2 %collective-permute-done.2.refs_0_ = bf16[10,128,128]{2,1,0:T(8,128)(2,1)S(1)} collective-permute-done((bf16[10,128,128]{2,1,0:T(8,128)(2,1)S(1)}, bf16[10,128,128]{2,1,0:T(8,128)(2,1)S(1)}, u32[]{:S(2)}, u32[]{:S(2)}) %collective-permute-start.2) | collective-permute-done | bytes 327712 | tf_op jit(solution)/shard_map/mid_sums/ppermute | solution.py:25
  21.3 8.2 %collective-permute-done.3.refs_1_ = bf16[10,128,128]{2,1,0:T(8,128)(2,1)S(1)} collective-permute-done((bf16[10,128,128]{2,1,0:T(8,128)(2,1)S(1)}, bf16[10,128,128]{2,1,0:T(8,128)(2,1)S(1)}, u32[]{:S(2)}, u32[]{:S(2)}) %collective-permute-start.3) | collective-permute-done | bytes 327712 | tf_op jit(solution)/shard_map/mid_sums/ppermute | solution.py:25
  29.5 0.7 mid_grads.1
  30.3 1.3 %collective-permute-done.9.other_ref = bf16[4,128,128]{2,1,0:T(8,128)(2,1)S(1)} collective-permute-done((bf16[4,128,128]{2,1,0:T(8,128)(2,1)S(1)}, bf16[4,128,128]{2,1,0:T(8,128)(2,1)S(1)}, u32[]{:S(2)}, u32[]{:S(2)}) %collective-permute-start.9) | collective-permute-done | bytes 131104 | tf_op jit(solution)/shard_map/mid_sums/ppermute | solution.py:25
  31.7 1.4 %products.1 = bf16[8,1168,128]{2,1,0:T(8,128)(2,1)S(1)} custom-call(s32[2]{0:T(128)S(1)} %copy-done.12, s32[8]{0:T(128)S(1)} %bitcast.8, s32[8]{0:T(128)S(1)} %copy-done.14, s32[32]{0:T(128)S(1)} %copy-done.15, bf16[1024,1024]{1,0:T(8,128)(2,1)S(1)} %copy-done.1, bf16[4,128,128]{2,1,0:T(8,128)(2,1)S(1)} %get-tuple-element.30.mids_ref, ...), custom_call_target="tpu_custom_call" | custom-call | tf_op jit(solution)/shard_map/terms_over_first/products/pallas_call | solution.py:156
  33.1 1.4 %copy-done = bf16[8,1168,128]{2,1,0:T(8,128)(2,1)} copy-done((bf16[8,1168,128]{2,1,0:T(8,128)(2,1)}, bf16[8,1168,128]{2,1,0:T(8,128)(2,1)S(1)}, u32[]{:S(2)}) %copy-start) | copy-done | bytes 2392088
  34.5 5.9 %all-to-all-start = ((bf16[8,1168,128]{2,1,0:T(8,128)(2,1)}), bf16[8,1168,128]{2,1,0:T(8,128)(2,1)S(1)}, u32[]{:S(2)}, u32[]{:S(2)}) async-start(bf16[8,1168,128]{2,1,0:T(8,128)(2,1)} %copy-done), calls=%async_computation | async-start | bytes 4784128 | tf_op jit(solution)/shard_map/terms_over_first/all_to_all | solution.py:302
  40.4 1.6 %copy-done.2 = bf16[1024,1024]{1,0:T(8,128)(2,1)S(1)} copy-done((bf16[1024,1024]{1,0:T(8,128)(2,1)S(1)}, bf16[1024,1024]{1,0:T(8,128)(2,1)}, u32[]{:S(2)}) %copy-start.2) | copy-done | bytes 2097176
  42.0 1.6 %copy-done.4 = bf16[1024,1024]{1,0:T(8,128)(2,1)S(1)} copy-done((bf16[1024,1024]{1,0:T(8,128)(2,1)S(1)}, bf16[1024,1024]{1,0:T(8,128)(2,1)}, u32[]{:S(2)}) %copy-start.4) | copy-done | bytes 2097176
  43.6 5.6 %keys_partials.1 = (f32[4,128,1024]{2,1,0:T(8,128)S(1)}, f32[4,128,1024]{2,1,0:T(8,128)}) custom-call(s32[2]{0:T(128)S(1)} %copy-done.12, bf16[1024,1024]{1,0:T(8,128)(2,1)S(1)} %copy-done.2, bf16[1024,1024]{1,0:T(8,128)(2,1)S(1)} %copy-done.4, bf16[8,128,128]{2,1,0:T(8,128)(2,1)S(1)} %get-tuple-element.22.saved_ref, bf16[8,128,128]{2,1,0:T(8,128)(2,1)S(1)} %copy-done.8), custom_call_target="tpu_custom_call" | custom-call | tf_op jit(solution)/shard_map/keys_core/keys_partials/pallas_call | solution.py:237
  49.2 1.4 %copy-done.5 = f32[4,128,1024]{2,1,0:T(8,128)} copy-done((f32[4,128,1024]{2,1,0:T(8,128)}, f32[4,128,1024]{2,1,0:T(8,128)S(1)}, u32[]{:S(2)}) %copy-start.5) | copy-done | bytes 2097176
  50.5 19.1 %all-to-all-done.terms_ref = bf16[8,1168,128]{2,1,0:T(8,128)(2,1)S(1)} async-done(((bf16[8,1168,128]{2,1,0:T(8,128)(2,1)}), bf16[8,1168,128]{2,1,0:T(8,128)(2,1)S(1)}, u32[]{:S(2)}, u32[]{:S(2)}) %all-to-all-start) | async-done | bytes 2392096 | tf_op jit(solution)/shard_map/terms_over_first/all_to_all | solution.py:302
  69.8 1.5 %slot_sums.1 = bf16[32,144,128]{2,1,0:T(8,128)(2,1)S(1)} custom-call(s32[8,8]{1,0:T(8,128)S(1)} %convert_reduce_fusion.slots_ref, bf16[8,1168,128]{2,1,0:T(8,128)(2,1)S(1)} %all-to-all-done.terms_ref), custom_call_target="tpu_custom_call" | custom-call | tf_op jit(solution)/shard_map/sums_over_adapter/slot_sums/pallas_call | solution.py:178
  71.3 1.0 copy-done.3
  72.4 10.0 %all-to-all-start.1 = ((bf16[32,144,128]{2,1,0:T(8,128)(2,1)}), bf16[32,144,128]{2,1,0:T(8,128)(2,1)S(1)}, u32[]{:S(2)}, u32[]{:S(2)}) async-start(bf16[32,144,128]{2,1,0:T(8,128)(2,1)} %copy-done.3), calls=%async_computation.1 | async-start | bytes 2359296 | tf_op jit(solution)/shard_map/sums_over_adapter/all_to_all | solution.py:315
  82.4 1.8 %keys_chip_sums.1 = (f32[128,1024]{1,0:T(8,128)S(1)}, f32[128,1024]{1,0:T(8,128)S(1)}, f32[128,1024]{1,0:T(8,128)S(1)}, f32[128,1024]{1,0:T(8,128)S(1)}) custom-call(s32[2]{0:T(128)S(1)} %copy-done.12, f32[4,128,1024]{2,1,0:T(8,128)S(1)} %copy-done.6, f32[4,128,1024]{2,1,0:T(8,128)} %collective-permute-done.5.received_ref), custom_call_target="tpu_custom_call" | custom-call | tf_op jit(solution)/shard_map/keys_core/keys_chip_sums/pallas_call | solution.py:267
  84.2 2.2 %collective-permute-start.8 = (f32[128,1024]{1,0:T(8,128)S(1)}, f32[128,1024]{1,0:T(8,128)S(1)}, u32[]{:S(2)}, u32[]{:S(2)}) collective-permute-start(f32[128,1024]{1,0:T(8,128)S(1)} %get-tuple-element.29), channel_id=1, source_target_pairs={{0,6},{2,0},{4,2},{6,4},{1,7},{3,1},{5,3},{7,5},{8,14},{10,8},{12,... | collective-permute-start | bytes 1572872 | tf_op jit(solution)/shard_map/keys_y/ppermute | solution.py:25
  86.4 1.1 %collective-permute-start.7 = (f32[128,1024]{1,0:T(8,128)S(1)}, f32[128,1024]{1,0:T(8,128)S(1)}, u32[]{:S(2)}, u32[]{:S(2)}) collective-permute-start(f32[128,1024]{1,0:T(8,128)S(1)} %get-tuple-element.28), channel_id=1, source_target_pairs={{0,4},{2,6},{4,0},{6,2},{1,5},{3,7},{5,1},{7,3},{8,12},{10,14},{12... | collective-permute-start | bytes 1572872 | tf_op jit(solution)/shard_map/keys_y/ppermute | solution.py:25
  87.6 0.7 collective-permute-start.6
  88.3 19.3 %collective-permute-done.8 = f32[128,1024]{1,0:T(8,128)S(1)} collective-permute-done((f32[128,1024]{1,0:T(8,128)S(1)}, f32[128,1024]{1,0:T(8,128)S(1)}, u32[]{:S(2)}, u32[]{:S(2)}) %collective-permute-start.8) | collective-permute-done | bytes 524320 | tf_op jit(solution)/shard_map/keys_y/ppermute | solution.py:25
  107.6 3.7 %collective-permute-done.6 = f32[128,1024]{1,0:T(8,128)S(1)} collective-permute-done((f32[128,1024]{1,0:T(8,128)S(1)}, f32[128,1024]{1,0:T(8,128)S(1)}, u32[]{:S(2)}, u32[]{:S(2)}) %collective-permute-start.6) | collective-permute-done | bytes 524320 | tf_op jit(solution)/shard_map/keys_y/ppermute | solution.py:25
  111.2 0.8 add_convert_fusion
  112.1 0.7 all-to-all-done.1
  112.8 1.0 finish.1
  (35 shorter events, 2.2 us)
Async XLA Ops:
  0.6 31.0 %copy-start.7 = (bf16[1024,128]{1,0:T(8,128)(2,1)S(1)}, bf16[1024,128]{1,0:T(8,128)(2,1)}, u32[]{:S(2)}) copy-start(bf16[1024,128]{1,0:T(8,128)(2,1)} %cot_ref.3) | copy-start | bytes 786436
  0.6 31.0 %copy-start.1 = (bf16[1024,1024]{1,0:T(8,128)(2,1)S(1)}, bf16[1024,1024]{1,0:T(8,128)(2,1)}, u32[]{:S(2)}) copy-start(bf16[1024,1024]{1,0:T(8,128)(2,1)} %tokens_ref.3) | copy-start | bytes 6291460
  5.3 1.9 %collective-permute-start = (f32[4,128,128]{2,1,0:T(8,128)}, f32[4,128,128]{2,1,0:T(8,128)S(1)}, u32[]{:S(2)}, u32[]{:S(2)}) collective-permute-start(f32[4,128,128]{2,1,0:T(8,128)} %get-tuple-element.19), channel_id=1, source_target_pairs={{0,1},{1,0},{2,3},{3,2},{4,5},{5,4},{6,7},{7,6},{8,9},{9,8},{10,11... | collective-permute-start | bytes 786440 | tf_op jit(solution)/shard_map/mid_sums/ppermute | solution.py:25
  5.4 1.8 %collective-permute-start.1 = (bf16[128,128]{1,0:T(8,128)(2,1)}, bf16[128,128]{1,0:T(8,128)(2,1)S(1)}, u32[]{:S(2)}, u32[]{:S(2)}) collective-permute-start(bf16[128,128]{1,0:T(8,128)(2,1)} %saved_ref.1), channel_id=1, source_target_pairs={{0,1},{1,0},{2,3},{3,2},{4,5},{5,4},{6,7},{7,6},{8,9},{9,8},{10,11... | collective-permute-start | bytes 98312 | tf_op jit(solution)/shard_map/mid_sums/ppermute | solution.py:25
  7.2 1.0 copy-start.9
  8.2 0.8 copy-start.10
  8.9 0.7 copy-start.11
  9.6 22.0 %copy-start.12 = (s32[2]{0:T(128)S(1)}, s32[2]{0:T(128)}, u32[]{:S(2)}) copy-start(s32[2]{0:T(128)} %pad_add_fusion.place_ref) | copy-start | bytes 28
  9.6 22.0 %copy-start.13 = (s32[8,1]{0,1:T(1,128)S(1)}, s32[8,1]{0,1:T(1,128)}, u32[]{:S(2)}) copy-start(s32[8,1]{0,1:T(1,128)} %param.13) | copy-start | bytes 100
  9.6 22.1 %copy-start.14 = (s32[8]{0:T(128)S(1)}, s32[8]{0:T(128)}, u32[]{:S(2)}) copy-start(s32[8]{0:T(128)} %fill_ref.3) | copy-start | bytes 100
  9.6 22.1 %copy-start.15 = (s32[32]{0:T(128)S(1)}, s32[32]{0:T(128)}, u32[]{:S(2)}) copy-start(s32[32]{0:T(128)} %slot_ref.1) | copy-start | bytes 388
  10.2 11.1 %collective-permute-start.2 = (bf16[10,128,128]{2,1,0:T(8,128)(2,1)S(1)}, bf16[10,128,128]{2,1,0:T(8,128)(2,1)S(1)}, u32[]{:S(2)}, u32[]{:S(2)}) collective-permute-start(bf16[10,128,128]{2,1,0:T(8,128)(2,1)S(1)} %get-tuple-element.21.sent_ref), channel_id=1, source_target_pairs={{0,2},{2,4},{4,6},{6,0},{1,3},{3,5},{5,7},{7,1},{8,10},{10,12},{12... | collective-permute-start | bytes 983048 | tf_op jit(solution)/shard_map/mid_sums/ppermute | solution.py:25
  11.9 17.6 %collective-permute-start.3 = (bf16[10,128,128]{2,1,0:T(8,128)(2,1)S(1)}, bf16[10,128,128]{2,1,0:T(8,128)(2,1)S(1)}, u32[]{:S(2)}, u32[]{:S(2)}) collective-permute-start(bf16[10,128,128]{2,1,0:T(8,128)(2,1)S(1)} %get-tuple-element.21.sent_ref), channel_id=1, source_target_pairs={{0,4},{2,6},{4,0},{6,2},{1,5},{3,7},{5,1},{7,3},{8,12},{10,14},{12... | collective-permute-start | bytes 983048 | tf_op jit(solution)/shard_map/mid_sums/ppermute | solution.py:25
  14.8 14.8 %collective-permute-start.4 = (bf16[10,128,128]{2,1,0:T(8,128)(2,1)S(1)}, bf16[10,128,128]{2,1,0:T(8,128)(2,1)S(1)}, u32[]{:S(2)}, u32[]{:S(2)}) collective-permute-start(bf16[10,128,128]{2,1,0:T(8,128)(2,1)S(1)} %get-tuple-element.21.sent_ref), channel_id=1, source_target_pairs={{0,6},{2,0},{4,2},{6,4},{1,7},{3,1},{5,3},{7,5},{8,14},{10,8},{12,... | collective-permute-start | bytes 983048 | tf_op jit(solution)/shard_map/mid_sums/ppermute | solution.py:25
  30.2 1.4 %collective-permute-start.9 = (bf16[4,128,128]{2,1,0:T(8,128)(2,1)S(1)}, bf16[4,128,128]{2,1,0:T(8,128)(2,1)S(1)}, u32[]{:S(2)}, u32[]{:S(2)}) collective-permute-start(bf16[4,128,128]{2,1,0:T(8,128)(2,1)S(1)} %get-tuple-element.30.mids_ref), channel_id=1, source_target_pairs={{0,1},{1,0},{2,3},{3,2},{4,5},{5,4},{6,7},{7,6},{8,9},{9,8},{10,11... | collective-permute-start | bytes 393224 | tf_op jit(solution)/shard_map/mid_sums/ppermute | solution.py:25
  33.1 1.4 %copy-start = (bf16[8,1168,128]{2,1,0:T(8,128)(2,1)}, bf16[8,1168,128]{2,1,0:T(8,128)(2,1)S(1)}, u32[]{:S(2)}) copy-start(bf16[8,1168,128]{2,1,0:T(8,128)(2,1)S(1)} %products.1) | copy-start | bytes 7176196
  34.5 5.9 %copy-start.8 = (bf16[8,128,128]{2,1,0:T(8,128)(2,1)S(1)}, bf16[8,128,128]{2,1,0:T(8,128)(2,1)}, u32[]{:S(2)}) copy-start(bf16[8,128,128]{2,1,0:T(8,128)(2,1)} %get-tuple-element.23.picked_ref) | copy-start | bytes 786436
  34.5 35.1 %all-to-all-start = ((bf16[8,1168,128]{2,1,0:T(8,128)(2,1)}), bf16[8,1168,128]{2,1,0:T(8,128)(2,1)S(1)}, u32[]{:S(2)}, u32[]{:S(2)}) async-start(bf16[8,1168,128]{2,1,0:T(8,128)(2,1)} %copy-done), calls=%async_computation | async-start | bytes 4784128 | tf_op jit(solution)/shard_map/terms_over_first/all_to_all | solution.py:302
  40.4 1.6 %copy-start.2 = (bf16[1024,1024]{1,0:T(8,128)(2,1)S(1)}, bf16[1024,1024]{1,0:T(8,128)(2,1)}, u32[]{:S(2)}) copy-start(bf16[1024,1024]{1,0:T(8,128)(2,1)} %tokens_ref.3) | copy-start | bytes 6291460
  42.0 1.6 %copy-start.4 = (bf16[1024,1024]{1,0:T(8,128)(2,1)S(1)}, bf16[1024,1024]{1,0:T(8,128)(2,1)}, u32[]{:S(2)}) copy-start(bf16[1024,1024]{1,0:T(8,128)(2,1)} %weight_ref.1) | copy-start | bytes 6291460
  49.2 1.4 %copy-start.5 = (f32[4,128,1024]{2,1,0:T(8,128)}, f32[4,128,1024]{2,1,0:T(8,128)S(1)}, u32[]{:S(2)}) copy-start(f32[4,128,1024]{2,1,0:T(8,128)S(1)} %get-tuple-element.24.own_ref) | copy-start | bytes 6291460
  50.5 31.8 %collective-permute-start.5 = (f32[4,128,1024]{2,1,0:T(8,128)}, f32[4,128,1024]{2,1,0:T(8,128)}, u32[]{:S(2)}, u32[]{:S(2)}) collective-permute-start(f32[4,128,1024]{2,1,0:T(8,128)} %get-tuple-element.25), channel_id=1, source_target_pairs={{0,1},{1,0},{2,3},{3,2},{4,5},{5,4},{6,7},{7,6},{8,9},{9,8},{10,11... | collective-permute-start | bytes 6291464 | tf_op jit(solution)/shard_map/keys_core/ppermute | solution.py:25
  71.3 1.0 copy-start.3
  72.4 10.0 %copy-start.6 = (f32[4,128,1024]{2,1,0:T(8,128)S(1)}, f32[4,128,1024]{2,1,0:T(8,128)}, u32[]{:S(2)}) copy-start(f32[4,128,1024]{2,1,0:T(8,128)} %copy-done.5) | copy-start | bytes 6291460
  72.4 40.4 %all-to-all-start.1 = ((bf16[32,144,128]{2,1,0:T(8,128)(2,1)}), bf16[32,144,128]{2,1,0:T(8,128)(2,1)S(1)}, u32[]{:S(2)}, u32[]{:S(2)}) async-start(bf16[32,144,128]{2,1,0:T(8,128)(2,1)} %copy-done.3), calls=%async_computation.1 | async-start | bytes 2359296 | tf_op jit(solution)/shard_map/sums_over_adapter/all_to_all | solution.py:315
  84.2 23.4 %collective-permute-start.8 = (f32[128,1024]{1,0:T(8,128)S(1)}, f32[128,1024]{1,0:T(8,128)S(1)}, u32[]{:S(2)}, u32[]{:S(2)}) collective-permute-start(f32[128,1024]{1,0:T(8,128)S(1)} %get-tuple-element.29), channel_id=1, source_target_pairs={{0,6},{2,0},{4,2},{6,4},{1,7},{3,1},{5,3},{7,5},{8,14},{10,8},{12,... | collective-permute-start | bytes 1572872 | tf_op jit(solution)/shard_map/keys_y/ppermute | solution.py:25
  86.4 21.1 %collective-permute-start.7 = (f32[128,1024]{1,0:T(8,128)S(1)}, f32[128,1024]{1,0:T(8,128)S(1)}, u32[]{:S(2)}, u32[]{:S(2)}) collective-permute-start(f32[128,1024]{1,0:T(8,128)S(1)} %get-tuple-element.28), channel_id=1, source_target_pairs={{0,4},{2,6},{4,0},{6,2},{1,5},{3,7},{5,1},{7,3},{8,12},{10,14},{12... | collective-permute-start | bytes 1572872 | tf_op jit(solution)/shard_map/keys_y/ppermute | solution.py:25
  87.6 23.7 %collective-permute-start.6 = (f32[128,1024]{1,0:T(8,128)S(1)}, f32[128,1024]{1,0:T(8,128)S(1)}, u32[]{:S(2)}, u32[]{:S(2)}) collective-permute-start(f32[128,1024]{1,0:T(8,128)S(1)} %get-tuple-element.27), channel_id=1, source_target_pairs={{0,2},{2,4},{4,6},{6,0},{1,3},{3,5},{5,7},{7,1},{8,10},{10,12},{12... | collective-permute-start | bytes 1572872 | tf_op jit(solution)/shard_map/keys_y/ppermute | solution.py:25

commit v3 on v2

--- a/solution.py
+++ b/solution.py
@@ -37,47 +37,61 @@
     return jnp.where(position < fill_ref[b], block, jnp.zeros_like(block))
 
 
-def mid_partials(place, jobs, fills, up_stack, cotangent):
+def mid_partials(jobs, fills, up_stack, cotangent, saved):
     nblocks = jobs.shape[0]
     rank, features = up_stack.shape[1:]
-
-    def kernel(place_ref, jobs_ref, fill_ref, up_ref, cot_ref, own_ref, other_ref, picked_ref, sems):
-        copies = [
-            pltpu.make_async_copy(up_ref.at[jobs_ref[b]], picked_ref.at[b], sems.at[b])
-            for b in range(nblocks)
-        ]
-        for copy in copies:
-            copy.start()
-        core = place_ref[1]
-        for pair in range(nblocks // 2):
+    half = nblocks // 2
+
+    def kernel(
+        jobs_ref, fill_ref, up_ref, cot_ref, saved_ref, own_ref, other_ref, picked_ref, cot, sems
+    ):
+        copies = []
+        for b in range(nblocks):
+            block = slice(b * BLK, (b + 1) * BLK)
+            pair = (
+                pltpu.make_async_copy(up_ref.at[jobs_ref[b]], picked_ref.at[b], sems.at[2 * b]),
+                pltpu.make_async_copy(cot_ref.at[block, :], cot.at[block, :], sems.at[2 * b + 1]),
+            )
+            for copy in pair:
+                copy.start()
+            copies.append(pair)
+        core = lax.axis_index("core")
+        own_ref[half] = saved_ref[...].astype(F32)
+        other_ref[half] = saved_ref[...].astype(F32)
+        for i in range(half):
             partials = []
-            for b in (2 * pair, 2 * pair + 1):
-                copies[b].wait()
-                partials.append(contract(masked(cot_ref, fill_ref, b), picked_ref[b], 1, 1))
-            own_ref[pair] = jnp.where(core == 0, partials[0], partials[1])
-            other_ref[pair] = jnp.where(core == 0, partials[1], partials[0])
-
-    half = jax.ShapeDtypeStruct((nblocks // 2, BLK, rank), F32)
-    return pl.pallas_call(
-        kernel,
-        out_shape=[half, half, jax.ShapeDtypeStruct((nblocks, rank, features), BF16)],
-        in_specs=[SMEM, SMEM, SMEM, HBM, VMEM],
-        out_specs=[VMEM, VMEM, VMEM],
-        scratch_shapes=[pltpu.SemaphoreType.DMA((nblocks,))],
+            for b in (2 * i, 2 * i + 1):
+                for copy in copies[b]:
+                    copy.wait()
+                partials.append(contract(masked(cot, fill_ref, b), picked_ref[b], 1, 1))
+            own_ref[i] = jnp.where(core == 0, partials[0], partials[1])
+            other_ref[i] = jnp.where(core == 0, partials[1], partials[0])
+
+    out = jax.ShapeDtypeStruct((half + 1, BLK, rank), F32)
+    return pl.pallas_call(
+        kernel,
+        out_shape=[out, out, jax.ShapeDtypeStruct((nblocks, rank, features), BF16)],
+        in_specs=[SMEM, SMEM, HBM, HBM, VMEM],
+        out_specs=[VMEM] * 3,
+        scratch_shapes=[
+            pltpu.VMEM(cotangent.shape, BF16),
+            pltpu.SemaphoreType.DMA((2 * nblocks,)),
+        ],
         compiler_params=WHOLE,
         name="mid_partials",
-    )(place, jobs, fills, up_stack, cotangent)
-
-
-def y_payload(place, own, received, saved, saved_other):
+    )(jobs, fills, up_stack, cotangent, saved)
+
+
+def y_payload(own, received):
     half, _, rank = own.shape
-
-    def kernel(place_ref, own_ref, received_ref, saved_ref, saved_other_ref, keep_ref, out_ref):
-        core = place_ref[1]
-        first, second = saved_ref[...], saved_other_ref[...]
-        out_ref[2 * half] = jnp.where(core == 0, first, second)
-        out_ref[2 * half + 1] = jnp.where(core == 0, second, first)
-        total = own_ref[...] + received_ref[...]
+    half -= 1
+
+    def kernel(own_ref, received_ref, keep_ref, out_ref):
+        first = lax.axis_index("core") == 0
+        mine, theirs = own_ref[half], received_ref[half]
+        out_ref[2 * half] = jnp.where(first, mine, theirs).astype(BF16)
+        out_ref[2 * half + 1] = jnp.where(first, theirs, mine).astype(BF16)
+        total = own_ref[:half] + received_ref[:half]
         keep_ref[...] = total
         high = total.astype(BF16)
         out_ref[:half] = high
@@ -89,21 +103,21 @@
             jax.ShapeDtypeStruct((half, BLK, rank), F32),
             jax.ShapeDtypeStruct((2 * half + 2, BLK, rank), BF16),
         ],
-        in_specs=[SMEM] + [VMEM] * 4,
+        in_specs=[VMEM] * 2,
         out_specs=[VMEM] * 2,
         compiler_params=LIMIT,
         name="y_payload",
-    )(place, own, received, saved, saved_other)
-
-
-def mid_grads(place, keep, sent, received):
+    )(own, received)
+
+
+def mid_grads(keep, sent, received):
     half, _, rank = keep.shape
     ny = len(received) + 1
 
-    def kernel(place_ref, keep_ref, sent_ref, *refs):
+    def kernel(keep_ref, sent_ref, *refs):
         got = refs[: ny - 1]
         mids_ref, rows_ref = refs[ny - 1 :]
-        y = place_ref[0]
+        y = lax.axis_index("y")
         total = keep_ref[...]
         for ref in got:
             total += ref[:half].astype(F32) + ref[half : 2 * half].astype(F32)
@@ -119,23 +133,23 @@
             jax.ShapeDtypeStruct((half, BLK, rank), BF16),
             jax.ShapeDtypeStruct((2 * half, BLK, rank), BF16),
         ],
-        in_specs=[SMEM] + [VMEM] * (ny + 1),
+        in_specs=[VMEM] * (ny + 1),
         out_specs=[VMEM] * 2,
         compiler_params=LIMIT,
         name="mid_grads",
-    )(place, keep, sent, *received)
-
-
-def products(place, jobs, fills, slot_of, tokens, mids, mids_other, saved_rows, cotangent, parts):
+    )(keep, sent, *received)
+
+
+def products(jobs, fills, slot_of, tokens, mids, mids_other, saved_rows, cotangent, parts):
     width = tokens.shape[1]
     nblocks, _, rank = saved_rows.shape
     part, split = width // parts, rank // parts
     height = part + split
 
     def kernel(
-        place_ref, jobs_ref, fill_ref, slot_ref, tokens_ref, mids_ref, other_ref, saved_ref, cot_ref, out_ref
+        jobs_ref, fill_ref, slot_ref, tokens_ref, mids_ref, other_ref, saved_ref, cot_ref, out_ref
     ):
-        core = place_ref[1]
+        core = lax.axis_index("core")
         row = lax.broadcasted_iota(jnp.int32, (SLOT_ROWS, rank), 0)
         slots = jnp.zeros((SLOT_ROWS, rank), jnp.int32)
         for b in range(nblocks):
@@ -156,11 +170,11 @@
     return pl.pallas_call(
         kernel,
         out_shape=jax.ShapeDtypeStruct((parts, nblocks * height + SLOT_ROWS, rank), BF16),
-        in_specs=[SMEM] * 4 + [VMEM] * 5,
+        in_specs=[SMEM] * 3 + [VMEM] * 5,
         out_specs=VMEM,
         compiler_params=LIMIT,
         name="products",
-    )(place, jobs, fills, slot_of, tokens, mids, mids_other, saved_rows, cotangent)
+    )(jobs, fills, slot_of, tokens, mids, mids_other, saved_rows, cotangent)
 
 
 def slot_sums(slots, terms, slot_count):
@@ -256,22 +270,22 @@
     )(place, tokens, frozen_weight, saved_rows, picked)
 
 
-def keys_chip_sums(place, own, received):
+def keys_chip_sums(own, received):
     ny, block, total = own.shape
 
-    def kernel(place_ref, own_ref, received_ref, *outs):
+    def kernel(own_ref, received_ref, *outs):
         for d in range(ny):
-            to = lax.rem(place_ref[0] + d, ny)
+            to = lax.rem(lax.axis_index("y") + d, ny)
             outs[d][...] = own_ref[to] + received_ref[to]
 
     return pl.pallas_call(
         kernel,
         out_shape=[jax.ShapeDtypeStruct((block, total), F32)] * ny,
-        in_specs=[SMEM, VMEM, VMEM],
+        in_specs=[VMEM, VMEM],
         out_specs=[VMEM] * ny,
         compiler_params=LIMIT,
         name="keys_chip_sums",
-    )(place, own, received)
+    )(own, received)
 
 
 def per_device(
@@ -289,28 +303,28 @@
     place = jnp.stack([lax.axis_index(name) for name in SEQ]).astype(jnp.int32)
 
     with jax.named_scope("mid_sums"):
-        saved_other = shift(saved_mid, "core", 1)
-        own, other, picked = mid_partials(place, jobs, block_fill, up_stack, cotangent)
-        keep, sent = y_payload(place, own, shift(other, "core", 1), saved_mid, saved_other)
+        own, other, picked = mid_partials(jobs, block_fill, up_stack, cotangent, saved_mid)
+        keep, sent = y_payload(own, shift(other, "core", 1))
         received = [shift(sent, "y", d) for d in range(1, ny)]
-        mids, saved_rows = mid_grads(place, keep, sent, received)
+        mids, saved_rows = mid_grads(keep, sent, received)
         mids_other = shift(mids, "core", 1)
     with jax.named_scope("terms_over_first"):
         terms = products(
-            place, jobs, block_fill, slot_of, tokens, mids, mids_other, saved_rows, cotangent, parts
+            jobs, block_fill, slot_of, tokens, mids, mids_other, saved_rows, cotangent, parts
         )
         terms = lax.all_to_all(terms, FIRST, split_axis=0, concat_axis=0, tiled=True)
-        tail = nblocks * (part + split)
-        slots = terms[:, tail : tail + nblocks, 0].astype(jnp.int32)
     with jax.named_scope("keys_core"):
         keys_own, keys_other = keys_partials(place, tokens, frozen_weight, saved_rows, picked)
-        keys_parts = keys_chip_sums(place, keys_own, shift(keys_other, "core", 1))
+        keys_parts = keys_chip_sums(keys_own, shift(keys_other, "core", 1))
+        terms, keys_parts = lax.optimization_barrier((terms, keys_parts))
     with jax.named_scope("keys_y"):
         keys = keys_parts[0]
         for d in range(1, ny):
             keys = keys + shift(keys_parts[d], "y", d)
         keys = keys.astype(BF16)
     with jax.named_scope("sums_over_adapter"):
+        tail = nblocks * (part + split)
+        slots = terms[:, tail : tail + nblocks, 0].astype(jnp.int32)
         sums = slot_sums(slots, terms, slot_count)
         owned = lax.all_to_all(sums, ADAPTER, split_axis=0, concat_axis=0, tiled=True)
     grad_down, grad_up = finish(owned.reshape((nx, nq, npair) + owned.shape[1:]), part)

time: 115 us -> 111 us (0.965)
  Pallas kernels: 16.5 us -> 12.7 us
  waiting for transfers between devices: 58.8 us -> 60.5 us
  local copies, waits for them, and re-layouts: 9.4 us -> 8.2 us
    all_to_all x1, waiting for transfers between devices: 19.1 us -> 15.4 us  [per_device(): lax.all_to_all(terms, FIRST, split_axis=0, concat_axis=0, tiled=True)]
    all_to_all x1, waiting for transfers between devices: 0.72 us -> 4.11 us  [per_device(): lax.all_to_all(sums, ADAPTER, split_axis=0, concat_axis=0, tiled=True)]
    ppermute x10 -> x9, waiting for transfers between devices: 39 us -> 40.9 us  [shift(): lax.ppermute(value, axis, [(i, (i + distance) % size) for i in range(size)])]
    pallas_call x1, Pallas kernels: 1.82 us -> 0.21 us  [keys_chip_sums(): pl.pallas_call(kernel, out_shape=[jax.ShapeDtypeStruct((block, total), F3...]
    unnamed x32 -> x30, local copies, waits for them, and re-layouts: 9.4 us -> 8.2 us
    ppermute x10 -> x9, starting transfers between devices: 10.7 us -> 11.5 us  [shift(): lax.ppermute(value, axis, [(i, (i + distance) % size) for i in range(size)])]
  transfers between devices with their start and end apart: 12 -> 11, of which waited for: 8 -> 10; matrix products, arithmetic and copies ran while one was open for 1% -> 1% of each run, Pallas kernels for 8% -> 4%
where the time goes in v3:
time: 111 us
  waiting for transfers between devices  60.5 us (55%)
  starting transfers between devices  27.3 us (25%)
  Pallas kernels  12.7 us (11%)
  local copies, waits for them, and re-layouts  8.2 us (7%)
  other arithmetic  1.12 us (1%)
    ppermute x9, waiting for transfers between devices, shift(): lax.ppermute(value, axis, [(i, (i + distance) % size) for i in range(size)])  40.9 us
    all_to_all x1, waiting for transfers between devices, per_device(): lax.all_to_all(terms, FIRST, split_axis=0, concat_axis=0, tiled=True)  15.4 us
    ppermute x9, starting transfers between devices, shift(): lax.ppermute(value, axis, [(i, (i + distance) % size) for i in range(size)])  11.5 us
    all_to_all x1, starting transfers between devices, per_device(): lax.all_to_all(sums, ADAPTER, split_axis=0, concat_axis=0, tiled=True)  9.96 us
    unnamed x30, local copies, waits for them, and re-layouts  8.2 us
    all_to_all x1, starting transfers between devices, per_device(): lax.all_to_all(terms, FIRST, split_axis=0, concat_axis=0, tiled=True)  5.89 us
    pallas_call x1, Pallas kernels, keys_partials(): pl.pallas_call(kernel, grid_spec=pltpu.PrefetchScalarGridSpec(num_scalar_...  4.47 us
    all_to_all x1, waiting for transfers between devices, per_device(): lax.all_to_all(sums, ADAPTER, split_axis=0, concat_axis=0, tiled=True)  4.11 us
  transfers between devices with their start and end apart: 11, of which 10 were waited for; matrix products, arithmetic and copies ran while one was open for 1% of the time, Pallas kernels for 4%

profile of v3, /device:TPU:32, one launch (start us, length us, event | category | flops | bytes accessed | tf_op | source)
XLA Modules:
  0.0 110.6 jit_solution(1748386201078013904)
XLA Ops:
  0.7 4.1 %mid_partials.1 = (f32[5,128,128]{2,1,0:T(8,128)}, f32[5,128,128]{2,1,0:T(8,128)}, bf16[8,128,128]{2,1,0:T(8,128)(2,1)}) custom-call(s32[8]{0:T(128)} %bitcast.7, s32[8]{0:T(128)} %fill_ref.3, bf16[32,128,128]{2,1,0:T(8,128)(2,1)} %up_ref.1, bf16[1024,128]{1,0:T(8,128)(2,1)} %cot_ref.3, bf16[128,128]{1,0:T(8,128)(2,1)} %saved_ref.1), custom_call_target="tpu_custom_call" | custom-call | tf_op jit(solution)/shard_map/mid_sums/mid_partials/pallas_call | solution.py:71
  4.8 1.8 %collective-permute-done.received_ref = f32[5,128,128]{2,1,0:T(8,128)S(1)} collective-permute-done((f32[5,128,128]{2,1,0:T(8,128)}, f32[5,128,128]{2,1,0:T(8,128)S(1)}, u32[]{:S(2)}, u32[]{:S(2)}) %collective-permute-start) | collective-permute-done | bytes 327712 | tf_op jit(solution)/shard_map/mid_sums/ppermute | solution.py:25
  6.7 1.0 copy-done.6
  7.7 1.7 %collective-permute-start.1 = (bf16[10,128,128]{2,1,0:T(8,128)(2,1)S(1)}, bf16[10,128,128]{2,1,0:T(8,128)(2,1)S(1)}, u32[]{:S(2)}, u32[]{:S(2)}) collective-permute-start(bf16[10,128,128]{2,1,0:T(8,128)(2,1)S(1)} %get-tuple-element.26.sent_ref), channel_id=1, source_target_pairs={{0,2},{2,4},{4,6},{6,0},{1,3},{3,5},{5,7},{7,1},{8,10},{10,12},{12... | collective-permute-start | bytes 983048 | tf_op jit(solution)/shard_map/mid_sums/ppermute | solution.py:25
  9.4 2.9 %collective-permute-start.2 = (bf16[10,128,128]{2,1,0:T(8,128)(2,1)S(1)}, bf16[10,128,128]{2,1,0:T(8,128)(2,1)S(1)}, u32[]{:S(2)}, u32[]{:S(2)}) collective-permute-start(bf16[10,128,128]{2,1,0:T(8,128)(2,1)S(1)} %get-tuple-element.26.sent_ref), channel_id=1, source_target_pairs={{0,4},{2,6},{4,0},{6,2},{1,5},{3,7},{5,1},{7,3},{8,12},{10,14},{12... | collective-permute-start | bytes 983048 | tf_op jit(solution)/shard_map/mid_sums/ppermute | solution.py:25
  12.3 1.3 %collective-permute-start.3 = (bf16[10,128,128]{2,1,0:T(8,128)(2,1)S(1)}, bf16[10,128,128]{2,1,0:T(8,128)(2,1)S(1)}, u32[]{:S(2)}, u32[]{:S(2)}) collective-permute-start(bf16[10,128,128]{2,1,0:T(8,128)(2,1)S(1)} %get-tuple-element.26.sent_ref), channel_id=1, source_target_pairs={{0,6},{2,0},{4,2},{6,4},{1,7},{3,1},{5,3},{7,5},{8,14},{10,8},{12,... | collective-permute-start | bytes 983048 | tf_op jit(solution)/shard_map/mid_sums/ppermute | solution.py:25
  13.6 5.2 %collective-permute-done.1.refs_0_ = bf16[10,128,128]{2,1,0:T(8,128)(2,1)S(1)} collective-permute-done((bf16[10,128,128]{2,1,0:T(8,128)(2,1)S(1)}, bf16[10,128,128]{2,1,0:T(8,128)(2,1)S(1)}, u32[]{:S(2)}, u32[]{:S(2)}) %collective-permute-start.1) | collective-permute-done | bytes 327712 | tf_op jit(solution)/shard_map/mid_sums/ppermute | solution.py:25
  18.8 8.2 %collective-permute-done.2.refs_1_ = bf16[10,128,128]{2,1,0:T(8,128)(2,1)S(1)} collective-permute-done((bf16[10,128,128]{2,1,0:T(8,128)(2,1)S(1)}, bf16[10,128,128]{2,1,0:T(8,128)(2,1)S(1)}, u32[]{:S(2)}, u32[]{:S(2)}) %collective-permute-start.2) | collective-permute-done | bytes 327712 | tf_op jit(solution)/shard_map/mid_sums/ppermute | solution.py:25
  27.2 1.3 %collective-permute-done.4.other_ref = bf16[4,128,128]{2,1,0:T(8,128)(2,1)S(1)} collective-permute-done((bf16[4,128,128]{2,1,0:T(8,128)(2,1)S(1)}, bf16[4,128,128]{2,1,0:T(8,128)(2,1)S(1)}, u32[]{:S(2)}, u32[]{:S(2)}) %collective-permute-start.4) | collective-permute-done | bytes 131104 | tf_op jit(solution)/shard_map/mid_sums/ppermute | solution.py:25
  28.6 1.4 %products.1 = bf16[8,1168,128]{2,1,0:T(8,128)(2,1)S(1)} custom-call(s32[8]{0:T(128)S(1)} %bitcast.8, s32[8]{0:T(128)S(1)} %copy-done.9, s32[32]{0:T(128)S(1)} %copy-done.10, bf16[1024,1024]{1,0:T(8,128)(2,1)S(1)} %copy-done.1, bf16[4,128,128]{2,1,0:T(8,128)(2,1)S(1)} %get-tuple-element.27.mids_ref, ...), custom_call_target="tpu_custom_call" | custom-call | tf_op jit(solution)/shard_map/terms_over_first/products/pallas_call | solution.py:170
  30.0 1.4 %copy-done = bf16[8,1168,128]{2,1,0:T(8,128)(2,1)} copy-done((bf16[8,1168,128]{2,1,0:T(8,128)(2,1)}, bf16[8,1168,128]{2,1,0:T(8,128)(2,1)S(1)}, u32[]{:S(2)}) %copy-start) | copy-done | bytes 2392088
  31.4 5.9 %all-to-all-start = ((bf16[8,1168,128]{2,1,0:T(8,128)(2,1)}), bf16[8,1168,128]{2,1,0:T(8,128)(2,1)S(1)}, u32[]{:S(2)}, u32[]{:S(2)}) async-start(bf16[8,1168,128]{2,1,0:T(8,128)(2,1)} %copy-done), calls=%async_computation | async-start | bytes 4784128 | tf_op jit(solution)/shard_map/terms_over_first/all_to_all | solution.py:315
  37.4 1.6 %copy-done.2 = bf16[1024,1024]{1,0:T(8,128)(2,1)S(1)} copy-done((bf16[1024,1024]{1,0:T(8,128)(2,1)S(1)}, bf16[1024,1024]{1,0:T(8,128)(2,1)}, u32[]{:S(2)}) %copy-start.2) | copy-done | bytes 2097176
  39.0 1.6 %copy-done.4 = bf16[1024,1024]{1,0:T(8,128)(2,1)S(1)} copy-done((bf16[1024,1024]{1,0:T(8,128)(2,1)S(1)}, bf16[1024,1024]{1,0:T(8,128)(2,1)}, u32[]{:S(2)}) %copy-start.4) | copy-done | bytes 2097176
  40.6 4.5 %keys_partials.1 = (f32[4,128,1024]{2,1,0:T(8,128)S(1)}, f32[4,128,1024]{2,1,0:T(8,128)S(1)}) custom-call(s32[2]{0:T(128)S(1)} %pad_add_fusion.place_ref, bf16[1024,1024]{1,0:T(8,128)(2,1)S(1)} %copy-done.2, bf16[1024,1024]{1,0:T(8,128)(2,1)S(1)} %copy-done.4, bf16[8,128,128]{2,1,0:T(8,128)(2,1)S(1)} %get-tuple-element.28.saved_ref, ...), custom_call_target="tpu_custom_call" | custom-call | tf_op jit(solution)/shard_map/keys_core/keys_partials/pallas_call | solution.py:251
  45.1 4.1 %collective-permute-done.5.received_ref = f32[4,128,1024]{2,1,0:T(8,128)S(1)} collective-permute-done((f32[4,128,1024]{2,1,0:T(8,128)S(1)}, f32[4,128,1024]{2,1,0:T(8,128)S(1)}, u32[]{:S(2)}, u32[]{:S(2)}) %collective-permute-start.5) | collective-permute-done | bytes 2097184 | tf_op jit(solution)/shard_map/keys_core/ppermute | solution.py:25
  49.3 0.2 keys_chip_sums.1
  49.5 0.8 copy-done.11
  50.3 0.8 copy-done.13
  51.1 15.4 %all-to-all-done.terms_ref = bf16[8,1168,128]{2,1,0:T(8,128)(2,1)S(1)} async-done(((bf16[8,1168,128]{2,1,0:T(8,128)(2,1)}), bf16[8,1168,128]{2,1,0:T(8,128)(2,1)S(1)}, u32[]{:S(2)}, u32[]{:S(2)}) %all-to-all-start) | async-done | bytes 2392096 | tf_op jit(solution)/shard_map/terms_over_first/all_to_all | solution.py:315
  66.7 1.5 %slot_sums.1 = bf16[32,144,128]{2,1,0:T(8,128)(2,1)S(1)} custom-call(s32[8,8]{1,0:T(8,128)S(1)} %convert_reduce_fusion.slots_ref, bf16[8,1168,128]{2,1,0:T(8,128)(2,1)S(1)} %all-to-all-done.terms_ref), custom_call_target="tpu_custom_call" | custom-call | tf_op jit(solution)/shard_map/sums_over_adapter/slot_sums/pallas_call | solution.py:192
  68.2 1.0 copy-done.3
  69.3 10.0 %all-to-all-start.1 = ((bf16[32,144,128]{2,1,0:T(8,128)(2,1)}), bf16[32,144,128]{2,1,0:T(8,128)(2,1)S(1)}, u32[]{:S(2)}, u32[]{:S(2)}) async-start(bf16[32,144,128]{2,1,0:T(8,128)(2,1)} %copy-done.3), calls=%async_computation.1 | async-start | bytes 2359296 | tf_op jit(solution)/shard_map/sums_over_adapter/all_to_all | solution.py:329
  79.2 1.3 %collective-permute-start.6 = (f32[128,1024]{1,0:T(8,128)S(1)}, f32[128,1024]{1,0:T(8,128)S(1)}, u32[]{:S(2)}, u32[]{:S(2)}) collective-permute-start(f32[128,1024]{1,0:T(8,128)S(1)} %copy-done.14), channel_id=1, source_target_pairs={{0,2},{2,4},{4,6},{6,0},{1,3},{3,5},{5,7},{7,1},{8,10},{10,12},{12... | collective-permute-start | bytes 1572872 | tf_op jit(solution)/shard_map/keys_y/ppermute | solution.py:25
  80.6 2.4 %collective-permute-start.7 = (f32[128,1024]{1,0:T(8,128)S(1)}, f32[128,1024]{1,0:T(8,128)S(1)}, u32[]{:S(2)}, u32[]{:S(2)}) collective-permute-start(f32[128,1024]{1,0:T(8,128)S(1)} %copy-done.12), channel_id=1, source_target_pairs={{0,4},{2,6},{4,0},{6,2},{1,5},{3,7},{5,1},{7,3},{8,12},{10,14},{12... | collective-permute-start | bytes 1572872 | tf_op jit(solution)/shard_map/keys_y/ppermute | solution.py:25
  82.9 1.6 %collective-permute-start.8 = (f32[128,1024]{1,0:T(8,128)S(1)}, f32[128,1024]{1,0:T(8,128)S(1)}, u32[]{:S(2)}, u32[]{:S(2)}) collective-permute-start(f32[128,1024]{1,0:T(8,128)S(1)} %get-tuple-element.39), channel_id=1, source_target_pairs={{0,6},{2,0},{4,2},{6,4},{1,7},{3,1},{5,3},{7,5},{8,14},{10,8},{12,... | collective-permute-start | bytes 1572872 | tf_op jit(solution)/shard_map/keys_y/ppermute | solution.py:25
  84.5 10.5 %collective-permute-done.6 = f32[128,1024]{1,0:T(8,128)S(1)} collective-permute-done((f32[128,1024]{1,0:T(8,128)S(1)}, f32[128,1024]{1,0:T(8,128)S(1)}, u32[]{:S(2)}, u32[]{:S(2)}) %collective-permute-start.6) | collective-permute-done | bytes 524320 | tf_op jit(solution)/shard_map/keys_y/ppermute | solution.py:25
  95.0 9.5 %collective-permute-done.7 = f32[128,1024]{1,0:T(8,128)S(1)} collective-permute-done((f32[128,1024]{1,0:T(8,128)S(1)}, f32[128,1024]{1,0:T(8,128)S(1)}, u32[]{:S(2)}, u32[]{:S(2)}) %collective-permute-start.7) | collective-permute-done | bytes 524320 | tf_op jit(solution)/shard_map/keys_y/ppermute | solution.py:25
  104.5 0.2 collective-permute-done.8
  104.7 0.8 add_convert_fusion
  105.6 4.1 %all-to-all-done.1 = bf16[32,144,128]{2,1,0:T(8,128)(2,1)S(1)} async-done(((bf16[32,144,128]{2,1,0:T(8,128)(2,1)}), bf16[32,144,128]{2,1,0:T(8,128)(2,1)S(1)}, u32[]{:S(2)}, u32[]{:S(2)}) %all-to-all-start.1) | async-done | bytes 1179680 | tf_op jit(solution)/shard_map/sums_over_adapter/all_to_all | solution.py:329
  109.7 1.0 finish.1
  (31 shorter events, 0.8 us)
Async XLA Ops:
  0.6 27.9 %copy-start.5 = (bf16[1024,128]{1,0:T(8,128)(2,1)S(1)}, bf16[1024,128]{1,0:T(8,128)(2,1)}, u32[]{:S(2)}) copy-start(bf16[1024,128]{1,0:T(8,128)(2,1)} %cot_ref.3) | copy-start | bytes 786436
  0.6 27.9 %copy-start.1 = (bf16[1024,1024]{1,0:T(8,128)(2,1)S(1)}, bf16[1024,1024]{1,0:T(8,128)(2,1)}, u32[]{:S(2)}) copy-start(bf16[1024,1024]{1,0:T(8,128)(2,1)} %tokens_ref.3) | copy-start | bytes 6291460
  4.7 1.9 %collective-permute-start = (f32[5,128,128]{2,1,0:T(8,128)}, f32[5,128,128]{2,1,0:T(8,128)S(1)}, u32[]{:S(2)}, u32[]{:S(2)}) collective-permute-start(f32[5,128,128]{2,1,0:T(8,128)} %get-tuple-element.24), channel_id=1, source_target_pairs={{0,1},{1,0},{2,3},{3,2},{4,5},{5,4},{6,7},{7,6},{8,9},{9,8},{10,11... | collective-permute-start | bytes 983048 | tf_op jit(solution)/shard_map/mid_sums/ppermute | solution.py:25
  6.7 1.0 copy-start.6
  7.6 20.9 %copy-start.8 = (s32[8,1]{0,1:T(1,128)S(1)}, s32[8,1]{0,1:T(1,128)}, u32[]{:S(2)}) copy-start(s32[8,1]{0,1:T(1,128)} %param.13) | copy-start | bytes 100
  7.6 21.0 %copy-start.9 = (s32[8]{0:T(128)S(1)}, s32[8]{0:T(128)}, u32[]{:S(2)}) copy-start(s32[8]{0:T(128)} %fill_ref.3) | copy-start | bytes 100
  7.6 21.0 %copy-start.10 = (s32[32]{0:T(128)S(1)}, s32[32]{0:T(128)}, u32[]{:S(2)}) copy-start(s32[32]{0:T(128)} %slot_ref.1) | copy-start | bytes 388
  7.7 11.1 %collective-permute-start.1 = (bf16[10,128,128]{2,1,0:T(8,128)(2,1)S(1)}, bf16[10,128,128]{2,1,0:T(8,128)(2,1)S(1)}, u32[]{:S(2)}, u32[]{:S(2)}) collective-permute-start(bf16[10,128,128]{2,1,0:T(8,128)(2,1)S(1)} %get-tuple-element.26.sent_ref), channel_id=1, source_target_pairs={{0,2},{2,4},{4,6},{6,0},{1,3},{3,5},{5,7},{7,1},{8,10},{10,12},{12... | collective-permute-start | bytes 983048 | tf_op jit(solution)/shard_map/mid_sums/ppermute | solution.py:25
  9.4 17.6 %collective-permute-start.2 = (bf16[10,128,128]{2,1,0:T(8,128)(2,1)S(1)}, bf16[10,128,128]{2,1,0:T(8,128)(2,1)S(1)}, u32[]{:S(2)}, u32[]{:S(2)}) collective-permute-start(bf16[10,128,128]{2,1,0:T(8,128)(2,1)S(1)} %get-tuple-element.26.sent_ref), channel_id=1, source_target_pairs={{0,4},{2,6},{4,0},{6,2},{1,5},{3,7},{5,1},{7,3},{8,12},{10,14},{12... | collective-permute-start | bytes 983048 | tf_op jit(solution)/shard_map/mid_sums/ppermute | solution.py:25
  12.3 14.8 %collective-permute-start.3 = (bf16[10,128,128]{2,1,0:T(8,128)(2,1)S(1)}, bf16[10,128,128]{2,1,0:T(8,128)(2,1)S(1)}, u32[]{:S(2)}, u32[]{:S(2)}) collective-permute-start(bf16[10,128,128]{2,1,0:T(8,128)(2,1)S(1)} %get-tuple-element.26.sent_ref), channel_id=1, source_target_pairs={{0,6},{2,0},{4,2},{6,4},{1,7},{3,1},{5,3},{7,5},{8,14},{10,8},{12,... | collective-permute-start | bytes 983048 | tf_op jit(solution)/shard_map/mid_sums/ppermute | solution.py:25
  27.1 1.4 %collective-permute-start.4 = (bf16[4,128,128]{2,1,0:T(8,128)(2,1)S(1)}, bf16[4,128,128]{2,1,0:T(8,128)(2,1)S(1)}, u32[]{:S(2)}, u32[]{:S(2)}) collective-permute-start(bf16[4,128,128]{2,1,0:T(8,128)(2,1)S(1)} %get-tuple-element.27.mids_ref), channel_id=1, source_target_pairs={{0,1},{1,0},{2,3},{3,2},{4,5},{5,4},{6,7},{7,6},{8,9},{9,8},{10,11... | collective-permute-start | bytes 393224 | tf_op jit(solution)/shard_map/mid_sums/ppermute | solution.py:25
  30.0 1.4 %copy-start = (bf16[8,1168,128]{2,1,0:T(8,128)(2,1)}, bf16[8,1168,128]{2,1,0:T(8,128)(2,1)S(1)}, u32[]{:S(2)}) copy-start(bf16[8,1168,128]{2,1,0:T(8,128)(2,1)S(1)} %products.1) | copy-start | bytes 7176196
  31.4 6.0 %copy-start.7 = (bf16[8,128,128]{2,1,0:T(8,128)(2,1)S(1)}, bf16[8,128,128]{2,1,0:T(8,128)(2,1)}, u32[]{:S(2)}) copy-start(bf16[8,128,128]{2,1,0:T(8,128)(2,1)} %get-tuple-element.29.picked_ref) | copy-start | bytes 786436
  31.4 35.1 %all-to-all-start = ((bf16[8,1168,128]{2,1,0:T(8,128)(2,1)}), bf16[8,1168,128]{2,1,0:T(8,128)(2,1)S(1)}, u32[]{:S(2)}, u32[]{:S(2)}) async-start(bf16[8,1168,128]{2,1,0:T(8,128)(2,1)} %copy-done), calls=%async_computation | async-start | bytes 4784128 | tf_op jit(solution)/shard_map/terms_over_first/all_to_all | solution.py:315
  37.4 1.6 %copy-start.2 = (bf16[1024,1024]{1,0:T(8,128)(2,1)S(1)}, bf16[1024,1024]{1,0:T(8,128)(2,1)}, u32[]{:S(2)}) copy-start(bf16[1024,1024]{1,0:T(8,128)(2,1)} %tokens_ref.3) | copy-start | bytes 6291460
  39.0 1.6 %copy-start.4 = (bf16[1024,1024]{1,0:T(8,128)(2,1)S(1)}, bf16[1024,1024]{1,0:T(8,128)(2,1)}, u32[]{:S(2)}) copy-start(bf16[1024,1024]{1,0:T(8,128)(2,1)} %weight_ref.1) | copy-start | bytes 6291460
  45.0 4.2 %collective-permute-start.5 = (f32[4,128,1024]{2,1,0:T(8,128)S(1)}, f32[4,128,1024]{2,1,0:T(8,128)S(1)}, u32[]{:S(2)}, u32[]{:S(2)}) collective-permute-start(f32[4,128,1024]{2,1,0:T(8,128)S(1)} %get-tuple-element.31), channel_id=1, source_target_pairs={{0,1},{1,0},{2,3},{3,2},{4,5},{5,4},{6,7},{7,6},{8,9},{9,8},{10,11... | collective-permute-start | bytes 6291464 | tf_op jit(solution)/shard_map/keys_core/ppermute | solution.py:25
  49.5 0.8 copy-start.11
  50.3 0.8 copy-start.13
  68.2 1.0 copy-start.3
  69.3 10.0 %copy-start.14 = (f32[128,1024]{1,0:T(8,128)S(1)}, f32[128,1024]{1,0:T(8,128)}, u32[]{:S(2)}) copy-start(f32[128,1024]{1,0:T(8,128)} %copy-done.13) | copy-start | bytes 1572868
  69.3 11.3 %copy-start.12 = (f32[128,1024]{1,0:T(8,128)S(1)}, f32[128,1024]{1,0:T(8,128)}, u32[]{:S(2)}) copy-start(f32[128,1024]{1,0:T(8,128)} %copy-done.11) | copy-start | bytes 1572868
  69.3 40.4 %all-to-all-start.1 = ((bf16[32,144,128]{2,1,0:T(8,128)(2,1)}), bf16[32,144,128]{2,1,0:T(8,128)(2,1)S(1)}, u32[]{:S(2)}, u32[]{:S(2)}) async-start(bf16[32,144,128]{2,1,0:T(8,128)(2,1)} %copy-done.3), calls=%async_computation.1 | async-start | bytes 2359296 | tf_op jit(solution)/shard_map/sums_over_adapter/all_to_all | solution.py:329
  79.2 15.8 %collective-permute-start.6 = (f32[128,1024]{1,0:T(8,128)S(1)}, f32[128,1024]{1,0:T(8,128)S(1)}, u32[]{:S(2)}, u32[]{:S(2)}) collective-permute-start(f32[128,1024]{1,0:T(8,128)S(1)} %copy-done.14), channel_id=1, source_target_pairs={{0,2},{2,4},{4,6},{6,0},{1,3},{3,5},{5,7},{7,1},{8,10},{10,12},{12... | collective-permute-start | bytes 1572872 | tf_op jit(solution)/shard_map/keys_y/ppermute | solution.py:25
  80.6 23.9 %collective-permute-start.7 = (f32[128,1024]{1,0:T(8,128)S(1)}, f32[128,1024]{1,0:T(8,128)S(1)}, u32[]{:S(2)}, u32[]{:S(2)}) collective-permute-start(f32[128,1024]{1,0:T(8,128)S(1)} %copy-done.12), channel_id=1, source_target_pairs={{0,4},{2,6},{4,0},{6,2},{1,5},{3,7},{5,1},{7,3},{8,12},{10,14},{12... | collective-permute-start | bytes 1572872 | tf_op jit(solution)/shard_map/keys_y/ppermute | solution.py:25
  82.9 21.8 %collective-permute-start.8 = (f32[128,1024]{1,0:T(8,128)S(1)}, f32[128,1024]{1,0:T(8,128)S(1)}, u32[]{:S(2)}, u32[]{:S(2)}) collective-permute-start(f32[128,1024]{1,0:T(8,128)S(1)} %get-tuple-element.39), channel_id=1, source_target_pairs={{0,6},{2,0},{4,2},{6,4},{1,7},{3,1},{5,3},{7,5},{8,14},{10,8},{12,... | collective-permute-start | bytes 1572872 | tf_op jit(solution)/shard_map/keys_y/ppermute | solution.py:25

commit v4 on v3

--- a/solution.py
+++ b/solution.py
@@ -82,50 +82,82 @@
     )(jobs, fills, up_stack, cotangent, saved)
 
 
-def y_payload(own, received):
+def halves_of(total):
+    high = total.astype(BF16)
+    return high, (total - high.astype(F32)).astype(BF16)
+
+
+def y_first(own, received):
     half, _, rank = own.shape
     half -= 1
-
-    def kernel(own_ref, received_ref, keep_ref, out_ref):
+    each = half // 2
+
+    def kernel(own_ref, received_ref, keep_ref, *outs):
         first = lax.axis_index("core") == 0
         mine, theirs = own_ref[half], received_ref[half]
-        out_ref[2 * half] = jnp.where(first, mine, theirs).astype(BF16)
-        out_ref[2 * half + 1] = jnp.where(first, theirs, mine).astype(BF16)
         total = own_ref[:half] + received_ref[:half]
         keep_ref[...] = total
-        high = total.astype(BF16)
-        out_ref[:half] = high
-        out_ref[half : 2 * half] = (total - high.astype(F32)).astype(BF16)
-
-    return pl.pallas_call(
-        kernel,
-        out_shape=[
-            jax.ShapeDtypeStruct((half, BLK, rank), F32),
-            jax.ShapeDtypeStruct((2 * half + 2, BLK, rank), BF16),
-        ],
+        for i, out in enumerate(outs):
+            out[:each], out[each : 2 * each] = halves_of(total[i * each : (i + 1) * each])
+            saved = jnp.where(first, mine, theirs) if i == 0 else jnp.where(first, theirs, mine)
+            out[2 * each] = saved.astype(BF16)
+
+    return pl.pallas_call(
+        kernel,
+        out_shape=[jax.ShapeDtypeStruct((half, BLK, rank), F32)]
+        + [jax.ShapeDtypeStruct((2 * each + 1, BLK, rank), BF16)] * 2,
         in_specs=[VMEM] * 2,
-        out_specs=[VMEM] * 2,
-        compiler_params=LIMIT,
-        name="y_payload",
+        out_specs=[VMEM] * 3,
+        compiler_params=LIMIT,
+        name="y_first",
     )(own, received)
 
 
-def mid_grads(keep, sent, received):
+def y_second(keep, sent, received):
     half, _, rank = keep.shape
-    ny = len(received) + 1
-
-    def kernel(keep_ref, sent_ref, *refs):
-        got = refs[: ny - 1]
-        mids_ref, rows_ref = refs[ny - 1 :]
+    each = half // 2
+
+    def kernel(keep_ref, *refs):
+        sent_refs, got_refs, total_ref, outs = refs[:2], refs[2:4], refs[4], refs[5:]
+        for i in range(2):
+            got = got_refs[i]
+            blocks = slice(i * each, (i + 1) * each)
+            total = keep_ref[blocks] + got[:each].astype(F32) + got[each : 2 * each].astype(F32)
+            total_ref[blocks] = total
+            outs[i][:each], outs[i][each : 2 * each] = halves_of(total)
+            outs[i][2 * each] = sent_refs[i][2 * each]
+            outs[i][2 * each + 1] = got[2 * each]
+
+    return pl.pallas_call(
+        kernel,
+        out_shape=[jax.ShapeDtypeStruct(keep.shape, F32)]
+        + [jax.ShapeDtypeStruct((2 * each + 2, BLK, rank), BF16)] * 2,
+        in_specs=[VMEM] * 5,
+        out_specs=[VMEM] * 3,
+        compiler_params=LIMIT,
+        name="y_second",
+    )(keep, *sent, *received)
+
+
+def mid_grads(total, sent, received):
+    half, _, rank = total.shape
+    each = half // 2
+
+    def kernel(total_ref, *refs):
+        sent_refs, got_refs, mids_ref, rows_ref = refs[:2], refs[2:4], refs[4], refs[5]
         y = lax.axis_index("y")
-        total = keep_ref[...]
-        for ref in got:
-            total += ref[:half].astype(F32) + ref[half : 2 * half].astype(F32)
-        mids_ref[...] = total.astype(BF16)
-        for d, ref in enumerate((sent_ref,) + got):
-            source = lax.rem(y + ny - d, ny)
-            rows_ref[2 * source] = ref[2 * half]
-            rows_ref[2 * source + 1] = ref[2 * half + 1]
+        pair, mirror = lax.bitwise_xor(y, 1), half - 1 - y
+        for i, (near, far) in enumerate(((pair, mirror), (mirror, pair))):
+            got = got_refs[i]
+            blocks = slice(i * each, (i + 1) * each)
+            mids_ref[blocks] = (
+                total_ref[blocks] + got[:each].astype(F32) + got[each : 2 * each].astype(F32)
+            ).astype(BF16)
+            beyond = lax.bitwise_xor(far, 1) if i == 0 else half - 1 - far
+            rows_ref[2 * y + i] = sent_refs[i][2 * each]
+            rows_ref[2 * near + i] = sent_refs[i][2 * each + 1]
+            rows_ref[2 * far + i] = got[2 * each]
+            rows_ref[2 * beyond + i] = got[2 * each + 1]
 
     return pl.pallas_call(
         kernel,
@@ -133,11 +165,11 @@
             jax.ShapeDtypeStruct((half, BLK, rank), BF16),
             jax.ShapeDtypeStruct((2 * half, BLK, rank), BF16),
         ],
-        in_specs=[VMEM] * (ny + 1),
+        in_specs=[VMEM] * 5,
         out_specs=[VMEM] * 2,
         compiler_params=LIMIT,
         name="mid_grads",
-    )(keep, sent, *received)
+    )(total, *sent, *received)
 
 
 def products(jobs, fills, slot_of, tokens, mids, mids_other, saved_rows, cotangent, parts):
@@ -304,9 +336,13 @@
 
     with jax.named_scope("mid_sums"):
         own, other, picked = mid_partials(jobs, block_fill, up_stack, cotangent, saved_mid)
-        keep, sent = y_payload(own, shift(other, "core", 1))
-        received = [shift(sent, "y", d) for d in range(1, ny)]
-        mids, saved_rows = mid_grads(keep, sent, received)
+        keep, *sent = y_first(own, shift(other, "core", 1))
+        pair = [(i, i ^ 1) for i in range(ny)]
+        mirror = [(i, ny - 1 - i) for i in range(ny)]
+        received = [lax.ppermute(sent[0], "y", pair), lax.ppermute(sent[1], "y", mirror)]
+        total, *sent = y_second(keep, sent, received)
+        received = [lax.ppermute(sent[0], "y", mirror), lax.ppermute(sent[1], "y", pair)]
+        mids, saved_rows = mid_grads(total, sent, received)
         mids_other = shift(mids, "core", 1)
     with jax.named_scope("terms_over_first"):
         terms = products(

time: 111 us -> 109 us (0.982)
  starting transfers between devices: 27.3 us -> 25.6 us
    ppermute x9 -> x6, waiting for transfers between devices: 40.9 us -> 29.5 us  [shift(): lax.ppermute(value, axis, [(i, (i + distance) % size) for i in range(size)])]
    ppermute x0 -> x4, waiting for transfers between devices: none -> 10.7 us  [the longest x1 4.82 us: per_device(): lax.ppermute(sent[0], 'y', mirror)]
    ppermute x9 -> x6, starting transfers between devices: 11.5 us -> 3.6 us  [shift(): lax.ppermute(value, axis, [(i, (i + distance) % size) for i in range(size)])]
    ppermute x0 -> x4, starting transfers between devices: none -> 6.11 us  [the longest x1 2.27 us: per_device(): lax.ppermute(sent[0], 'y', mirror)]
  transfers between devices with their start and end apart: 11 -> 12, of which waited for: 10 -> 11; matrix products, arithmetic and copies ran while one was open for 1% -> 1% of each run, Pallas kernels for 4% -> 4%
where the time goes in v4:
time: 109 us; the launch traced here: 108 us
  waiting for transfers between devices  59.7 us (55%)
  starting transfers between devices  25.6 us (23%)
  Pallas kernels  12.7 us (12%)
  local copies, waits for them, and re-layouts  8.21 us (8%)
  other arithmetic  1.12 us (1%)
    ppermute x6, waiting for transfers between devices, shift(): lax.ppermute(value, axis, [(i, (i + distance) % size) for i in range(size)])  29.5 us
    all_to_all x1, waiting for transfers between devices, per_device(): lax.all_to_all(terms, FIRST, split_axis=0, concat_axis=0, tiled=True)  15.4 us
    all_to_all x1, starting transfers between devices, per_device(): lax.all_to_all(sums, ADAPTER, split_axis=0, concat_axis=0, tiled=True)  9.96 us
    unnamed x30, local copies, waits for them, and re-layouts  8.21 us
    all_to_all x1, starting transfers between devices, per_device(): lax.all_to_all(terms, FIRST, split_axis=0, concat_axis=0, tiled=True)  5.89 us
    ppermute x1, waiting for transfers between devices, per_device(): lax.ppermute(sent[0], 'y', mirror)  4.82 us
    pallas_call x1, Pallas kernels, keys_partials(): pl.pallas_call(kernel, grid_spec=pltpu.PrefetchScalarGridSpec(num_scalar_...  4.47 us
    all_to_all x1, waiting for transfers between devices, per_device(): lax.all_to_all(sums, ADAPTER, split_axis=0, concat_axis=0, tiled=True)  4.1 us
  transfers between devices with their start and end apart: 12, of which 11 were waited for; matrix products, arithmetic and copies ran while one was open for 1% of the time, Pallas kernels for 4%

profile of v4, /device:TPU:32, one launch (start us, length us, event | category | flops | bytes accessed | tf_op | source)
XLA Modules:
  0.0 108.1 jit_solution(3866347021123646862)
XLA Ops:
  0.7 4.1 %mid_partials.1 = (f32[5,128,128]{2,1,0:T(8,128)}, f32[5,128,128]{2,1,0:T(8,128)}, bf16[8,128,128]{2,1,0:T(8,128)(2,1)}) custom-call(s32[8]{0:T(128)} %bitcast.7, s32[8]{0:T(128)} %fill_ref.3, bf16[32,128,128]{2,1,0:T(8,128)(2,1)} %up_ref.1, bf16[1024,128]{1,0:T(8,128)(2,1)} %cot_ref.3, bf16[128,128]{1,0:T(8,128)(2,1)} %saved_ref.1), custom_call_target="tpu_custom_call" | custom-call | tf_op jit(solution)/shard_map/mid_sums/mid_partials/pallas_call | solution.py:71
  4.8 1.8 %collective-permute-done.received_ref = f32[5,128,128]{2,1,0:T(8,128)S(1)} collective-permute-done((f32[5,128,128]{2,1,0:T(8,128)}, f32[5,128,128]{2,1,0:T(8,128)S(1)}, u32[]{:S(2)}, u32[]{:S(2)}) %collective-permute-start) | collective-permute-done | bytes 327712 | tf_op jit(solution)/shard_map/mid_sums/ppermute | solution.py:25
  6.7 1.0 copy-done.6
  7.7 1.7 %collective-permute-start.1 = (bf16[5,128,128]{2,1,0:T(8,128)(2,1)S(1)}, bf16[5,128,128]{2,1,0:T(8,128)(2,1)S(1)}, u32[]{:S(2)}, u32[]{:S(2)}) collective-permute-start(bf16[5,128,128]{2,1,0:T(8,128)(2,1)S(1)} %get-tuple-element.30.refs_0_), channel_id=1, source_target_pairs={{0,2},{2,0},{4,6},{6,4},{1,3},{3,1},{5,7},{7,5},{8,10},{10,8},{12,... | collective-permute-start | bytes 491528 | tf_op jit(solution)/shard_map/mid_sums/ppermute | solution.py:342
  9.4 2.2 %collective-permute-start.2 = (bf16[5,128,128]{2,1,0:T(8,128)(2,1)S(1)}, bf16[5,128,128]{2,1,0:T(8,128)(2,1)S(1)}, u32[]{:S(2)}, u32[]{:S(2)}) collective-permute-start(bf16[5,128,128]{2,1,0:T(8,128)(2,1)S(1)} %get-tuple-element.31.refs_1_), channel_id=1, source_target_pairs={{0,6},{2,4},{4,2},{6,0},{1,7},{3,5},{5,3},{7,1},{8,14},{10,12},{12... | collective-permute-start | bytes 491528 | tf_op jit(solution)/shard_map/mid_sums/ppermute | solution.py:342
  11.5 2.5 %collective-permute-done.1.refs_2_ = bf16[5,128,128]{2,1,0:T(8,128)(2,1)S(1)} collective-permute-done((bf16[5,128,128]{2,1,0:T(8,128)(2,1)S(1)}, bf16[5,128,128]{2,1,0:T(8,128)(2,1)S(1)}, u32[]{:S(2)}, u32[]{:S(2)}) %collective-permute-start.1) | collective-permute-done | bytes 163872 | tf_op jit(solution)/shard_map/mid_sums/ppermute | solution.py:342
  14.0 2.5 %collective-permute-done.2.refs_3_ = bf16[5,128,128]{2,1,0:T(8,128)(2,1)S(1)} collective-permute-done((bf16[5,128,128]{2,1,0:T(8,128)(2,1)S(1)}, bf16[5,128,128]{2,1,0:T(8,128)(2,1)S(1)}, u32[]{:S(2)}, u32[]{:S(2)}) %collective-permute-start.2) | collective-permute-done | bytes 163872 | tf_op jit(solution)/shard_map/mid_sums/ppermute | solution.py:342
  16.6 2.3 %collective-permute-start.3 = (bf16[6,128,128]{2,1,0:T(8,128)(2,1)S(1)}, bf16[6,128,128]{2,1,0:T(8,128)(2,1)S(1)}, u32[]{:S(2)}, u32[]{:S(2)}) collective-permute-start(bf16[6,128,128]{2,1,0:T(8,128)(2,1)S(1)} %get-tuple-element.33.refs_0_), channel_id=1, source_target_pairs={{0,6},{2,4},{4,2},{6,0},{1,7},{3,5},{5,3},{7,1},{8,14},{10,12},{12... | collective-permute-start | bytes 589832 | tf_op jit(solution)/shard_map/mid_sums/ppermute | solution.py:344
  18.9 4.8 %collective-permute-done.3.refs_2_ = bf16[6,128,128]{2,1,0:T(8,128)(2,1)S(1)} collective-permute-done((bf16[6,128,128]{2,1,0:T(8,128)(2,1)S(1)}, bf16[6,128,128]{2,1,0:T(8,128)(2,1)S(1)}, u32[]{:S(2)}, u32[]{:S(2)}) %collective-permute-start.3) | collective-permute-done | bytes 196640 | tf_op jit(solution)/shard_map/mid_sums/ppermute | solution.py:344
  23.7 0.8 collective-permute-done.4.refs_3_
  24.7 1.3 %collective-permute-done.5.other_ref = bf16[4,128,128]{2,1,0:T(8,128)(2,1)S(1)} collective-permute-done((bf16[4,128,128]{2,1,0:T(8,128)(2,1)S(1)}, bf16[4,128,128]{2,1,0:T(8,128)(2,1)S(1)}, u32[]{:S(2)}, u32[]{:S(2)}) %collective-permute-start.5) | collective-permute-done | bytes 131104 | tf_op jit(solution)/shard_map/mid_sums/ppermute | solution.py:25
  26.1 1.4 %products.1 = bf16[8,1168,128]{2,1,0:T(8,128)(2,1)S(1)} custom-call(s32[8]{0:T(128)S(1)} %bitcast.8, s32[8]{0:T(128)S(1)} %copy-done.9, s32[32]{0:T(128)S(1)} %copy-done.10, bf16[1024,1024]{1,0:T(8,128)(2,1)S(1)} %copy-done.1, bf16[4,128,128]{2,1,0:T(8,128)(2,1)S(1)} %get-tuple-element.35.mids_ref, ...), custom_call_target="tpu_custom_call" | custom-call | tf_op jit(solution)/shard_map/terms_over_first/products/pallas_call | solution.py:202
  27.5 1.4 %copy-done = bf16[8,1168,128]{2,1,0:T(8,128)(2,1)} copy-done((bf16[8,1168,128]{2,1,0:T(8,128)(2,1)}, bf16[8,1168,128]{2,1,0:T(8,128)(2,1)S(1)}, u32[]{:S(2)}) %copy-start) | copy-done | bytes 2392088
  28.9 5.9 %all-to-all-start = ((bf16[8,1168,128]{2,1,0:T(8,128)(2,1)}), bf16[8,1168,128]{2,1,0:T(8,128)(2,1)S(1)}, u32[]{:S(2)}, u32[]{:S(2)}) async-start(bf16[8,1168,128]{2,1,0:T(8,128)(2,1)} %copy-done), calls=%async_computation | async-start | bytes 4784128 | tf_op jit(solution)/shard_map/terms_over_first/all_to_all | solution.py:351
  34.8 1.6 %copy-done.2 = bf16[1024,1024]{1,0:T(8,128)(2,1)S(1)} copy-done((bf16[1024,1024]{1,0:T(8,128)(2,1)S(1)}, bf16[1024,1024]{1,0:T(8,128)(2,1)}, u32[]{:S(2)}) %copy-start.2) | copy-done | bytes 2097176
  36.4 1.6 %copy-done.4 = bf16[1024,1024]{1,0:T(8,128)(2,1)S(1)} copy-done((bf16[1024,1024]{1,0:T(8,128)(2,1)S(1)}, bf16[1024,1024]{1,0:T(8,128)(2,1)}, u32[]{:S(2)}) %copy-start.4) | copy-done | bytes 2097176
  38.0 4.5 %keys_partials.1 = (f32[4,128,1024]{2,1,0:T(8,128)S(1)}, f32[4,128,1024]{2,1,0:T(8,128)S(1)}) custom-call(s32[2]{0:T(128)S(1)} %pad_add_fusion.place_ref, bf16[1024,1024]{1,0:T(8,128)(2,1)S(1)} %copy-done.2, bf16[1024,1024]{1,0:T(8,128)(2,1)S(1)} %copy-done.4, bf16[8,128,128]{2,1,0:T(8,128)(2,1)S(1)} %get-tuple-element.36.saved_ref, ...), custom_call_target="tpu_custom_call" | custom-call | tf_op jit(solution)/shard_map/keys_core/keys_partials/pallas_call | solution.py:283
  42.6 4.1 %collective-permute-done.6.received_ref = f32[4,128,1024]{2,1,0:T(8,128)S(1)} collective-permute-done((f32[4,128,1024]{2,1,0:T(8,128)S(1)}, f32[4,128,1024]{2,1,0:T(8,128)S(1)}, u32[]{:S(2)}, u32[]{:S(2)}) %collective-permute-start.6) | collective-permute-done | bytes 2097184 | tf_op jit(solution)/shard_map/keys_core/ppermute | solution.py:25
  46.8 0.2 keys_chip_sums.1
  47.0 0.8 copy-done.11
  47.8 0.8 copy-done.13
  48.6 15.4 %all-to-all-done.terms_ref = bf16[8,1168,128]{2,1,0:T(8,128)(2,1)S(1)} async-done(((bf16[8,1168,128]{2,1,0:T(8,128)(2,1)}), bf16[8,1168,128]{2,1,0:T(8,128)(2,1)S(1)}, u32[]{:S(2)}, u32[]{:S(2)}) %all-to-all-start) | async-done | bytes 2392096 | tf_op jit(solution)/shard_map/terms_over_first/all_to_all | solution.py:351
  64.2 1.5 %slot_sums.1 = bf16[32,144,128]{2,1,0:T(8,128)(2,1)S(1)} custom-call(s32[8,8]{1,0:T(8,128)S(1)} %convert_reduce_fusion.slots_ref, bf16[8,1168,128]{2,1,0:T(8,128)(2,1)S(1)} %all-to-all-done.terms_ref), custom_call_target="tpu_custom_call" | custom-call | tf_op jit(solution)/shard_map/sums_over_adapter/slot_sums/pallas_call | solution.py:224
  65.7 1.0 copy-done.3
  66.7 10.0 %all-to-all-start.1 = ((bf16[32,144,128]{2,1,0:T(8,128)(2,1)}), bf16[32,144,128]{2,1,0:T(8,128)(2,1)S(1)}, u32[]{:S(2)}, u32[]{:S(2)}) async-start(bf16[32,144,128]{2,1,0:T(8,128)(2,1)} %copy-done.3), calls=%async_computation.1 | async-start | bytes 2359296 | tf_op jit(solution)/shard_map/sums_over_adapter/all_to_all | solution.py:365
  76.9 2.7 %collective-permute-start.8 = (f32[128,1024]{1,0:T(8,128)S(1)}, f32[128,1024]{1,0:T(8,128)S(1)}, u32[]{:S(2)}, u32[]{:S(2)}) collective-permute-start(f32[128,1024]{1,0:T(8,128)S(1)} %copy-done.12), channel_id=1, source_target_pairs={{0,4},{2,6},{4,0},{6,2},{1,5},{3,7},{5,1},{7,3},{8,12},{10,14},{12... | collective-permute-start | bytes 1572872 | tf_op jit(solution)/shard_map/keys_y/ppermute | solution.py:25
  79.6 0.4 collective-permute-start.9
  80.0 21.5 %collective-permute-done.7 = f32[128,1024]{1,0:T(8,128)S(1)} collective-permute-done((f32[128,1024]{1,0:T(8,128)S(1)}, f32[128,1024]{1,0:T(8,128)S(1)}, u32[]{:S(2)}, u32[]{:S(2)}) %collective-permute-start.7) | collective-permute-done | bytes 524320 | tf_op jit(solution)/shard_map/keys_y/ppermute | solution.py:25
  101.6 0.6 collective-permute-done.9
  102.2 0.8 add_convert_fusion
  103.0 4.1 %all-to-all-done.1 = bf16[32,144,128]{2,1,0:T(8,128)(2,1)S(1)} async-done(((bf16[32,144,128]{2,1,0:T(8,128)(2,1)}), bf16[32,144,128]{2,1,0:T(8,128)(2,1)S(1)}, u32[]{:S(2)}, u32[]{:S(2)}) %all-to-all-start.1) | async-done | bytes 1179680 | tf_op jit(solution)/shard_map/sums_over_adapter/all_to_all | solution.py:365
  107.1 1.0 finish.1
  (34 shorter events, 1.0 us)
Async XLA Ops:
  0.6 25.4 %copy-start.5 = (bf16[1024,128]{1,0:T(8,128)(2,1)S(1)}, bf16[1024,128]{1,0:T(8,128)(2,1)}, u32[]{:S(2)}) copy-start(bf16[1024,128]{1,0:T(8,128)(2,1)} %cot_ref.3) | copy-start | bytes 786436
  0.6 25.4 %copy-start.1 = (bf16[1024,1024]{1,0:T(8,128)(2,1)S(1)}, bf16[1024,1024]{1,0:T(8,128)(2,1)}, u32[]{:S(2)}) copy-start(bf16[1024,1024]{1,0:T(8,128)(2,1)} %tokens_ref.3) | copy-start | bytes 6291460
  4.7 1.9 %collective-permute-start = (f32[5,128,128]{2,1,0:T(8,128)}, f32[5,128,128]{2,1,0:T(8,128)S(1)}, u32[]{:S(2)}, u32[]{:S(2)}) collective-permute-start(f32[5,128,128]{2,1,0:T(8,128)} %get-tuple-element.28), channel_id=1, source_target_pairs={{0,1},{1,0},{2,3},{3,2},{4,5},{5,4},{6,7},{7,6},{8,9},{9,8},{10,11... | collective-permute-start | bytes 983048 | tf_op jit(solution)/shard_map/mid_sums/ppermute | solution.py:25
  6.7 1.0 copy-start.6
  7.6 18.4 %copy-start.8 = (s32[8,1]{0,1:T(1,128)S(1)}, s32[8,1]{0,1:T(1,128)}, u32[]{:S(2)}) copy-start(s32[8,1]{0,1:T(1,128)} %param.13) | copy-start | bytes 100
  7.6 18.4 %copy-start.9 = (s32[8]{0:T(128)S(1)}, s32[8]{0:T(128)}, u32[]{:S(2)}) copy-start(s32[8]{0:T(128)} %fill_ref.3) | copy-start | bytes 100
  7.6 18.4 %copy-start.10 = (s32[32]{0:T(128)S(1)}, s32[32]{0:T(128)}, u32[]{:S(2)}) copy-start(s32[32]{0:T(128)} %slot_ref.1) | copy-start | bytes 388
  7.7 6.3 %collective-permute-start.1 = (bf16[5,128,128]{2,1,0:T(8,128)(2,1)S(1)}, bf16[5,128,128]{2,1,0:T(8,128)(2,1)S(1)}, u32[]{:S(2)}, u32[]{:S(2)}) collective-permute-start(bf16[5,128,128]{2,1,0:T(8,128)(2,1)S(1)} %get-tuple-element.30.refs_0_), channel_id=1, source_target_pairs={{0,2},{2,0},{4,6},{6,4},{1,3},{3,1},{5,7},{7,5},{8,10},{10,8},{12,... | collective-permute-start | bytes 491528 | tf_op jit(solution)/shard_map/mid_sums/ppermute | solution.py:342
  9.4 7.2 %collective-permute-start.2 = (bf16[5,128,128]{2,1,0:T(8,128)(2,1)S(1)}, bf16[5,128,128]{2,1,0:T(8,128)(2,1)S(1)}, u32[]{:S(2)}, u32[]{:S(2)}) collective-permute-start(bf16[5,128,128]{2,1,0:T(8,128)(2,1)S(1)} %get-tuple-element.31.refs_1_), channel_id=1, source_target_pairs={{0,6},{2,4},{4,2},{6,0},{1,7},{3,5},{5,3},{7,1},{8,14},{10,12},{12... | collective-permute-start | bytes 491528 | tf_op jit(solution)/shard_map/mid_sums/ppermute | solution.py:342
  16.6 7.1 %collective-permute-start.3 = (bf16[6,128,128]{2,1,0:T(8,128)(2,1)S(1)}, bf16[6,128,128]{2,1,0:T(8,128)(2,1)S(1)}, u32[]{:S(2)}, u32[]{:S(2)}) collective-permute-start(bf16[6,128,128]{2,1,0:T(8,128)(2,1)S(1)} %get-tuple-element.33.refs_0_), channel_id=1, source_target_pairs={{0,6},{2,4},{4,2},{6,0},{1,7},{3,5},{5,3},{7,1},{8,14},{10,12},{12... | collective-permute-start | bytes 589832 | tf_op jit(solution)/shard_map/mid_sums/ppermute | solution.py:344
  18.9 5.7 %collective-permute-start.4 = (bf16[6,128,128]{2,1,0:T(8,128)(2,1)S(1)}, bf16[6,128,128]{2,1,0:T(8,128)(2,1)S(1)}, u32[]{:S(2)}, u32[]{:S(2)}) collective-permute-start(bf16[6,128,128]{2,1,0:T(8,128)(2,1)S(1)} %get-tuple-element.34.refs_1_), channel_id=1, source_target_pairs={{0,2},{2,0},{4,6},{6,4},{1,3},{3,1},{5,7},{7,5},{8,10},{10,8},{12,... | collective-permute-start | bytes 589832 | tf_op jit(solution)/shard_map/mid_sums/ppermute | solution.py:344
  24.6 1.4 %collective-permute-start.5 = (bf16[4,128,128]{2,1,0:T(8,128)(2,1)S(1)}, bf16[4,128,128]{2,1,0:T(8,128)(2,1)S(1)}, u32[]{:S(2)}, u32[]{:S(2)}) collective-permute-start(bf16[4,128,128]{2,1,0:T(8,128)(2,1)S(1)} %get-tuple-element.35.mids_ref), channel_id=1, source_target_pairs={{0,1},{1,0},{2,3},{3,2},{4,5},{5,4},{6,7},{7,6},{8,9},{9,8},{10,11... | collective-permute-start | bytes 393224 | tf_op jit(solution)/shard_map/mid_sums/ppermute | solution.py:25
  27.4 1.4 %copy-start = (bf16[8,1168,128]{2,1,0:T(8,128)(2,1)}, bf16[8,1168,128]{2,1,0:T(8,128)(2,1)S(1)}, u32[]{:S(2)}) copy-start(bf16[8,1168,128]{2,1,0:T(8,128)(2,1)S(1)} %products.1) | copy-start | bytes 7176196
  28.9 6.0 %copy-start.7 = (bf16[8,128,128]{2,1,0:T(8,128)(2,1)S(1)}, bf16[8,128,128]{2,1,0:T(8,128)(2,1)}, u32[]{:S(2)}) copy-start(bf16[8,128,128]{2,1,0:T(8,128)(2,1)} %get-tuple-element.37.picked_ref) | copy-start | bytes 786436
  28.9 35.1 %all-to-all-start = ((bf16[8,1168,128]{2,1,0:T(8,128)(2,1)}), bf16[8,1168,128]{2,1,0:T(8,128)(2,1)S(1)}, u32[]{:S(2)}, u32[]{:S(2)}) async-start(bf16[8,1168,128]{2,1,0:T(8,128)(2,1)} %copy-done), calls=%async_computation | async-start | bytes 4784128 | tf_op jit(solution)/shard_map/terms_over_first/all_to_all | solution.py:351
  34.8 1.6 %copy-start.2 = (bf16[1024,1024]{1,0:T(8,128)(2,1)S(1)}, bf16[1024,1024]{1,0:T(8,128)(2,1)}, u32[]{:S(2)}) copy-start(bf16[1024,1024]{1,0:T(8,128)(2,1)} %tokens_ref.3) | copy-start | bytes 6291460
  36.4 1.6 %copy-start.4 = (bf16[1024,1024]{1,0:T(8,128)(2,1)S(1)}, bf16[1024,1024]{1,0:T(8,128)(2,1)}, u32[]{:S(2)}) copy-start(bf16[1024,1024]{1,0:T(8,128)(2,1)} %weight_ref.1) | copy-start | bytes 6291460
  42.5 4.2 %collective-permute-start.6 = (f32[4,128,1024]{2,1,0:T(8,128)S(1)}, f32[4,128,1024]{2,1,0:T(8,128)S(1)}, u32[]{:S(2)}, u32[]{:S(2)}) collective-permute-start(f32[4,128,1024]{2,1,0:T(8,128)S(1)} %get-tuple-element.39), channel_id=1, source_target_pairs={{0,1},{1,0},{2,3},{3,2},{4,5},{5,4},{6,7},{7,6},{8,9},{9,8},{10,11... | collective-permute-start | bytes 6291464 | tf_op jit(solution)/shard_map/keys_core/ppermute | solution.py:25
  47.0 0.8 copy-start.11
  47.8 0.8 copy-start.13
  65.7 1.0 copy-start.3
  66.7 10.0 %copy-start.14 = (f32[128,1024]{1,0:T(8,128)S(1)}, f32[128,1024]{1,0:T(8,128)}, u32[]{:S(2)}) copy-start(f32[128,1024]{1,0:T(8,128)} %copy-done.13) | copy-start | bytes 1572868
  66.7 10.2 %copy-start.12 = (f32[128,1024]{1,0:T(8,128)S(1)}, f32[128,1024]{1,0:T(8,128)}, u32[]{:S(2)}) copy-start(f32[128,1024]{1,0:T(8,128)} %copy-done.11) | copy-start | bytes 1572868
  66.7 40.4 %all-to-all-start.1 = ((bf16[32,144,128]{2,1,0:T(8,128)(2,1)}), bf16[32,144,128]{2,1,0:T(8,128)(2,1)S(1)}, u32[]{:S(2)}, u32[]{:S(2)}) async-start(bf16[32,144,128]{2,1,0:T(8,128)(2,1)} %copy-done.3), calls=%async_computation.1 | async-start | bytes 2359296 | tf_op jit(solution)/shard_map/sums_over_adapter/all_to_all | solution.py:365
  76.7 24.9 %collective-permute-start.7 = (f32[128,1024]{1,0:T(8,128)S(1)}, f32[128,1024]{1,0:T(8,128)S(1)}, u32[]{:S(2)}, u32[]{:S(2)}) collective-permute-start(f32[128,1024]{1,0:T(8,128)S(1)} %copy-done.14), channel_id=1, source_target_pairs={{0,2},{2,4},{4,6},{6,0},{1,3},{3,5},{5,7},{7,1},{8,10},{10,12},{12... | collective-permute-start | bytes 1572872 | tf_op jit(solution)/shard_map/keys_y/ppermute | solution.py:25
  76.9 24.7 %collective-permute-start.8 = (f32[128,1024]{1,0:T(8,128)S(1)}, f32[128,1024]{1,0:T(8,128)S(1)}, u32[]{:S(2)}, u32[]{:S(2)}) collective-permute-start(f32[128,1024]{1,0:T(8,128)S(1)} %copy-done.12), channel_id=1, source_target_pairs={{0,4},{2,6},{4,0},{6,2},{1,5},{3,7},{5,1},{7,3},{8,12},{10,14},{12... | collective-permute-start | bytes 1572872 | tf_op jit(solution)/shard_map/keys_y/ppermute | solution.py:25
  79.6 22.6 %collective-permute-start.9 = (f32[128,1024]{1,0:T(8,128)S(1)}, f32[128,1024]{1,0:T(8,128)S(1)}, u32[]{:S(2)}, u32[]{:S(2)}) collective-permute-start(f32[128,1024]{1,0:T(8,128)S(1)} %get-tuple-element.47), channel_id=1, source_target_pairs={{0,6},{2,0},{4,2},{6,4},{1,7},{3,1},{5,3},{7,5},{8,14},{10,8},{12,... | collective-permute-start | bytes 1572872 | tf_op jit(solution)/shard_map/keys_y/ppermute | solution.py:25

commit v5 on v4

--- a/solution.py
+++ b/solution.py
@@ -45,24 +45,23 @@
     def kernel(
         jobs_ref, fill_ref, up_ref, cot_ref, saved_ref, own_ref, other_ref, picked_ref, cot, sems
     ):
-        copies = []
-        for b in range(nblocks):
-            block = slice(b * BLK, (b + 1) * BLK)
-            pair = (
-                pltpu.make_async_copy(up_ref.at[jobs_ref[b]], picked_ref.at[b], sems.at[2 * b]),
-                pltpu.make_async_copy(cot_ref.at[block, :], cot.at[block, :], sems.at[2 * b + 1]),
-            )
-            for copy in pair:
-                copy.start()
-            copies.append(pair)
+        whole = pltpu.make_async_copy(cot_ref, cot, sems.at[nblocks])
+        whole.start()
+        copies = [
+            pltpu.make_async_copy(up_ref.at[jobs_ref[b]], picked_ref.at[b], sems.at[b])
+            for b in range(nblocks)
+        ]
+        for copy in copies:
+            copy.start()
         core = lax.axis_index("core")
         own_ref[half] = saved_ref[...].astype(F32)
         other_ref[half] = saved_ref[...].astype(F32)
+        whole.wait()
+        for copy in copies:
+            copy.wait()
         for i in range(half):
             partials = []
             for b in (2 * i, 2 * i + 1):
-                for copy in copies[b]:
-                    copy.wait()
                 partials.append(contract(masked(cot, fill_ref, b), picked_ref[b], 1, 1))
             own_ref[i] = jnp.where(core == 0, partials[0], partials[1])
             other_ref[i] = jnp.where(core == 0, partials[1], partials[0])
@@ -70,12 +69,13 @@
     out = jax.ShapeDtypeStruct((half + 1, BLK, rank), F32)
     return pl.pallas_call(
         kernel,
-        out_shape=[out, out, jax.ShapeDtypeStruct((nblocks, rank, features), BF16)],
+        out_shape=[out, out],
         in_specs=[SMEM, SMEM, HBM, HBM, VMEM],
-        out_specs=[VMEM] * 3,
+        out_specs=[VMEM] * 2,
         scratch_shapes=[
+            pltpu.VMEM((nblocks, rank, features), BF16),
             pltpu.VMEM(cotangent.shape, BF16),
-            pltpu.SemaphoreType.DMA((2 * nblocks,)),
+            pltpu.SemaphoreType.DMA((nblocks + 1,)),
         ],
         compiler_params=WHOLE,
         name="mid_partials",
@@ -87,30 +87,49 @@
     return high, (total - high.astype(F32)).astype(BF16)
 
 
-def y_first(own, received):
+def own_parts(own):
     half, _, rank = own.shape
     half -= 1
+
+    def kernel(own_ref, sums_ref, saved_ref):
+        sums_ref[...] = own_ref[:half]
+        saved_ref[...] = own_ref[half].astype(BF16)
+
+    return pl.pallas_call(
+        kernel,
+        out_shape=[
+            jax.ShapeDtypeStruct((half, BLK, rank), F32),
+            jax.ShapeDtypeStruct((BLK, rank), BF16),
+        ],
+        in_specs=[VMEM],
+        out_specs=[VMEM] * 2,
+        compiler_params=LIMIT,
+        name="own_parts",
+    )(own)
+
+
+def y_first(own, saved, received):
+    half, _, rank = own.shape
     each = half // 2
 
-    def kernel(own_ref, received_ref, keep_ref, *outs):
+    def kernel(own_ref, saved_ref, received_ref, keep_ref, *outs):
         first = lax.axis_index("core") == 0
-        mine, theirs = own_ref[half], received_ref[half]
-        total = own_ref[:half] + received_ref[:half]
+        mine, theirs = saved_ref[...], received_ref[half].astype(BF16)
+        total = own_ref[...] + received_ref[:half]
         keep_ref[...] = total
         for i, out in enumerate(outs):
             out[:each], out[each : 2 * each] = halves_of(total[i * each : (i + 1) * each])
-            saved = jnp.where(first, mine, theirs) if i == 0 else jnp.where(first, theirs, mine)
-            out[2 * each] = saved.astype(BF16)
+            out[2 * each] = jnp.where(first, *((mine, theirs) if i == 0 else (theirs, mine)))
 
     return pl.pallas_call(
         kernel,
         out_shape=[jax.ShapeDtypeStruct((half, BLK, rank), F32)]
         + [jax.ShapeDtypeStruct((2 * each + 1, BLK, rank), BF16)] * 2,
-        in_specs=[VMEM] * 2,
+        in_specs=[VMEM] * 3,
         out_specs=[VMEM] * 3,
         compiler_params=LIMIT,
         name="y_first",
-    )(own, received)
+    )(own, saved, received)
 
 
 def y_second(keep, sent, received):
@@ -259,16 +278,17 @@
     )(owned)
 
 
-def keys_partials(place, tokens, frozen_weight, saved_rows, picked):
+def keys_partials(place, jobs, tokens, frozen_weight, saved_rows, up_stack):
     rows, width = tokens.shape
-    nblocks, rank, features = picked.shape
+    nblocks = jobs.shape[0]
+    rank, features = up_stack.shape[1:]
     half = nblocks // 2
     total = frozen_weight.shape[1]
 
     def block_of(i, j, place_ref):
         return 2 * j + lax.rem(place_ref[1] + i, 2)
 
-    def kernel(place_ref, tokens_ref, weight_ref, saved_ref, picked_ref, own_ref, other_ref):
+    def kernel(place_ref, jobs_ref, tokens_ref, weight_ref, saved_ref, picked_ref, own_ref, other_ref):
         columns = pl.ds(pl.multiple_of((2 * place_ref[0] + place_ref[1]) * features, features), features)
         for i, out_ref in enumerate((own_ref, other_ref)):
 
@@ -283,23 +303,26 @@
     return pl.pallas_call(
         kernel,
         grid_spec=pltpu.PrefetchScalarGridSpec(
-            num_scalar_prefetch=1,
+            num_scalar_prefetch=2,
             grid=(2, half),
             in_specs=[
-                pl.BlockSpec((BLK, width), lambda i, j, place: (block_of(i, j, place), 0)),
-                pl.BlockSpec((width, total), lambda i, j, place: (0, 0)),
-                pl.BlockSpec((1, BLK, rank), lambda i, j, place: (block_of(i, j, place), 0, 0)),
-                pl.BlockSpec((1, rank, features), lambda i, j, place: (block_of(i, j, place), 0, 0)),
+                pl.BlockSpec((BLK, width), lambda i, j, place, jobs: (block_of(i, j, place), 0)),
+                pl.BlockSpec((width, total), lambda i, j, place, jobs: (0, 0)),
+                pl.BlockSpec((1, BLK, rank), lambda i, j, place, jobs: (block_of(i, j, place), 0, 0)),
+                pl.BlockSpec(
+                    (1, rank, features),
+                    lambda i, j, place, jobs: (jobs[block_of(i, j, place)], 0, 0),
+                ),
             ],
             out_specs=[
-                pl.BlockSpec((1, BLK, total), lambda i, j, place: (jnp.where(i == 0, j, half - 1), 0, 0)),
-                pl.BlockSpec((1, BLK, total), lambda i, j, place: (jnp.where(i == 0, 0, j), 0, 0)),
+                pl.BlockSpec((1, BLK, total), lambda i, j, place, jobs: (jnp.where(i == 0, j, half - 1), 0, 0)),
+                pl.BlockSpec((1, BLK, total), lambda i, j, place, jobs: (jnp.where(i == 0, 0, j), 0, 0)),
             ],
         ),
         out_shape=[shape, shape],
         compiler_params=LIMIT,
         name="keys_partials",
-    )(place, tokens, frozen_weight, saved_rows, picked)
+    )(place, jobs, tokens, frozen_weight, saved_rows, up_stack)
 
 
 def keys_chip_sums(own, received):
@@ -335,8 +358,9 @@
     place = jnp.stack([lax.axis_index(name) for name in SEQ]).astype(jnp.int32)
 
     with jax.named_scope("mid_sums"):
-        own, other, picked = mid_partials(jobs, block_fill, up_stack, cotangent, saved_mid)
-        keep, *sent = y_first(own, shift(other, "core", 1))
+        own, other = mid_partials(jobs, block_fill, up_stack, cotangent, saved_mid)
+        own_sums, own_saved = own_parts(own)
+        keep, *sent = y_first(own_sums, own_saved, shift(other, "core", 1))
         pair = [(i, i ^ 1) for i in range(ny)]
         mirror = [(i, ny - 1 - i) for i in range(ny)]
         received = [lax.ppermute(sent[0], "y", pair), lax.ppermute(sent[1], "y", mirror)]
@@ -350,7 +374,9 @@
         )
         terms = lax.all_to_all(terms, FIRST, split_axis=0, concat_axis=0, tiled=True)
     with jax.named_scope("keys_core"):
-        keys_own, keys_other = keys_partials(place, tokens, frozen_weight, saved_rows, picked)
+        keys_own, keys_other = keys_partials(
+            place, jobs, tokens, frozen_weight, saved_rows, up_stack
+        )
         keys_parts = keys_chip_sums(keys_own, shift(keys_other, "core", 1))
         terms, keys_parts = lax.optimization_barrier((terms, keys_parts))
     with jax.named_scope("keys_y"):

time: 109 us -> 107 us (0.982)
  waiting for transfers between devices: 59.7 us -> 57.6 us
  local copies, waits for them, and re-layouts: 8.21 us -> 9.86 us
    unnamed x30 -> x34, local copies, waits for them, and re-layouts: 8.21 us -> 9.86 us
    pallas_call x1 -> x2, Pallas kernels: 4.07 us -> 3.12 us  [the longest x1 3.09 us: mid_partials(): pl.pallas_call(kernel, out_shape=[out, out], in_specs=[SMEM, SMEM, HBM, H...]
where the time goes in v5:
time: 107 us
  waiting for transfers between devices  57.6 us (54%)
  starting transfers between devices  25.6 us (24%)
  Pallas kernels  11.8 us (11%)
  local copies, waits for them, and re-layouts  9.86 us (9%)
  other arithmetic  1.12 us (1%)
    ppermute x6, waiting for transfers between devices, shift(): lax.ppermute(value, axis, [(i, (i + distance) % size) for i in range(size)])  28.5 us
    all_to_all x1, waiting for transfers between devices, per_device(): lax.all_to_all(terms, FIRST, split_axis=0, concat_axis=0, tiled=True)  14.4 us
    all_to_all x1, starting transfers between devices, per_device(): lax.all_to_all(sums, ADAPTER, split_axis=0, concat_axis=0, tiled=True)  9.96 us
    unnamed x34, local copies, waits for them, and re-layouts  9.86 us
    all_to_all x1, starting transfers between devices, per_device(): lax.all_to_all(terms, FIRST, split_axis=0, concat_axis=0, tiled=True)  5.89 us
    ppermute x1, waiting for transfers between devices, per_device(): lax.ppermute(sent[0], 'y', mirror)  4.82 us
    pallas_call x1, Pallas kernels, keys_partials(): pl.pallas_call(kernel, grid_spec=pltpu.PrefetchScalarGridSpec(num_scalar_...  4.48 us
    all_to_all x1, waiting for transfers between devices, per_device(): lax.all_to_all(sums, ADAPTER, split_axis=0, concat_axis=0, tiled=True)  4.1 us
  transfers between devices with their start and end apart: 12, of which 11 were waited for; matrix products, arithmetic and copies ran while one was open for 1% of the time, Pallas kernels for 4%

profile of v5, /device:TPU:32, one launch (start us, length us, event | category | flops | bytes accessed | tf_op | source)
XLA Modules:
  0.0 106.9 jit_solution(12337022277455285094)
XLA Ops:
  0.7 3.1 %mid_partials.1 = (f32[5,128,128]{2,1,0:T(8,128)}, f32[5,128,128]{2,1,0:T(8,128)}) custom-call(s32[8]{0:T(128)} %bitcast.7, s32[8]{0:T(128)} %fill_ref.3, bf16[32,128,128]{2,1,0:T(8,128)(2,1)} %picked_ref.1, bf16[1024,128]{1,0:T(8,128)(2,1)} %cot_ref.3, bf16[128,128]{1,0:T(8,128)(2,1)} %saved_ref.1), custom_call_target="tpu_custom_call" | custom-call | tf_op jit(solution)/shard_map/mid_sums/mid_partials/pallas_call | solution.py:70
  3.9 1.0 copy-done.9
  4.9 0.8 collective-permute-done.received_ref
  5.8 1.7 %collective-permute-start.1 = (bf16[5,128,128]{2,1,0:T(8,128)(2,1)S(1)}, bf16[5,128,128]{2,1,0:T(8,128)(2,1)S(1)}, u32[]{:S(2)}, u32[]{:S(2)}) collective-permute-start(bf16[5,128,128]{2,1,0:T(8,128)(2,1)S(1)} %get-tuple-element.33.refs_0_), channel_id=1, source_target_pairs={{0,2},{2,0},{4,6},{6,4},{1,3},{3,1},{5,7},{7,5},{8,10},{10,8},{12,... | collective-permute-start | bytes 491528 | tf_op jit(solution)/shard_map/mid_sums/ppermute | solution.py:366
  7.4 2.2 %collective-permute-start.2 = (bf16[5,128,128]{2,1,0:T(8,128)(2,1)S(1)}, bf16[5,128,128]{2,1,0:T(8,128)(2,1)S(1)}, u32[]{:S(2)}, u32[]{:S(2)}) collective-permute-start(bf16[5,128,128]{2,1,0:T(8,128)(2,1)S(1)} %get-tuple-element.34.refs_1_), channel_id=1, source_target_pairs={{0,6},{2,4},{4,2},{6,0},{1,7},{3,5},{5,3},{7,1},{8,14},{10,12},{12... | collective-permute-start | bytes 491528 | tf_op jit(solution)/shard_map/mid_sums/ppermute | solution.py:366
  9.6 2.5 %collective-permute-done.1.refs_2_ = bf16[5,128,128]{2,1,0:T(8,128)(2,1)S(1)} collective-permute-done((bf16[5,128,128]{2,1,0:T(8,128)(2,1)S(1)}, bf16[5,128,128]{2,1,0:T(8,128)(2,1)S(1)}, u32[]{:S(2)}, u32[]{:S(2)}) %collective-permute-start.1) | collective-permute-done | bytes 163872 | tf_op jit(solution)/shard_map/mid_sums/ppermute | solution.py:366
  12.1 2.5 %collective-permute-done.2.refs_3_ = bf16[5,128,128]{2,1,0:T(8,128)(2,1)S(1)} collective-permute-done((bf16[5,128,128]{2,1,0:T(8,128)(2,1)S(1)}, bf16[5,128,128]{2,1,0:T(8,128)(2,1)S(1)}, u32[]{:S(2)}, u32[]{:S(2)}) %collective-permute-start.2) | collective-permute-done | bytes 163872 | tf_op jit(solution)/shard_map/mid_sums/ppermute | solution.py:366
  14.7 2.3 %collective-permute-start.3 = (bf16[6,128,128]{2,1,0:T(8,128)(2,1)S(1)}, bf16[6,128,128]{2,1,0:T(8,128)(2,1)S(1)}, u32[]{:S(2)}, u32[]{:S(2)}) collective-permute-start(bf16[6,128,128]{2,1,0:T(8,128)(2,1)S(1)} %get-tuple-element.36.refs_0_), channel_id=1, source_target_pairs={{0,6},{2,4},{4,2},{6,0},{1,7},{3,5},{5,3},{7,1},{8,14},{10,12},{12... | collective-permute-start | bytes 589832 | tf_op jit(solution)/shard_map/mid_sums/ppermute | solution.py:368
  17.0 4.8 %collective-permute-done.3.refs_2_ = bf16[6,128,128]{2,1,0:T(8,128)(2,1)S(1)} collective-permute-done((bf16[6,128,128]{2,1,0:T(8,128)(2,1)S(1)}, bf16[6,128,128]{2,1,0:T(8,128)(2,1)S(1)}, u32[]{:S(2)}, u32[]{:S(2)}) %collective-permute-start.3) | collective-permute-done | bytes 196640 | tf_op jit(solution)/shard_map/mid_sums/ppermute | solution.py:368
  21.8 0.8 collective-permute-done.4.refs_3_
  22.8 1.3 %collective-permute-done.5.other_ref = bf16[4,128,128]{2,1,0:T(8,128)(2,1)S(1)} collective-permute-done((bf16[4,128,128]{2,1,0:T(8,128)(2,1)S(1)}, bf16[4,128,128]{2,1,0:T(8,128)(2,1)S(1)}, u32[]{:S(2)}, u32[]{:S(2)}) %collective-permute-start.5) | collective-permute-done | bytes 131104 | tf_op jit(solution)/shard_map/mid_sums/ppermute | solution.py:25
  24.1 1.4 %products.1 = bf16[8,1168,128]{2,1,0:T(8,128)(2,1)S(1)} custom-call(s32[8]{0:T(128)S(1)} %bitcast.8, s32[8]{0:T(128)S(1)} %copy-done.11, s32[32]{0:T(128)S(1)} %copy-done.12, bf16[1024,1024]{1,0:T(8,128)(2,1)S(1)} %copy-done.1, bf16[4,128,128]{2,1,0:T(8,128)(2,1)S(1)} %get-tuple-element.38.mids_ref, ...), custom_call_target="tpu_custom_call" | custom-call | tf_op jit(solution)/shard_map/terms_over_first/products/pallas_call | solution.py:221
  25.5 1.4 %copy-done = bf16[8,1168,128]{2,1,0:T(8,128)(2,1)} copy-done((bf16[8,1168,128]{2,1,0:T(8,128)(2,1)}, bf16[8,1168,128]{2,1,0:T(8,128)(2,1)S(1)}, u32[]{:S(2)}) %copy-start) | copy-done | bytes 2392088
  27.0 0.7 copy-done.6
  27.7 5.9 %all-to-all-start = ((bf16[8,1168,128]{2,1,0:T(8,128)(2,1)}), bf16[8,1168,128]{2,1,0:T(8,128)(2,1)S(1)}, u32[]{:S(2)}, u32[]{:S(2)}) async-start(bf16[8,1168,128]{2,1,0:T(8,128)(2,1)} %copy-done), calls=%async_computation | async-start | bytes 4784128 | tf_op jit(solution)/shard_map/terms_over_first/all_to_all | solution.py:375
  33.6 1.6 %copy-done.2 = bf16[1024,1024]{1,0:T(8,128)(2,1)S(1)} copy-done((bf16[1024,1024]{1,0:T(8,128)(2,1)S(1)}, bf16[1024,1024]{1,0:T(8,128)(2,1)}, u32[]{:S(2)}) %copy-start.2) | copy-done | bytes 2097176
  35.2 1.6 %copy-done.5 = bf16[1024,1024]{1,0:T(8,128)(2,1)S(1)} copy-done((bf16[1024,1024]{1,0:T(8,128)(2,1)S(1)}, bf16[1024,1024]{1,0:T(8,128)(2,1)}, u32[]{:S(2)}) %copy-start.5) | copy-done | bytes 2097176
  36.8 0.9 copy-done.7
  37.8 4.5 %keys_partials.1 = (f32[4,128,1024]{2,1,0:T(8,128)S(1)}, f32[4,128,1024]{2,1,0:T(8,128)S(1)}) custom-call(s32[2]{0:T(128)S(1)} %pad_add_fusion.place_ref, s32[8]{0:T(128)S(1)} %bitcast.9, bf16[1024,1024]{1,0:T(8,128)(2,1)S(1)} %copy-done.2, bf16[1024,1024]{1,0:T(8,128)(2,1)S(1)} %copy-done.5, bf16[8,128,128]{2,1,0:T(8,128)(2,1)S(1)} %copy-done.7, ...), custom_call_target="tpu_custom_call" | custom-call | tf_op jit(solution)/shard_map/keys_core/keys_partials/pallas_call | solution.py:303
  42.3 4.1 %collective-permute-done.6.received_ref = f32[4,128,1024]{2,1,0:T(8,128)S(1)} collective-permute-done((f32[4,128,1024]{2,1,0:T(8,128)S(1)}, f32[4,128,1024]{2,1,0:T(8,128)S(1)}, u32[]{:S(2)}, u32[]{:S(2)}) %collective-permute-start.6) | collective-permute-done | bytes 2097184 | tf_op jit(solution)/shard_map/keys_core/ppermute | solution.py:25
  46.8 0.8 copy-done.13
  47.6 0.8 copy-done.15
  48.4 14.4 %all-to-all-done.terms_ref = bf16[8,1168,128]{2,1,0:T(8,128)(2,1)S(1)} async-done(((bf16[8,1168,128]{2,1,0:T(8,128)(2,1)}), bf16[8,1168,128]{2,1,0:T(8,128)(2,1)S(1)}, u32[]{:S(2)}, u32[]{:S(2)}) %all-to-all-start) | async-done | bytes 2392096 | tf_op jit(solution)/shard_map/terms_over_first/all_to_all | solution.py:375
  63.0 1.5 %slot_sums.1 = bf16[32,144,128]{2,1,0:T(8,128)(2,1)S(1)} custom-call(s32[8,8]{1,0:T(8,128)S(1)} %convert_reduce_fusion.slots_ref, bf16[8,1168,128]{2,1,0:T(8,128)(2,1)S(1)} %all-to-all-done.terms_ref), custom_call_target="tpu_custom_call" | custom-call | tf_op jit(solution)/shard_map/sums_over_adapter/slot_sums/pallas_call | solution.py:243
  64.5 1.0 copy-done.3
  65.5 10.0 %all-to-all-start.1 = ((bf16[32,144,128]{2,1,0:T(8,128)(2,1)}), bf16[32,144,128]{2,1,0:T(8,128)(2,1)S(1)}, u32[]{:S(2)}, u32[]{:S(2)}) async-start(bf16[32,144,128]{2,1,0:T(8,128)(2,1)} %copy-done.3), calls=%async_computation.1 | async-start | bytes 2359296 | tf_op jit(solution)/shard_map/sums_over_adapter/all_to_all | solution.py:391
  75.7 2.7 %collective-permute-start.8 = (f32[128,1024]{1,0:T(8,128)S(1)}, f32[128,1024]{1,0:T(8,128)S(1)}, u32[]{:S(2)}, u32[]{:S(2)}) collective-permute-start(f32[128,1024]{1,0:T(8,128)S(1)} %copy-done.14), channel_id=1, source_target_pairs={{0,4},{2,6},{4,0},{6,2},{1,5},{3,7},{5,1},{7,3},{8,12},{10,14},{12... | collective-permute-start | bytes 1572872 | tf_op jit(solution)/shard_map/keys_y/ppermute | solution.py:25
  78.8 21.5 %collective-permute-done.7 = f32[128,1024]{1,0:T(8,128)S(1)} collective-permute-done((f32[128,1024]{1,0:T(8,128)S(1)}, f32[128,1024]{1,0:T(8,128)S(1)}, u32[]{:S(2)}, u32[]{:S(2)}) %collective-permute-start.7) | collective-permute-done | bytes 524320 | tf_op jit(solution)/shard_map/keys_y/ppermute | solution.py:25
  100.4 0.6 collective-permute-done.9
  101.0 0.8 add_convert_fusion
  101.8 4.1 %all-to-all-done.1 = bf16[32,144,128]{2,1,0:T(8,128)(2,1)S(1)} async-done(((bf16[32,144,128]{2,1,0:T(8,128)(2,1)}), bf16[32,144,128]{2,1,0:T(8,128)(2,1)S(1)}, u32[]{:S(2)}, u32[]{:S(2)}) %all-to-all-start.1) | async-done | bytes 1179680 | tf_op jit(solution)/shard_map/sums_over_adapter/all_to_all | solution.py:391
  105.9 1.0 finish.1
  (39 shorter events, 1.7 us)
Async XLA Ops:
  0.6 23.5 %copy-start.10 = (s32[8,1]{0,1:T(1,128)S(1)}, s32[8,1]{0,1:T(1,128)}, u32[]{:S(2)}) copy-start(s32[8,1]{0,1:T(1,128)} %param.13) | copy-start | bytes 100
  0.6 23.5 %copy-start.11 = (s32[8]{0:T(128)S(1)}, s32[8]{0:T(128)}, u32[]{:S(2)}) copy-start(s32[8]{0:T(128)} %fill_ref.3) | copy-start | bytes 100
  0.7 23.5 %copy-start.12 = (s32[32]{0:T(128)S(1)}, s32[32]{0:T(128)}, u32[]{:S(2)}) copy-start(s32[32]{0:T(128)} %slot_ref.1) | copy-start | bytes 388
  0.7 23.5 %copy-start.1 = (bf16[1024,1024]{1,0:T(8,128)(2,1)S(1)}, bf16[1024,1024]{1,0:T(8,128)(2,1)}, u32[]{:S(2)}) copy-start(bf16[1024,1024]{1,0:T(8,128)(2,1)} %tokens_ref.3) | copy-start | bytes 6291460
  0.7 23.5 %copy-start.8 = (bf16[1024,128]{1,0:T(8,128)(2,1)S(1)}, bf16[1024,128]{1,0:T(8,128)(2,1)}, u32[]{:S(2)}) copy-start(bf16[1024,128]{1,0:T(8,128)(2,1)} %cot_ref.3) | copy-start | bytes 786436
  3.8 1.9 %collective-permute-start = (f32[5,128,128]{2,1,0:T(8,128)}, f32[5,128,128]{2,1,0:T(8,128)S(1)}, u32[]{:S(2)}, u32[]{:S(2)}) collective-permute-start(f32[5,128,128]{2,1,0:T(8,128)} %get-tuple-element.31), channel_id=1, source_target_pairs={{0,1},{1,0},{2,3},{3,2},{4,5},{5,4},{6,7},{7,6},{8,9},{9,8},{10,11... | collective-permute-start | bytes 983048 | tf_op jit(solution)/shard_map/mid_sums/ppermute | solution.py:25
  3.9 1.0 copy-start.9
  5.8 6.3 %collective-permute-start.1 = (bf16[5,128,128]{2,1,0:T(8,128)(2,1)S(1)}, bf16[5,128,128]{2,1,0:T(8,128)(2,1)S(1)}, u32[]{:S(2)}, u32[]{:S(2)}) collective-permute-start(bf16[5,128,128]{2,1,0:T(8,128)(2,1)S(1)} %get-tuple-element.33.refs_0_), channel_id=1, source_target_pairs={{0,2},{2,0},{4,6},{6,4},{1,3},{3,1},{5,7},{7,5},{8,10},{10,8},{12,... | collective-permute-start | bytes 491528 | tf_op jit(solution)/shard_map/mid_sums/ppermute | solution.py:366
  7.4 7.2 %collective-permute-start.2 = (bf16[5,128,128]{2,1,0:T(8,128)(2,1)S(1)}, bf16[5,128,128]{2,1,0:T(8,128)(2,1)S(1)}, u32[]{:S(2)}, u32[]{:S(2)}) collective-permute-start(bf16[5,128,128]{2,1,0:T(8,128)(2,1)S(1)} %get-tuple-element.34.refs_1_), channel_id=1, source_target_pairs={{0,6},{2,4},{4,2},{6,0},{1,7},{3,5},{5,3},{7,1},{8,14},{10,12},{12... | collective-permute-start | bytes 491528 | tf_op jit(solution)/shard_map/mid_sums/ppermute | solution.py:366
  14.7 7.1 %collective-permute-start.3 = (bf16[6,128,128]{2,1,0:T(8,128)(2,1)S(1)}, bf16[6,128,128]{2,1,0:T(8,128)(2,1)S(1)}, u32[]{:S(2)}, u32[]{:S(2)}) collective-permute-start(bf16[6,128,128]{2,1,0:T(8,128)(2,1)S(1)} %get-tuple-element.36.refs_0_), channel_id=1, source_target_pairs={{0,6},{2,4},{4,2},{6,0},{1,7},{3,5},{5,3},{7,1},{8,14},{10,12},{12... | collective-permute-start | bytes 589832 | tf_op jit(solution)/shard_map/mid_sums/ppermute | solution.py:368
  16.9 5.7 %collective-permute-start.4 = (bf16[6,128,128]{2,1,0:T(8,128)(2,1)S(1)}, bf16[6,128,128]{2,1,0:T(8,128)(2,1)S(1)}, u32[]{:S(2)}, u32[]{:S(2)}) collective-permute-start(bf16[6,128,128]{2,1,0:T(8,128)(2,1)S(1)} %get-tuple-element.37.refs_1_), channel_id=1, source_target_pairs={{0,2},{2,0},{4,6},{6,4},{1,3},{3,1},{5,7},{7,5},{8,10},{10,8},{12,... | collective-permute-start | bytes 589832 | tf_op jit(solution)/shard_map/mid_sums/ppermute | solution.py:368
  22.7 1.4 %collective-permute-start.5 = (bf16[4,128,128]{2,1,0:T(8,128)(2,1)S(1)}, bf16[4,128,128]{2,1,0:T(8,128)(2,1)S(1)}, u32[]{:S(2)}, u32[]{:S(2)}) collective-permute-start(bf16[4,128,128]{2,1,0:T(8,128)(2,1)S(1)} %get-tuple-element.38.mids_ref), channel_id=1, source_target_pairs={{0,1},{1,0},{2,3},{3,2},{4,5},{5,4},{6,7},{7,6},{8,9},{9,8},{10,11... | collective-permute-start | bytes 393224 | tf_op jit(solution)/shard_map/mid_sums/ppermute | solution.py:25
  25.5 1.4 %copy-start = (bf16[8,1168,128]{2,1,0:T(8,128)(2,1)}, bf16[8,1168,128]{2,1,0:T(8,128)(2,1)S(1)}, u32[]{:S(2)}) copy-start(bf16[8,1168,128]{2,1,0:T(8,128)(2,1)S(1)} %products.1) | copy-start | bytes 7176196
  26.9 0.7 copy-start.6
  27.7 6.0 %copy-start.4 = (bf16[32,128,128]{2,1,0:T(8,128)(2,1)S(1)}, bf16[32,128,128]{2,1,0:T(8,128)(2,1)}, u32[]{:S(2)}) copy-start(bf16[32,128,128]{2,1,0:T(8,128)(2,1)} %picked_ref.1) | copy-start | bytes 3145732
  27.7 35.1 %all-to-all-start = ((bf16[8,1168,128]{2,1,0:T(8,128)(2,1)}), bf16[8,1168,128]{2,1,0:T(8,128)(2,1)S(1)}, u32[]{:S(2)}, u32[]{:S(2)}) async-start(bf16[8,1168,128]{2,1,0:T(8,128)(2,1)} %copy-done), calls=%async_computation | async-start | bytes 4784128 | tf_op jit(solution)/shard_map/terms_over_first/all_to_all | solution.py:375
  33.6 1.6 %copy-start.2 = (bf16[1024,1024]{1,0:T(8,128)(2,1)S(1)}, bf16[1024,1024]{1,0:T(8,128)(2,1)}, u32[]{:S(2)}) copy-start(bf16[1024,1024]{1,0:T(8,128)(2,1)} %tokens_ref.3) | copy-start | bytes 6291460
  35.2 1.6 %copy-start.5 = (bf16[1024,1024]{1,0:T(8,128)(2,1)S(1)}, bf16[1024,1024]{1,0:T(8,128)(2,1)}, u32[]{:S(2)}) copy-start(bf16[1024,1024]{1,0:T(8,128)(2,1)} %weight_ref.1) | copy-start | bytes 6291460
  36.8 0.9 copy-start.7
  42.2 4.2 %collective-permute-start.6 = (f32[4,128,1024]{2,1,0:T(8,128)S(1)}, f32[4,128,1024]{2,1,0:T(8,128)S(1)}, u32[]{:S(2)}, u32[]{:S(2)}) collective-permute-start(f32[4,128,1024]{2,1,0:T(8,128)S(1)} %get-tuple-element.41), channel_id=1, source_target_pairs={{0,1},{1,0},{2,3},{3,2},{4,5},{5,4},{6,7},{7,6},{8,9},{9,8},{10,11... | collective-permute-start | bytes 6291464 | tf_op jit(solution)/shard_map/keys_core/ppermute | solution.py:25
  46.8 0.8 copy-start.13
  47.6 0.8 copy-start.15
  64.5 1.0 copy-start.3
  65.5 10.0 %copy-start.16 = (f32[128,1024]{1,0:T(8,128)S(1)}, f32[128,1024]{1,0:T(8,128)}, u32[]{:S(2)}) copy-start(f32[128,1024]{1,0:T(8,128)} %copy-done.15) | copy-start | bytes 1572868
  65.5 10.2 %copy-start.14 = (f32[128,1024]{1,0:T(8,128)S(1)}, f32[128,1024]{1,0:T(8,128)}, u32[]{:S(2)}) copy-start(f32[128,1024]{1,0:T(8,128)} %copy-done.13) | copy-start | bytes 1572868
  65.5 40.4 %all-to-all-start.1 = ((bf16[32,144,128]{2,1,0:T(8,128)(2,1)}), bf16[32,144,128]{2,1,0:T(8,128)(2,1)S(1)}, u32[]{:S(2)}, u32[]{:S(2)}) async-start(bf16[32,144,128]{2,1,0:T(8,128)(2,1)} %copy-done.3), calls=%async_computation.1 | async-start | bytes 2359296 | tf_op jit(solution)/shard_map/sums_over_adapter/all_to_all | solution.py:391
  75.5 24.9 %collective-permute-start.7 = (f32[128,1024]{1,0:T(8,128)S(1)}, f32[128,1024]{1,0:T(8,128)S(1)}, u32[]{:S(2)}, u32[]{:S(2)}) collective-permute-start(f32[128,1024]{1,0:T(8,128)S(1)} %copy-done.16), channel_id=1, source_target_pairs={{0,2},{2,4},{4,6},{6,0},{1,3},{3,5},{5,7},{7,1},{8,10},{10,12},{12... | collective-permute-start | bytes 1572872 | tf_op jit(solution)/shard_map/keys_y/ppermute | solution.py:25
  75.7 24.7 %collective-permute-start.8 = (f32[128,1024]{1,0:T(8,128)S(1)}, f32[128,1024]{1,0:T(8,128)S(1)}, u32[]{:S(2)}, u32[]{:S(2)}) collective-permute-start(f32[128,1024]{1,0:T(8,128)S(1)} %copy-done.14), channel_id=1, source_target_pairs={{0,4},{2,6},{4,0},{6,2},{1,5},{3,7},{5,1},{7,3},{8,12},{10,14},{12... | collective-permute-start | bytes 1572872 | tf_op jit(solution)/shard_map/keys_y/ppermute | solution.py:25
  78.4 22.6 %collective-permute-start.9 = (f32[128,1024]{1,0:T(8,128)S(1)}, f32[128,1024]{1,0:T(8,128)S(1)}, u32[]{:S(2)}, u32[]{:S(2)}) collective-permute-start(f32[128,1024]{1,0:T(8,128)S(1)} %get-tuple-element.49), channel_id=1, source_target_pairs={{0,6},{2,0},{4,2},{6,4},{1,7},{3,1},{5,3},{7,5},{8,14},{10,8},{12,... | collective-permute-start | bytes 1572872 | tf_op jit(solution)/shard_map/keys_y/ppermute | solution.py:25

commit v6 on v5

--- a/solution.py
+++ b/solution.py
@@ -69,11 +69,10 @@
     out = jax.ShapeDtypeStruct((half + 1, BLK, rank), F32)
     return pl.pallas_call(
         kernel,
-        out_shape=[out, out],
+        out_shape=[out, out, jax.ShapeDtypeStruct((nblocks, rank, features), BF16)],
         in_specs=[SMEM, SMEM, HBM, HBM, VMEM],
-        out_specs=[VMEM] * 2,
+        out_specs=[VMEM] * 3,
         scratch_shapes=[
-            pltpu.VMEM((nblocks, rank, features), BF16),
             pltpu.VMEM(cotangent.shape, BF16),
             pltpu.SemaphoreType.DMA((nblocks + 1,)),
         ],
@@ -278,17 +277,16 @@
     )(owned)
 
 
-def keys_partials(place, jobs, tokens, frozen_weight, saved_rows, up_stack):
+def keys_partials(place, tokens, frozen_weight, saved_rows, picked):
     rows, width = tokens.shape
-    nblocks = jobs.shape[0]
-    rank, features = up_stack.shape[1:]
+    nblocks, rank, features = picked.shape
     half = nblocks // 2
     total = frozen_weight.shape[1]
 
     def block_of(i, j, place_ref):
         return 2 * j + lax.rem(place_ref[1] + i, 2)
 
-    def kernel(place_ref, jobs_ref, tokens_ref, weight_ref, saved_ref, picked_ref, own_ref, other_ref):
+    def kernel(place_ref, tokens_ref, weight_ref, saved_ref, picked_ref, own_ref, other_ref):
         columns = pl.ds(pl.multiple_of((2 * place_ref[0] + place_ref[1]) * features, features), features)
         for i, out_ref in enumerate((own_ref, other_ref)):
 
@@ -303,26 +301,23 @@
     return pl.pallas_call(
         kernel,
         grid_spec=pltpu.PrefetchScalarGridSpec(
-            num_scalar_prefetch=2,
+            num_scalar_prefetch=1,
             grid=(2, half),
             in_specs=[
-                pl.BlockSpec((BLK, width), lambda i, j, place, jobs: (block_of(i, j, place), 0)),
-                pl.BlockSpec((width, total), lambda i, j, place, jobs: (0, 0)),
-                pl.BlockSpec((1, BLK, rank), lambda i, j, place, jobs: (block_of(i, j, place), 0, 0)),
-                pl.BlockSpec(
-                    (1, rank, features),
-                    lambda i, j, place, jobs: (jobs[block_of(i, j, place)], 0, 0),
-                ),
+                pl.BlockSpec((BLK, width), lambda i, j, place: (block_of(i, j, place), 0)),
+                pl.BlockSpec((width, total), lambda i, j, place: (0, 0)),
+                pl.BlockSpec((1, BLK, rank), lambda i, j, place: (block_of(i, j, place), 0, 0)),
+                pl.BlockSpec((1, rank, features), lambda i, j, place: (block_of(i, j, place), 0, 0)),
             ],
             out_specs=[
-                pl.BlockSpec((1, BLK, total), lambda i, j, place, jobs: (jnp.where(i == 0, j, half - 1), 0, 0)),
-                pl.BlockSpec((1, BLK, total), lambda i, j, place, jobs: (jnp.where(i == 0, 0, j), 0, 0)),
+                pl.BlockSpec((1, BLK, total), lambda i, j, place: (jnp.where(i == 0, j, half - 1), 0, 0)),
+                pl.BlockSpec((1, BLK, total), lambda i, j, place: (jnp.where(i == 0, 0, j), 0, 0)),
             ],
         ),
         out_shape=[shape, shape],
         compiler_params=LIMIT,
         name="keys_partials",
-    )(place, jobs, tokens, frozen_weight, saved_rows, up_stack)
+    )(place, tokens, frozen_weight, saved_rows, picked)
 
 
 def keys_chip_sums(own, received):
@@ -358,7 +353,7 @@
     place = jnp.stack([lax.axis_index(name) for name in SEQ]).astype(jnp.int32)
 
     with jax.named_scope("mid_sums"):
-        own, other = mid_partials(jobs, block_fill, up_stack, cotangent, saved_mid)
+        own, other, picked = mid_partials(jobs, block_fill, up_stack, cotangent, saved_mid)
         own_sums, own_saved = own_parts(own)
         keep, *sent = y_first(own_sums, own_saved, shift(other, "core", 1))
         pair = [(i, i ^ 1) for i in range(ny)]
@@ -374,9 +369,7 @@
         )
         terms = lax.all_to_all(terms, FIRST, split_axis=0, concat_axis=0, tiled=True)
     with jax.named_scope("keys_core"):
-        keys_own, keys_other = keys_partials(
-            place, jobs, tokens, frozen_weight, saved_rows, up_stack
-        )
+        keys_own, keys_other = keys_partials(place, tokens, frozen_weight, saved_rows, picked)
         keys_parts = keys_chip_sums(keys_own, shift(keys_other, "core", 1))
         terms, keys_parts = lax.optimization_barrier((terms, keys_parts))
     with jax.named_scope("keys_y"):

time: 107 us -> 107 us (level)
  local copies, waits for them, and re-layouts: 9.86 us -> 8.21 us
  waiting for transfers between devices: 57.6 us -> 58.7 us
    unnamed x34 -> x30, local copies, waits for them, and re-layouts: 9.86 us -> 8.21 us
where the time goes in v6:
time: 107 us; the launch traced here: 106 us
  waiting for transfers between devices  58.7 us (55%)
  starting transfers between devices  25.6 us (24%)
  Pallas kernels  11.9 us (11%)
  local copies, waits for them, and re-layouts  8.21 us (8%)
  other arithmetic  1.12 us (1%)
    ppermute x6, waiting for transfers between devices, shift(): lax.ppermute(value, axis, [(i, (i + distance) % size) for i in range(size)])  28.5 us
    all_to_all x1, waiting for transfers between devices, per_device(): lax.all_to_all(terms, FIRST, split_axis=0, concat_axis=0, tiled=True)  15.4 us
    all_to_all x1, starting transfers between devices, per_device(): lax.all_to_all(sums, ADAPTER, split_axis=0, concat_axis=0, tiled=True)  9.96 us
    unnamed x30, local copies, waits for them, and re-layouts  8.21 us
    all_to_all x1, starting transfers between devices, per_device(): lax.all_to_all(terms, FIRST, split_axis=0, concat_axis=0, tiled=True)  5.89 us
    ppermute x1, waiting for transfers between devices, per_device(): lax.ppermute(sent[0], 'y', mirror)  4.82 us
    pallas_call x1, Pallas kernels, keys_partials(): pl.pallas_call(kernel, grid_spec=pltpu.PrefetchScalarGridSpec(num_scalar_...  4.47 us
    all_to_all x1, waiting for transfers between devices, per_device(): lax.all_to_all(sums, ADAPTER, split_axis=0, concat_axis=0, tiled=True)  4.1 us
  transfers between devices with their start and end apart: 12, of which 11 were waited for; matrix products, arithmetic and copies ran while one was open for 1% of the time, Pallas kernels for 4%

profile of v6, /device:TPU:32, one launch (start us, length us, event | category | flops | bytes accessed | tf_op | source)
XLA Modules:
  0.0 106.3 jit_solution(425391825799136612)
XLA Ops:
  0.7 3.2 %mid_partials.1 = (f32[5,128,128]{2,1,0:T(8,128)}, f32[5,128,128]{2,1,0:T(8,128)}, bf16[8,128,128]{2,1,0:T(8,128)(2,1)}) custom-call(s32[8]{0:T(128)} %bitcast.7, s32[8]{0:T(128)} %fill_ref.3, bf16[32,128,128]{2,1,0:T(8,128)(2,1)} %up_ref.1, bf16[1024,128]{1,0:T(8,128)(2,1)} %cot_ref.3, bf16[128,128]{1,0:T(8,128)(2,1)} %saved_ref.1), custom_call_target="tpu_custom_call" | custom-call | tf_op jit(solution)/shard_map/mid_sums/mid_partials/pallas_call | solution.py:70
  4.0 1.0 copy-done.6
  5.0 0.8 collective-permute-done.received_ref
  5.9 1.7 %collective-permute-start.1 = (bf16[5,128,128]{2,1,0:T(8,128)(2,1)S(1)}, bf16[5,128,128]{2,1,0:T(8,128)(2,1)S(1)}, u32[]{:S(2)}, u32[]{:S(2)}) collective-permute-start(bf16[5,128,128]{2,1,0:T(8,128)(2,1)S(1)} %get-tuple-element.34.refs_0_), channel_id=1, source_target_pairs={{0,2},{2,0},{4,6},{6,4},{1,3},{3,1},{5,7},{7,5},{8,10},{10,8},{12,... | collective-permute-start | bytes 491528 | tf_op jit(solution)/shard_map/mid_sums/ppermute | solution.py:361
  7.5 2.2 %collective-permute-start.2 = (bf16[5,128,128]{2,1,0:T(8,128)(2,1)S(1)}, bf16[5,128,128]{2,1,0:T(8,128)(2,1)S(1)}, u32[]{:S(2)}, u32[]{:S(2)}) collective-permute-start(bf16[5,128,128]{2,1,0:T(8,128)(2,1)S(1)} %get-tuple-element.35.refs_1_), channel_id=1, source_target_pairs={{0,6},{2,4},{4,2},{6,0},{1,7},{3,5},{5,3},{7,1},{8,14},{10,12},{12... | collective-permute-start | bytes 491528 | tf_op jit(solution)/shard_map/mid_sums/ppermute | solution.py:361
  9.7 2.5 %collective-permute-done.1.refs_2_ = bf16[5,128,128]{2,1,0:T(8,128)(2,1)S(1)} collective-permute-done((bf16[5,128,128]{2,1,0:T(8,128)(2,1)S(1)}, bf16[5,128,128]{2,1,0:T(8,128)(2,1)S(1)}, u32[]{:S(2)}, u32[]{:S(2)}) %collective-permute-start.1) | collective-permute-done | bytes 163872 | tf_op jit(solution)/shard_map/mid_sums/ppermute | solution.py:361
  12.2 2.5 %collective-permute-done.2.refs_3_ = bf16[5,128,128]{2,1,0:T(8,128)(2,1)S(1)} collective-permute-done((bf16[5,128,128]{2,1,0:T(8,128)(2,1)S(1)}, bf16[5,128,128]{2,1,0:T(8,128)(2,1)S(1)}, u32[]{:S(2)}, u32[]{:S(2)}) %collective-permute-start.2) | collective-permute-done | bytes 163872 | tf_op jit(solution)/shard_map/mid_sums/ppermute | solution.py:361
  14.8 2.3 %collective-permute-start.3 = (bf16[6,128,128]{2,1,0:T(8,128)(2,1)S(1)}, bf16[6,128,128]{2,1,0:T(8,128)(2,1)S(1)}, u32[]{:S(2)}, u32[]{:S(2)}) collective-permute-start(bf16[6,128,128]{2,1,0:T(8,128)(2,1)S(1)} %get-tuple-element.37.refs_0_), channel_id=1, source_target_pairs={{0,6},{2,4},{4,2},{6,0},{1,7},{3,5},{5,3},{7,1},{8,14},{10,12},{12... | collective-permute-start | bytes 589832 | tf_op jit(solution)/shard_map/mid_sums/ppermute | solution.py:363
  17.0 4.8 %collective-permute-done.3.refs_2_ = bf16[6,128,128]{2,1,0:T(8,128)(2,1)S(1)} collective-permute-done((bf16[6,128,128]{2,1,0:T(8,128)(2,1)S(1)}, bf16[6,128,128]{2,1,0:T(8,128)(2,1)S(1)}, u32[]{:S(2)}, u32[]{:S(2)}) %collective-permute-start.3) | collective-permute-done | bytes 196640 | tf_op jit(solution)/shard_map/mid_sums/ppermute | solution.py:363
  21.9 0.8 collective-permute-done.4.refs_3_
  22.9 1.3 %collective-permute-done.5.other_ref = bf16[4,128,128]{2,1,0:T(8,128)(2,1)S(1)} collective-permute-done((bf16[4,128,128]{2,1,0:T(8,128)(2,1)S(1)}, bf16[4,128,128]{2,1,0:T(8,128)(2,1)S(1)}, u32[]{:S(2)}, u32[]{:S(2)}) %collective-permute-start.5) | collective-permute-done | bytes 131104 | tf_op jit(solution)/shard_map/mid_sums/ppermute | solution.py:25
  24.2 1.4 %products.1 = bf16[8,1168,128]{2,1,0:T(8,128)(2,1)S(1)} custom-call(s32[8]{0:T(128)S(1)} %bitcast.8, s32[8]{0:T(128)S(1)} %copy-done.9, s32[32]{0:T(128)S(1)} %copy-done.10, bf16[1024,1024]{1,0:T(8,128)(2,1)S(1)} %copy-done.1, bf16[4,128,128]{2,1,0:T(8,128)(2,1)S(1)} %get-tuple-element.39.mids_ref, ...), custom_call_target="tpu_custom_call" | custom-call | tf_op jit(solution)/shard_map/terms_over_first/products/pallas_call | solution.py:220
  25.6 1.4 %copy-done = bf16[8,1168,128]{2,1,0:T(8,128)(2,1)} copy-done((bf16[8,1168,128]{2,1,0:T(8,128)(2,1)}, bf16[8,1168,128]{2,1,0:T(8,128)(2,1)S(1)}, u32[]{:S(2)}) %copy-start) | copy-done | bytes 2392088
  27.0 5.9 %all-to-all-start = ((bf16[8,1168,128]{2,1,0:T(8,128)(2,1)}), bf16[8,1168,128]{2,1,0:T(8,128)(2,1)S(1)}, u32[]{:S(2)}, u32[]{:S(2)}) async-start(bf16[8,1168,128]{2,1,0:T(8,128)(2,1)} %copy-done), calls=%async_computation | async-start | bytes 4784128 | tf_op jit(solution)/shard_map/terms_over_first/all_to_all | solution.py:370
  33.0 1.6 %copy-done.2 = bf16[1024,1024]{1,0:T(8,128)(2,1)S(1)} copy-done((bf16[1024,1024]{1,0:T(8,128)(2,1)S(1)}, bf16[1024,1024]{1,0:T(8,128)(2,1)}, u32[]{:S(2)}) %copy-start.2) | copy-done | bytes 2097176
  34.6 1.6 %copy-done.4 = bf16[1024,1024]{1,0:T(8,128)(2,1)S(1)} copy-done((bf16[1024,1024]{1,0:T(8,128)(2,1)S(1)}, bf16[1024,1024]{1,0:T(8,128)(2,1)}, u32[]{:S(2)}) %copy-start.4) | copy-done | bytes 2097176
  36.2 4.5 %keys_partials.1 = (f32[4,128,1024]{2,1,0:T(8,128)S(1)}, f32[4,128,1024]{2,1,0:T(8,128)S(1)}) custom-call(s32[2]{0:T(128)S(1)} %pad_add_fusion.place_ref, bf16[1024,1024]{1,0:T(8,128)(2,1)S(1)} %copy-done.2, bf16[1024,1024]{1,0:T(8,128)(2,1)S(1)} %copy-done.4, bf16[8,128,128]{2,1,0:T(8,128)(2,1)S(1)} %get-tuple-element.40.saved_ref, ...), custom_call_target="tpu_custom_call" | custom-call | tf_op jit(solution)/shard_map/keys_core/keys_partials/pallas_call | solution.py:301
  40.8 4.1 %collective-permute-done.6.received_ref = f32[4,128,1024]{2,1,0:T(8,128)S(1)} collective-permute-done((f32[4,128,1024]{2,1,0:T(8,128)S(1)}, f32[4,128,1024]{2,1,0:T(8,128)S(1)}, u32[]{:S(2)}, u32[]{:S(2)}) %collective-permute-start.6) | collective-permute-done | bytes 2097184 | tf_op jit(solution)/shard_map/keys_core/ppermute | solution.py:25
  44.9 0.2 keys_chip_sums.1
  45.1 0.8 copy-done.11
  45.9 0.8 copy-done.13
  46.7 15.4 %all-to-all-done.terms_ref = bf16[8,1168,128]{2,1,0:T(8,128)(2,1)S(1)} async-done(((bf16[8,1168,128]{2,1,0:T(8,128)(2,1)}), bf16[8,1168,128]{2,1,0:T(8,128)(2,1)S(1)}, u32[]{:S(2)}, u32[]{:S(2)}) %all-to-all-start) | async-done | bytes 2392096 | tf_op jit(solution)/shard_map/terms_over_first/all_to_all | solution.py:370
  62.4 1.5 %slot_sums.1 = bf16[32,144,128]{2,1,0:T(8,128)(2,1)S(1)} custom-call(s32[8,8]{1,0:T(8,128)S(1)} %convert_reduce_fusion.slots_ref, bf16[8,1168,128]{2,1,0:T(8,128)(2,1)S(1)} %all-to-all-done.terms_ref), custom_call_target="tpu_custom_call" | custom-call | tf_op jit(solution)/shard_map/sums_over_adapter/slot_sums/pallas_call | solution.py:242
  63.9 1.0 copy-done.3
  64.9 10.0 %all-to-all-start.1 = ((bf16[32,144,128]{2,1,0:T(8,128)(2,1)}), bf16[32,144,128]{2,1,0:T(8,128)(2,1)S(1)}, u32[]{:S(2)}, u32[]{:S(2)}) async-start(bf16[32,144,128]{2,1,0:T(8,128)(2,1)} %copy-done.3), calls=%async_computation.1 | async-start | bytes 2359296 | tf_op jit(solution)/shard_map/sums_over_adapter/all_to_all | solution.py:384
  75.1 2.7 %collective-permute-start.8 = (f32[128,1024]{1,0:T(8,128)S(1)}, f32[128,1024]{1,0:T(8,128)S(1)}, u32[]{:S(2)}, u32[]{:S(2)}) collective-permute-start(f32[128,1024]{1,0:T(8,128)S(1)} %copy-done.12), channel_id=1, source_target_pairs={{0,4},{2,6},{4,0},{6,2},{1,5},{3,7},{5,1},{7,3},{8,12},{10,14},{12... | collective-permute-start | bytes 1572872 | tf_op jit(solution)/shard_map/keys_y/ppermute | solution.py:25
  77.8 0.4 collective-permute-start.9
  78.2 21.5 %collective-permute-done.7 = f32[128,1024]{1,0:T(8,128)S(1)} collective-permute-done((f32[128,1024]{1,0:T(8,128)S(1)}, f32[128,1024]{1,0:T(8,128)S(1)}, u32[]{:S(2)}, u32[]{:S(2)}) %collective-permute-start.7) | collective-permute-done | bytes 524320 | tf_op jit(solution)/shard_map/keys_y/ppermute | solution.py:25
  99.7 0.6 collective-permute-done.9
  100.4 0.8 add_convert_fusion
  101.2 4.1 %all-to-all-done.1 = bf16[32,144,128]{2,1,0:T(8,128)(2,1)S(1)} async-done(((bf16[32,144,128]{2,1,0:T(8,128)(2,1)}), bf16[32,144,128]{2,1,0:T(8,128)(2,1)S(1)}, u32[]{:S(2)}, u32[]{:S(2)}) %all-to-all-start.1) | async-done | bytes 1179680 | tf_op jit(solution)/shard_map/sums_over_adapter/all_to_all | solution.py:384
  105.3 1.0 finish.1
  (35 shorter events, 1.0 us)
Async XLA Ops:
  0.6 23.6 %copy-start.8 = (s32[8,1]{0,1:T(1,128)S(1)}, s32[8,1]{0,1:T(1,128)}, u32[]{:S(2)}) copy-start(s32[8,1]{0,1:T(1,128)} %param.13) | copy-start | bytes 100
  0.6 23.6 %copy-start.9 = (s32[8]{0:T(128)S(1)}, s32[8]{0:T(128)}, u32[]{:S(2)}) copy-start(s32[8]{0:T(128)} %fill_ref.3) | copy-start | bytes 100
  0.7 23.6 %copy-start.10 = (s32[32]{0:T(128)S(1)}, s32[32]{0:T(128)}, u32[]{:S(2)}) copy-start(s32[32]{0:T(128)} %slot_ref.1) | copy-start | bytes 388
  0.7 23.5 %copy-start.1 = (bf16[1024,1024]{1,0:T(8,128)(2,1)S(1)}, bf16[1024,1024]{1,0:T(8,128)(2,1)}, u32[]{:S(2)}) copy-start(bf16[1024,1024]{1,0:T(8,128)(2,1)} %tokens_ref.3) | copy-start | bytes 6291460
  0.7 23.5 %copy-start.5 = (bf16[1024,128]{1,0:T(8,128)(2,1)S(1)}, bf16[1024,128]{1,0:T(8,128)(2,1)}, u32[]{:S(2)}) copy-start(bf16[1024,128]{1,0:T(8,128)(2,1)} %cot_ref.3) | copy-start | bytes 786436
  3.9 1.9 %collective-permute-start = (f32[5,128,128]{2,1,0:T(8,128)}, f32[5,128,128]{2,1,0:T(8,128)S(1)}, u32[]{:S(2)}, u32[]{:S(2)}) collective-permute-start(f32[5,128,128]{2,1,0:T(8,128)} %get-tuple-element.32), channel_id=1, source_target_pairs={{0,1},{1,0},{2,3},{3,2},{4,5},{5,4},{6,7},{7,6},{8,9},{9,8},{10,11... | collective-permute-start | bytes 983048 | tf_op jit(solution)/shard_map/mid_sums/ppermute | solution.py:25
  4.0 1.0 copy-start.6
  5.9 6.3 %collective-permute-start.1 = (bf16[5,128,128]{2,1,0:T(8,128)(2,1)S(1)}, bf16[5,128,128]{2,1,0:T(8,128)(2,1)S(1)}, u32[]{:S(2)}, u32[]{:S(2)}) collective-permute-start(bf16[5,128,128]{2,1,0:T(8,128)(2,1)S(1)} %get-tuple-element.34.refs_0_), channel_id=1, source_target_pairs={{0,2},{2,0},{4,6},{6,4},{1,3},{3,1},{5,7},{7,5},{8,10},{10,8},{12,... | collective-permute-start | bytes 491528 | tf_op jit(solution)/shard_map/mid_sums/ppermute | solution.py:361
  7.5 7.2 %collective-permute-start.2 = (bf16[5,128,128]{2,1,0:T(8,128)(2,1)S(1)}, bf16[5,128,128]{2,1,0:T(8,128)(2,1)S(1)}, u32[]{:S(2)}, u32[]{:S(2)}) collective-permute-start(bf16[5,128,128]{2,1,0:T(8,128)(2,1)S(1)} %get-tuple-element.35.refs_1_), channel_id=1, source_target_pairs={{0,6},{2,4},{4,2},{6,0},{1,7},{3,5},{5,3},{7,1},{8,14},{10,12},{12... | collective-permute-start | bytes 491528 | tf_op jit(solution)/shard_map/mid_sums/ppermute | solution.py:361
  14.8 7.1 %collective-permute-start.3 = (bf16[6,128,128]{2,1,0:T(8,128)(2,1)S(1)}, bf16[6,128,128]{2,1,0:T(8,128)(2,1)S(1)}, u32[]{:S(2)}, u32[]{:S(2)}) collective-permute-start(bf16[6,128,128]{2,1,0:T(8,128)(2,1)S(1)} %get-tuple-element.37.refs_0_), channel_id=1, source_target_pairs={{0,6},{2,4},{4,2},{6,0},{1,7},{3,5},{5,3},{7,1},{8,14},{10,12},{12... | collective-permute-start | bytes 589832 | tf_op jit(solution)/shard_map/mid_sums/ppermute | solution.py:363
  17.0 5.7 %collective-permute-start.4 = (bf16[6,128,128]{2,1,0:T(8,128)(2,1)S(1)}, bf16[6,128,128]{2,1,0:T(8,128)(2,1)S(1)}, u32[]{:S(2)}, u32[]{:S(2)}) collective-permute-start(bf16[6,128,128]{2,1,0:T(8,128)(2,1)S(1)} %get-tuple-element.38.refs_1_), channel_id=1, source_target_pairs={{0,2},{2,0},{4,6},{6,4},{1,3},{3,1},{5,7},{7,5},{8,10},{10,8},{12,... | collective-permute-start | bytes 589832 | tf_op jit(solution)/shard_map/mid_sums/ppermute | solution.py:363
  22.8 1.4 %collective-permute-start.5 = (bf16[4,128,128]{2,1,0:T(8,128)(2,1)S(1)}, bf16[4,128,128]{2,1,0:T(8,128)(2,1)S(1)}, u32[]{:S(2)}, u32[]{:S(2)}) collective-permute-start(bf16[4,128,128]{2,1,0:T(8,128)(2,1)S(1)} %get-tuple-element.39.mids_ref), channel_id=1, source_target_pairs={{0,1},{1,0},{2,3},{3,2},{4,5},{5,4},{6,7},{7,6},{8,9},{9,8},{10,11... | collective-permute-start | bytes 393224 | tf_op jit(solution)/shard_map/mid_sums/ppermute | solution.py:25
  25.6 1.4 %copy-start = (bf16[8,1168,128]{2,1,0:T(8,128)(2,1)}, bf16[8,1168,128]{2,1,0:T(8,128)(2,1)S(1)}, u32[]{:S(2)}) copy-start(bf16[8,1168,128]{2,1,0:T(8,128)(2,1)S(1)} %products.1) | copy-start | bytes 7176196
  27.0 6.0 %copy-start.7 = (bf16[8,128,128]{2,1,0:T(8,128)(2,1)S(1)}, bf16[8,128,128]{2,1,0:T(8,128)(2,1)}, u32[]{:S(2)}) copy-start(bf16[8,128,128]{2,1,0:T(8,128)(2,1)} %get-tuple-element.41.picked_ref) | copy-start | bytes 786436
  27.0 35.1 %all-to-all-start = ((bf16[8,1168,128]{2,1,0:T(8,128)(2,1)}), bf16[8,1168,128]{2,1,0:T(8,128)(2,1)S(1)}, u32[]{:S(2)}, u32[]{:S(2)}) async-start(bf16[8,1168,128]{2,1,0:T(8,128)(2,1)} %copy-done), calls=%async_computation | async-start | bytes 4784128 | tf_op jit(solution)/shard_map/terms_over_first/all_to_all | solution.py:370
  33.0 1.6 %copy-start.2 = (bf16[1024,1024]{1,0:T(8,128)(2,1)S(1)}, bf16[1024,1024]{1,0:T(8,128)(2,1)}, u32[]{:S(2)}) copy-start(bf16[1024,1024]{1,0:T(8,128)(2,1)} %tokens_ref.3) | copy-start | bytes 6291460
  34.6 1.6 %copy-start.4 = (bf16[1024,1024]{1,0:T(8,128)(2,1)S(1)}, bf16[1024,1024]{1,0:T(8,128)(2,1)}, u32[]{:S(2)}) copy-start(bf16[1024,1024]{1,0:T(8,128)(2,1)} %weight_ref.1) | copy-start | bytes 6291460
  40.7 4.2 %collective-permute-start.6 = (f32[4,128,1024]{2,1,0:T(8,128)S(1)}, f32[4,128,1024]{2,1,0:T(8,128)S(1)}, u32[]{:S(2)}, u32[]{:S(2)}) collective-permute-start(f32[4,128,1024]{2,1,0:T(8,128)S(1)} %get-tuple-element.43), channel_id=1, source_target_pairs={{0,1},{1,0},{2,3},{3,2},{4,5},{5,4},{6,7},{7,6},{8,9},{9,8},{10,11... | collective-permute-start | bytes 6291464 | tf_op jit(solution)/shard_map/keys_core/ppermute | solution.py:25
  45.1 0.8 copy-start.11
  45.9 0.8 copy-start.13
  63.9 1.0 copy-start.3
  64.9 10.0 %copy-start.14 = (f32[128,1024]{1,0:T(8,128)S(1)}, f32[128,1024]{1,0:T(8,128)}, u32[]{:S(2)}) copy-start(f32[128,1024]{1,0:T(8,128)} %copy-done.13) | copy-start | bytes 1572868
  64.9 10.2 %copy-start.12 = (f32[128,1024]{1,0:T(8,128)S(1)}, f32[128,1024]{1,0:T(8,128)}, u32[]{:S(2)}) copy-start(f32[128,1024]{1,0:T(8,128)} %copy-done.11) | copy-start | bytes 1572868
  64.9 40.4 %all-to-all-start.1 = ((bf16[32,144,128]{2,1,0:T(8,128)(2,1)}), bf16[32,144,128]{2,1,0:T(8,128)(2,1)S(1)}, u32[]{:S(2)}, u32[]{:S(2)}) async-start(bf16[32,144,128]{2,1,0:T(8,128)(2,1)} %copy-done.3), calls=%async_computation.1 | async-start | bytes 2359296 | tf_op jit(solution)/shard_map/sums_over_adapter/all_to_all | solution.py:384
  74.9 24.9 %collective-permute-start.7 = (f32[128,1024]{1,0:T(8,128)S(1)}, f32[128,1024]{1,0:T(8,128)S(1)}, u32[]{:S(2)}, u32[]{:S(2)}) collective-permute-start(f32[128,1024]{1,0:T(8,128)S(1)} %copy-done.14), channel_id=1, source_target_pairs={{0,2},{2,4},{4,6},{6,0},{1,3},{3,5},{5,7},{7,1},{8,10},{10,12},{12... | collective-permute-start | bytes 1572872 | tf_op jit(solution)/shard_map/keys_y/ppermute | solution.py:25
  75.1 24.7 %collective-permute-start.8 = (f32[128,1024]{1,0:T(8,128)S(1)}, f32[128,1024]{1,0:T(8,128)S(1)}, u32[]{:S(2)}, u32[]{:S(2)}) collective-permute-start(f32[128,1024]{1,0:T(8,128)S(1)} %copy-done.12), channel_id=1, source_target_pairs={{0,4},{2,6},{4,0},{6,2},{1,5},{3,7},{5,1},{7,3},{8,12},{10,14},{12... | collective-permute-start | bytes 1572872 | tf_op jit(solution)/shard_map/keys_y/ppermute | solution.py:25
  77.8 22.6 %collective-permute-start.9 = (f32[128,1024]{1,0:T(8,128)S(1)}, f32[128,1024]{1,0:T(8,128)S(1)}, u32[]{:S(2)}, u32[]{:S(2)}) collective-permute-start(f32[128,1024]{1,0:T(8,128)S(1)} %get-tuple-element.51), channel_id=1, source_target_pairs={{0,6},{2,0},{4,2},{6,4},{1,7},{3,1},{5,3},{7,5},{8,14},{10,8},{12,... | collective-permute-start | bytes 1572872 | tf_op jit(solution)/shard_map/keys_y/ppermute | solution.py:25

commit v7 on v6

--- a/solution.py
+++ b/solution.py
@@ -190,41 +190,56 @@
     )(total, *sent, *received)
 
 
-def products(jobs, fills, slot_of, tokens, mids, mids_other, saved_rows, cotangent, parts):
-    width = tokens.shape[1]
+def up_products(jobs, fills, slot_of, saved_rows, cotangent):
     nblocks, _, rank = saved_rows.shape
-    part, split = width // parts, rank // parts
-    height = part + split
-
-    def kernel(
-        jobs_ref, fill_ref, slot_ref, tokens_ref, mids_ref, other_ref, saved_ref, cot_ref, out_ref
-    ):
-        core = lax.axis_index("core")
+
+    def kernel(jobs_ref, fill_ref, slot_ref, saved_ref, cot_ref, up_ref, slots_ref):
         row = lax.broadcasted_iota(jnp.int32, (SLOT_ROWS, rank), 0)
         slots = jnp.zeros((SLOT_ROWS, rank), jnp.int32)
         for b in range(nblocks):
             slots = jnp.where(row == b, slot_ref[jobs_ref[b]], slots)
-        slots = slots.astype(F32).astype(BF16)
+            up_ref[b] = contract(saved_ref[b], masked(cot_ref, fill_ref, b), 0, 0).astype(BF16)
+        slots_ref[...] = slots.astype(F32).astype(BF16)
+
+    return pl.pallas_call(
+        kernel,
+        out_shape=[
+            jax.ShapeDtypeStruct((nblocks, rank, cotangent.shape[1]), BF16),
+            jax.ShapeDtypeStruct((SLOT_ROWS, rank), BF16),
+        ],
+        in_specs=[SMEM] * 3 + [VMEM] * 2,
+        out_specs=[VMEM] * 2,
+        compiler_params=LIMIT,
+        name="up_products",
+    )(jobs, fills, slot_of, saved_rows, cotangent)
+
+
+def products(tokens, mids, mids_other, ups, slot_rows, parts):
+    width = tokens.shape[1]
+    nblocks, rank, _ = ups.shape
+    part, split = width // parts, rank // parts
+    height = part + split
+
+    def kernel(tokens_ref, mids_ref, other_ref, up_ref, slots_ref, out_ref):
+        core = lax.axis_index("core")
         for i in range(parts):
-            out_ref[i, nblocks * height :, :] = slots
+            out_ref[i, nblocks * height :, :] = slots_ref[...]
         for b in range(nblocks):
-            mine, other = mids_ref[b // 2], other_ref[b // 2]
-            mid = jnp.where(core == b % 2, mine, other)
-            up = contract(saved_ref[b], masked(cot_ref, fill_ref, b), 0, 0).astype(BF16)
+            mid = jnp.where(core == b % 2, mids_ref[b // 2], other_ref[b // 2])
             first = b * height
             for i in range(parts):
                 block = tokens_ref[b * BLK : (b + 1) * BLK, i * part : (i + 1) * part]
                 out_ref[i, first : first + part, :] = contract(block, mid, 0, 0).astype(BF16)
-                out_ref[i, first + part : first + height, :] = up[i * split : (i + 1) * split]
+                out_ref[i, first + part : first + height, :] = up_ref[b, i * split : (i + 1) * split]
 
     return pl.pallas_call(
         kernel,
         out_shape=jax.ShapeDtypeStruct((parts, nblocks * height + SLOT_ROWS, rank), BF16),
-        in_specs=[SMEM] * 3 + [VMEM] * 5,
+        in_specs=[VMEM] * 5,
         out_specs=VMEM,
         compiler_params=LIMIT,
         name="products",
-    )(jobs, fills, slot_of, tokens, mids, mids_other, saved_rows, cotangent)
+    )(tokens, mids, mids_other, ups, slot_rows)
 
 
 def slot_sums(slots, terms, slot_count):
@@ -364,9 +379,8 @@
         mids, saved_rows = mid_grads(total, sent, received)
         mids_other = shift(mids, "core", 1)
     with jax.named_scope("terms_over_first"):
-        terms = products(
-            jobs, block_fill, slot_of, tokens, mids, mids_other, saved_rows, cotangent, parts
-        )
+        ups, slot_rows = up_products(jobs, block_fill, slot_of, saved_rows, cotangent)
+        terms = products(tokens, mids, mids_other, ups, slot_rows, parts)
         terms = lax.all_to_all(terms, FIRST, split_axis=0, concat_axis=0, tiled=True)
     with jax.named_scope("keys_core"):
         keys_own, keys_other = keys_partials(place, tokens, frozen_weight, saved_rows, picked)

time: 107 us -> 106 us (level)
  transfers between devices with their start and end apart: 12 -> 12, of which waited for: 11 -> 11; matrix products, arithmetic and copies ran while one was open for 1% -> 1% of each run, Pallas kernels for 4% -> 5%
where the time goes in v7:
time: 106 us
  waiting for transfers between devices  57.8 us (55%)
  starting transfers between devices  25.6 us (24%)
  Pallas kernels  12.1 us (11%)
  local copies, waits for them, and re-layouts  8.2 us (8%)
  other arithmetic  1.12 us (1%)
    ppermute x6, waiting for transfers between devices, shift(): lax.ppermute(value, axis, [(i, (i + distance) % size) for i in range(size)])  27.6 us
    all_to_all x1, waiting for transfers between devices, per_device(): lax.all_to_all(terms, FIRST, split_axis=0, concat_axis=0, tiled=True)  15.4 us
    all_to_all x1, starting transfers between devices, per_device(): lax.all_to_all(sums, ADAPTER, split_axis=0, concat_axis=0, tiled=True)  9.96 us
    unnamed x30, local copies, waits for them, and re-layouts  8.2 us
    all_to_all x1, starting transfers between devices, per_device(): lax.all_to_all(terms, FIRST, split_axis=0, concat_axis=0, tiled=True)  5.89 us
    ppermute x1, waiting for transfers between devices, per_device(): lax.ppermute(sent[0], 'y', mirror)  4.82 us
    pallas_call x1, Pallas kernels, keys_partials(): pl.pallas_call(kernel, grid_spec=pltpu.PrefetchScalarGridSpec(num_scalar_...  4.47 us
    all_to_all x1, waiting for transfers between devices, per_device(): lax.all_to_all(sums, ADAPTER, split_axis=0, concat_axis=0, tiled=True)  4.1 us
  transfers between devices with their start and end apart: 12, of which 11 were waited for; matrix products, arithmetic and copies ran while one was open for 1% of the time, Pallas kernels for 5%

profile of v7, /device:TPU:32, one launch (start us, length us, event | category | flops | bytes accessed | tf_op | source)
XLA Modules:
  0.0 105.6 jit_solution(5749796166172364620)
XLA Ops:
  0.7 3.2 %mid_partials.1 = (f32[5,128,128]{2,1,0:T(8,128)}, f32[5,128,128]{2,1,0:T(8,128)}, bf16[8,128,128]{2,1,0:T(8,128)(2,1)}) custom-call(s32[8]{0:T(128)} %bitcast.7, s32[8]{0:T(128)} %fill_ref.3, bf16[32,128,128]{2,1,0:T(8,128)(2,1)} %up_ref.1, bf16[1024,128]{1,0:T(8,128)(2,1)} %cot_ref.3, bf16[128,128]{1,0:T(8,128)(2,1)} %saved_ref.1), custom_call_target="tpu_custom_call" | custom-call | tf_op jit(solution)/shard_map/mid_sums/mid_partials/pallas_call | solution.py:70
  4.0 1.0 copy-done.6
  5.0 0.8 collective-permute-done.received_ref
  5.9 1.7 %collective-permute-start.1 = (bf16[5,128,128]{2,1,0:T(8,128)(2,1)S(1)}, bf16[5,128,128]{2,1,0:T(8,128)(2,1)S(1)}, u32[]{:S(2)}, u32[]{:S(2)}) collective-permute-start(bf16[5,128,128]{2,1,0:T(8,128)(2,1)S(1)} %get-tuple-element.36.refs_0_), channel_id=1, source_target_pairs={{0,2},{2,0},{4,6},{6,4},{1,3},{3,1},{5,7},{7,5},{8,10},{10,8},{12,... | collective-permute-start | bytes 491528 | tf_op jit(solution)/shard_map/mid_sums/ppermute | solution.py:376
  7.5 2.2 %collective-permute-start.2 = (bf16[5,128,128]{2,1,0:T(8,128)(2,1)S(1)}, bf16[5,128,128]{2,1,0:T(8,128)(2,1)S(1)}, u32[]{:S(2)}, u32[]{:S(2)}) collective-permute-start(bf16[5,128,128]{2,1,0:T(8,128)(2,1)S(1)} %get-tuple-element.37.refs_1_), channel_id=1, source_target_pairs={{0,6},{2,4},{4,2},{6,0},{1,7},{3,5},{5,3},{7,1},{8,14},{10,12},{12... | collective-permute-start | bytes 491528 | tf_op jit(solution)/shard_map/mid_sums/ppermute | solution.py:376
  9.7 2.5 %collective-permute-done.1.refs_2_ = bf16[5,128,128]{2,1,0:T(8,128)(2,1)S(1)} collective-permute-done((bf16[5,128,128]{2,1,0:T(8,128)(2,1)S(1)}, bf16[5,128,128]{2,1,0:T(8,128)(2,1)S(1)}, u32[]{:S(2)}, u32[]{:S(2)}) %collective-permute-start.1) | collective-permute-done | bytes 163872 | tf_op jit(solution)/shard_map/mid_sums/ppermute | solution.py:376
  12.2 2.5 %collective-permute-done.2.refs_3_ = bf16[5,128,128]{2,1,0:T(8,128)(2,1)S(1)} collective-permute-done((bf16[5,128,128]{2,1,0:T(8,128)(2,1)S(1)}, bf16[5,128,128]{2,1,0:T(8,128)(2,1)S(1)}, u32[]{:S(2)}, u32[]{:S(2)}) %collective-permute-start.2) | collective-permute-done | bytes 163872 | tf_op jit(solution)/shard_map/mid_sums/ppermute | solution.py:376
  14.8 2.3 %collective-permute-start.3 = (bf16[6,128,128]{2,1,0:T(8,128)(2,1)S(1)}, bf16[6,128,128]{2,1,0:T(8,128)(2,1)S(1)}, u32[]{:S(2)}, u32[]{:S(2)}) collective-permute-start(bf16[6,128,128]{2,1,0:T(8,128)(2,1)S(1)} %get-tuple-element.39.refs_0_), channel_id=1, source_target_pairs={{0,6},{2,4},{4,2},{6,0},{1,7},{3,5},{5,3},{7,1},{8,14},{10,12},{12... | collective-permute-start | bytes 589832 | tf_op jit(solution)/shard_map/mid_sums/ppermute | solution.py:378
  17.0 4.8 %collective-permute-done.3.refs_2_ = bf16[6,128,128]{2,1,0:T(8,128)(2,1)S(1)} collective-permute-done((bf16[6,128,128]{2,1,0:T(8,128)(2,1)S(1)}, bf16[6,128,128]{2,1,0:T(8,128)(2,1)S(1)}, u32[]{:S(2)}, u32[]{:S(2)}) %collective-permute-start.3) | collective-permute-done | bytes 196640 | tf_op jit(solution)/shard_map/mid_sums/ppermute | solution.py:378
  21.9 0.8 collective-permute-done.4.refs_3_
  22.9 0.8 up_products.1
  23.7 0.5 collective-permute-done.5.other_ref
  24.2 0.8 products.1
  25.0 1.4 %copy-done = bf16[8,1168,128]{2,1,0:T(8,128)(2,1)} copy-done((bf16[8,1168,128]{2,1,0:T(8,128)(2,1)}, bf16[8,1168,128]{2,1,0:T(8,128)(2,1)S(1)}, u32[]{:S(2)}) %copy-start) | copy-done | bytes 2392088
  26.4 5.9 %all-to-all-start = ((bf16[8,1168,128]{2,1,0:T(8,128)(2,1)}), bf16[8,1168,128]{2,1,0:T(8,128)(2,1)S(1)}, u32[]{:S(2)}, u32[]{:S(2)}) async-start(bf16[8,1168,128]{2,1,0:T(8,128)(2,1)} %copy-done), calls=%async_computation | async-start | bytes 4784128 | tf_op jit(solution)/shard_map/terms_over_first/all_to_all | solution.py:384
  32.4 1.6 %copy-done.2 = bf16[1024,1024]{1,0:T(8,128)(2,1)S(1)} copy-done((bf16[1024,1024]{1,0:T(8,128)(2,1)S(1)}, bf16[1024,1024]{1,0:T(8,128)(2,1)}, u32[]{:S(2)}) %copy-start.2) | copy-done | bytes 2097176
  33.9 1.6 %copy-done.4 = bf16[1024,1024]{1,0:T(8,128)(2,1)S(1)} copy-done((bf16[1024,1024]{1,0:T(8,128)(2,1)S(1)}, bf16[1024,1024]{1,0:T(8,128)(2,1)}, u32[]{:S(2)}) %copy-start.4) | copy-done | bytes 2097176
  35.5 4.5 %keys_partials.1 = (f32[4,128,1024]{2,1,0:T(8,128)S(1)}, f32[4,128,1024]{2,1,0:T(8,128)S(1)}) custom-call(s32[2]{0:T(128)S(1)} %pad_add_fusion.place_ref, bf16[1024,1024]{1,0:T(8,128)(2,1)S(1)} %copy-done.2, bf16[1024,1024]{1,0:T(8,128)(2,1)S(1)} %copy-done.4, bf16[8,128,128]{2,1,0:T(8,128)(2,1)S(1)} %get-tuple-element.42.saved_ref, ...), custom_call_target="tpu_custom_call" | custom-call | tf_op jit(solution)/shard_map/keys_core/keys_partials/pallas_call | solution.py:316
  40.1 4.1 %collective-permute-done.6.received_ref = f32[4,128,1024]{2,1,0:T(8,128)S(1)} collective-permute-done((f32[4,128,1024]{2,1,0:T(8,128)S(1)}, f32[4,128,1024]{2,1,0:T(8,128)S(1)}, u32[]{:S(2)}, u32[]{:S(2)}) %collective-permute-start.6) | collective-permute-done | bytes 2097184 | tf_op jit(solution)/shard_map/keys_core/ppermute | solution.py:25
  44.5 0.8 copy-done.11
  45.3 0.8 copy-done.13
  46.1 15.4 %all-to-all-done.terms_ref = bf16[8,1168,128]{2,1,0:T(8,128)(2,1)S(1)} async-done(((bf16[8,1168,128]{2,1,0:T(8,128)(2,1)}), bf16[8,1168,128]{2,1,0:T(8,128)(2,1)S(1)}, u32[]{:S(2)}, u32[]{:S(2)}) %all-to-all-start) | async-done | bytes 2392096 | tf_op jit(solution)/shard_map/terms_over_first/all_to_all | solution.py:384
  61.7 1.5 %slot_sums.1 = bf16[32,144,128]{2,1,0:T(8,128)(2,1)S(1)} custom-call(s32[8,8]{1,0:T(8,128)S(1)} %convert_reduce_fusion.slots_ref, bf16[8,1168,128]{2,1,0:T(8,128)(2,1)S(1)} %all-to-all-done.terms_ref), custom_call_target="tpu_custom_call" | custom-call | tf_op jit(solution)/shard_map/sums_over_adapter/slot_sums/pallas_call | solution.py:257
  63.2 1.0 copy-done.3
  64.3 10.0 %all-to-all-start.1 = ((bf16[32,144,128]{2,1,0:T(8,128)(2,1)}), bf16[32,144,128]{2,1,0:T(8,128)(2,1)S(1)}, u32[]{:S(2)}, u32[]{:S(2)}) async-start(bf16[32,144,128]{2,1,0:T(8,128)(2,1)} %copy-done.3), calls=%async_computation.1 | async-start | bytes 2359296 | tf_op jit(solution)/shard_map/sums_over_adapter/all_to_all | solution.py:398
  74.4 2.7 %collective-permute-start.8 = (f32[128,1024]{1,0:T(8,128)S(1)}, f32[128,1024]{1,0:T(8,128)S(1)}, u32[]{:S(2)}, u32[]{:S(2)}) collective-permute-start(f32[128,1024]{1,0:T(8,128)S(1)} %copy-done.12), channel_id=1, source_target_pairs={{0,4},{2,6},{4,0},{6,2},{1,5},{3,7},{5,1},{7,3},{8,12},{10,14},{12... | collective-permute-start | bytes 1572872 | tf_op jit(solution)/shard_map/keys_y/ppermute | solution.py:25
  77.1 0.5 collective-permute-start.9
  77.6 21.5 %collective-permute-done.7 = f32[128,1024]{1,0:T(8,128)S(1)} collective-permute-done((f32[128,1024]{1,0:T(8,128)S(1)}, f32[128,1024]{1,0:T(8,128)S(1)}, u32[]{:S(2)}, u32[]{:S(2)}) %collective-permute-start.7) | collective-permute-done | bytes 524320 | tf_op jit(solution)/shard_map/keys_y/ppermute | solution.py:25
  99.1 0.6 collective-permute-done.9
  99.7 0.8 add_convert_fusion
  100.6 4.1 %all-to-all-done.1 = bf16[32,144,128]{2,1,0:T(8,128)(2,1)S(1)} async-done(((bf16[32,144,128]{2,1,0:T(8,128)(2,1)}), bf16[32,144,128]{2,1,0:T(8,128)(2,1)S(1)}, u32[]{:S(2)}, u32[]{:S(2)}) %all-to-all-start.1) | async-done | bytes 1179680 | tf_op jit(solution)/shard_map/sums_over_adapter/all_to_all | solution.py:398
  104.7 1.0 finish.1
  (36 shorter events, 1.2 us)
Async XLA Ops:
  0.6 22.2 %copy-start.8 = (s32[8,1]{0,1:T(1,128)S(1)}, s32[8,1]{0,1:T(1,128)}, u32[]{:S(2)}) copy-start(s32[8,1]{0,1:T(1,128)} %param.13) | copy-start | bytes 100
  0.6 22.2 %copy-start.9 = (s32[8]{0:T(128)S(1)}, s32[8]{0:T(128)}, u32[]{:S(2)}) copy-start(s32[8]{0:T(128)} %fill_ref.3) | copy-start | bytes 100
  0.7 22.2 %copy-start.10 = (s32[32]{0:T(128)S(1)}, s32[32]{0:T(128)}, u32[]{:S(2)}) copy-start(s32[32]{0:T(128)} %slot_ref.1) | copy-start | bytes 388
  0.7 22.2 %copy-start.5 = (bf16[1024,128]{1,0:T(8,128)(2,1)S(1)}, bf16[1024,128]{1,0:T(8,128)(2,1)}, u32[]{:S(2)}) copy-start(bf16[1024,128]{1,0:T(8,128)(2,1)} %cot_ref.3) | copy-start | bytes 786436
  0.7 23.5 %copy-start.1 = (bf16[1024,1024]{1,0:T(8,128)(2,1)S(1)}, bf16[1024,1024]{1,0:T(8,128)(2,1)}, u32[]{:S(2)}) copy-start(bf16[1024,1024]{1,0:T(8,128)(2,1)} %tokens_ref.3) | copy-start | bytes 6291460
  3.9 1.9 %collective-permute-start = (f32[5,128,128]{2,1,0:T(8,128)}, f32[5,128,128]{2,1,0:T(8,128)S(1)}, u32[]{:S(2)}, u32[]{:S(2)}) collective-permute-start(f32[5,128,128]{2,1,0:T(8,128)} %get-tuple-element.34), channel_id=1, source_target_pairs={{0,1},{1,0},{2,3},{3,2},{4,5},{5,4},{6,7},{7,6},{8,9},{9,8},{10,11... | collective-permute-start | bytes 983048 | tf_op jit(solution)/shard_map/mid_sums/ppermute | solution.py:25
  4.0 1.0 copy-start.6
  5.9 6.3 %collective-permute-start.1 = (bf16[5,128,128]{2,1,0:T(8,128)(2,1)S(1)}, bf16[5,128,128]{2,1,0:T(8,128)(2,1)S(1)}, u32[]{:S(2)}, u32[]{:S(2)}) collective-permute-start(bf16[5,128,128]{2,1,0:T(8,128)(2,1)S(1)} %get-tuple-element.36.refs_0_), channel_id=1, source_target_pairs={{0,2},{2,0},{4,6},{6,4},{1,3},{3,1},{5,7},{7,5},{8,10},{10,8},{12,... | collective-permute-start | bytes 491528 | tf_op jit(solution)/shard_map/mid_sums/ppermute | solution.py:376
  7.5 7.2 %collective-permute-start.2 = (bf16[5,128,128]{2,1,0:T(8,128)(2,1)S(1)}, bf16[5,128,128]{2,1,0:T(8,128)(2,1)S(1)}, u32[]{:S(2)}, u32[]{:S(2)}) collective-permute-start(bf16[5,128,128]{2,1,0:T(8,128)(2,1)S(1)} %get-tuple-element.37.refs_1_), channel_id=1, source_target_pairs={{0,6},{2,4},{4,2},{6,0},{1,7},{3,5},{5,3},{7,1},{8,14},{10,12},{12... | collective-permute-start | bytes 491528 | tf_op jit(solution)/shard_map/mid_sums/ppermute | solution.py:376
  14.8 7.1 %collective-permute-start.3 = (bf16[6,128,128]{2,1,0:T(8,128)(2,1)S(1)}, bf16[6,128,128]{2,1,0:T(8,128)(2,1)S(1)}, u32[]{:S(2)}, u32[]{:S(2)}) collective-permute-start(bf16[6,128,128]{2,1,0:T(8,128)(2,1)S(1)} %get-tuple-element.39.refs_0_), channel_id=1, source_target_pairs={{0,6},{2,4},{4,2},{6,0},{1,7},{3,5},{5,3},{7,1},{8,14},{10,12},{12... | collective-permute-start | bytes 589832 | tf_op jit(solution)/shard_map/mid_sums/ppermute | solution.py:378
  17.0 5.7 %collective-permute-start.4 = (bf16[6,128,128]{2,1,0:T(8,128)(2,1)S(1)}, bf16[6,128,128]{2,1,0:T(8,128)(2,1)S(1)}, u32[]{:S(2)}, u32[]{:S(2)}) collective-permute-start(bf16[6,128,128]{2,1,0:T(8,128)(2,1)S(1)} %get-tuple-element.40.refs_1_), channel_id=1, source_target_pairs={{0,2},{2,0},{4,6},{6,4},{1,3},{3,1},{5,7},{7,5},{8,10},{10,8},{12,... | collective-permute-start | bytes 589832 | tf_op jit(solution)/shard_map/mid_sums/ppermute | solution.py:378
  22.8 1.4 %collective-permute-start.5 = (bf16[4,128,128]{2,1,0:T(8,128)(2,1)S(1)}, bf16[4,128,128]{2,1,0:T(8,128)(2,1)S(1)}, u32[]{:S(2)}, u32[]{:S(2)}) collective-permute-start(bf16[4,128,128]{2,1,0:T(8,128)(2,1)S(1)} %get-tuple-element.41.mids_ref), channel_id=1, source_target_pairs={{0,1},{1,0},{2,3},{3,2},{4,5},{5,4},{6,7},{7,6},{8,9},{9,8},{10,11... | collective-permute-start | bytes 393224 | tf_op jit(solution)/shard_map/mid_sums/ppermute | solution.py:25
  25.0 1.4 %copy-start = (bf16[8,1168,128]{2,1,0:T(8,128)(2,1)}, bf16[8,1168,128]{2,1,0:T(8,128)(2,1)S(1)}, u32[]{:S(2)}) copy-start(bf16[8,1168,128]{2,1,0:T(8,128)(2,1)S(1)} %products.1) | copy-start | bytes 7176196
  26.4 6.0 %copy-start.7 = (bf16[8,128,128]{2,1,0:T(8,128)(2,1)S(1)}, bf16[8,128,128]{2,1,0:T(8,128)(2,1)}, u32[]{:S(2)}) copy-start(bf16[8,128,128]{2,1,0:T(8,128)(2,1)} %get-tuple-element.45.picked_ref) | copy-start | bytes 786436
  26.4 35.1 %all-to-all-start = ((bf16[8,1168,128]{2,1,0:T(8,128)(2,1)}), bf16[8,1168,128]{2,1,0:T(8,128)(2,1)S(1)}, u32[]{:S(2)}, u32[]{:S(2)}) async-start(bf16[8,1168,128]{2,1,0:T(8,128)(2,1)} %copy-done), calls=%async_computation | async-start | bytes 4784128 | tf_op jit(solution)/shard_map/terms_over_first/all_to_all | solution.py:384
  32.4 1.6 %copy-start.2 = (bf16[1024,1024]{1,0:T(8,128)(2,1)S(1)}, bf16[1024,1024]{1,0:T(8,128)(2,1)}, u32[]{:S(2)}) copy-start(bf16[1024,1024]{1,0:T(8,128)(2,1)} %tokens_ref.3) | copy-start | bytes 6291460
  33.9 1.6 %copy-start.4 = (bf16[1024,1024]{1,0:T(8,128)(2,1)S(1)}, bf16[1024,1024]{1,0:T(8,128)(2,1)}, u32[]{:S(2)}) copy-start(bf16[1024,1024]{1,0:T(8,128)(2,1)} %weight_ref.1) | copy-start | bytes 6291460
  40.0 4.2 %collective-permute-start.6 = (f32[4,128,1024]{2,1,0:T(8,128)S(1)}, f32[4,128,1024]{2,1,0:T(8,128)S(1)}, u32[]{:S(2)}, u32[]{:S(2)}) collective-permute-start(f32[4,128,1024]{2,1,0:T(8,128)S(1)} %get-tuple-element.47), channel_id=1, source_target_pairs={{0,1},{1,0},{2,3},{3,2},{4,5},{5,4},{6,7},{7,6},{8,9},{9,8},{10,11... | collective-permute-start | bytes 6291464 | tf_op jit(solution)/shard_map/keys_core/ppermute | solution.py:25
  44.5 0.8 copy-start.11
  45.3 0.8 copy-start.13
  63.2 1.0 copy-start.3
  64.3 10.0 %copy-start.14 = (f32[128,1024]{1,0:T(8,128)S(1)}, f32[128,1024]{1,0:T(8,128)}, u32[]{:S(2)}) copy-start(f32[128,1024]{1,0:T(8,128)} %copy-done.13) | copy-start | bytes 1572868
  64.3 10.2 %copy-start.12 = (f32[128,1024]{1,0:T(8,128)S(1)}, f32[128,1024]{1,0:T(8,128)}, u32[]{:S(2)}) copy-start(f32[128,1024]{1,0:T(8,128)} %copy-done.11) | copy-start | bytes 1572868
  64.3 40.4 %all-to-all-start.1 = ((bf16[32,144,128]{2,1,0:T(8,128)(2,1)}), bf16[32,144,128]{2,1,0:T(8,128)(2,1)S(1)}, u32[]{:S(2)}, u32[]{:S(2)}) async-start(bf16[32,144,128]{2,1,0:T(8,128)(2,1)} %copy-done.3), calls=%async_computation.1 | async-start | bytes 2359296 | tf_op jit(solution)/shard_map/sums_over_adapter/all_to_all | solution.py:398
  74.2 24.9 %collective-permute-start.7 = (f32[128,1024]{1,0:T(8,128)S(1)}, f32[128,1024]{1,0:T(8,128)S(1)}, u32[]{:S(2)}, u32[]{:S(2)}) collective-permute-start(f32[128,1024]{1,0:T(8,128)S(1)} %copy-done.14), channel_id=1, source_target_pairs={{0,2},{2,4},{4,6},{6,0},{1,3},{3,5},{5,7},{7,1},{8,10},{10,12},{12... | collective-permute-start | bytes 1572872 | tf_op jit(solution)/shard_map/keys_y/ppermute | solution.py:25
  74.4 24.7 %collective-permute-start.8 = (f32[128,1024]{1,0:T(8,128)S(1)}, f32[128,1024]{1,0:T(8,128)S(1)}, u32[]{:S(2)}, u32[]{:S(2)}) collective-permute-start(f32[128,1024]{1,0:T(8,128)S(1)} %copy-done.12), channel_id=1, source_target_pairs={{0,4},{2,6},{4,0},{6,2},{1,5},{3,7},{5,1},{7,3},{8,12},{10,14},{12... | collective-permute-start | bytes 1572872 | tf_op jit(solution)/shard_map/keys_y/ppermute | solution.py:25
  77.1 22.6 %collective-permute-start.9 = (f32[128,1024]{1,0:T(8,128)S(1)}, f32[128,1024]{1,0:T(8,128)S(1)}, u32[]{:S(2)}, u32[]{:S(2)}) collective-permute-start(f32[128,1024]{1,0:T(8,128)S(1)} %get-tuple-element.55), channel_id=1, source_target_pairs={{0,6},{2,0},{4,2},{6,4},{1,7},{3,1},{5,3},{7,5},{8,14},{10,8},{12,... | collective-permute-start | bytes 1572872 | tf_op jit(solution)/shard_map/keys_y/ppermute | solution.py:25

commit v8 on v7

--- a/solution.py
+++ b/solution.py
@@ -269,7 +269,8 @@
     nx, nq, npair, height, rank = owned.shape
     parts, split = nx * npair, height - part
 
-    def kernel(owned_ref, down_ref, up_ref):
+    def kernel(owned_ref, down_out, up_out, down_ref, up_ref, sems):
+        leaving = []
         for x in range(nx):
             for p in range(npair):
                 total = owned_ref[x, 0, p].astype(F32)
@@ -278,6 +279,15 @@
                 total = ADAPTER_SCALE * total
                 down_ref[x * npair + p] = total[:part]
                 up_ref[x * npair + p] = total[part:]
+            pieces = slice(x * npair, (x + 1) * npair)
+            for i, (source, target) in enumerate(((down_ref, down_out), (up_ref, up_out))):
+                copy = pltpu.make_async_copy(
+                    source.at[pieces], target.at[pieces], sems.at[2 * x + i]
+                )
+                copy.start()
+                leaving.append(copy)
+        for copy in leaving:
+            copy.wait()
 
     return pl.pallas_call(
         kernel,
@@ -286,7 +296,12 @@
             jax.ShapeDtypeStruct((parts, split, rank), F32),
         ],
         in_specs=[VMEM],
-        out_specs=[VMEM, VMEM],
+        out_specs=[HBM, HBM],
+        scratch_shapes=[
+            pltpu.VMEM((parts, part, rank), F32),
+            pltpu.VMEM((parts, split, rank), F32),
+            pltpu.SemaphoreType.DMA((2 * nx,)),
+        ],
         compiler_params=LIMIT,
         name="finish",
     )(owned)

time: 106 us -> 106 us (level)
  no operation moved by 1% of the time
where the time goes in v8:
time: 106 us
  waiting for transfers between devices  57.8 us (55%)
  starting transfers between devices  25.6 us (24%)
  Pallas kernels  12 us (11%)
  local copies, waits for them, and re-layouts  8.2 us (8%)
  other arithmetic  1.12 us (1%)
    ppermute x6, waiting for transfers between devices, shift(): lax.ppermute(value, axis, [(i, (i + distance) % size) for i in range(size)])  27.6 us
    all_to_all x1, waiting for transfers between devices, per_device(): lax.all_to_all(terms, FIRST, split_axis=0, concat_axis=0, tiled=True)  15.4 us
    all_to_all x1, starting transfers between devices, per_device(): lax.all_to_all(sums, ADAPTER, split_axis=0, concat_axis=0, tiled=True)  9.96 us
    unnamed x30, local copies, waits for them, and re-layouts  8.2 us
    all_to_all x1, starting transfers between devices, per_device(): lax.all_to_all(terms, FIRST, split_axis=0, concat_axis=0, tiled=True)  5.89 us
    ppermute x1, waiting for transfers between devices, per_device(): lax.ppermute(sent[0], 'y', mirror)  4.82 us
    pallas_call x1, Pallas kernels, keys_partials(): pl.pallas_call(kernel, grid_spec=pltpu.PrefetchScalarGridSpec(num_scalar_...  4.47 us
    all_to_all x1, waiting for transfers between devices, per_device(): lax.all_to_all(sums, ADAPTER, split_axis=0, concat_axis=0, tiled=True)  4.1 us
  transfers between devices with their start and end apart: 12, of which 11 were waited for; matrix products, arithmetic and copies ran while one was open for 1% of the time, Pallas kernels for 5%

profile of v8, /device:TPU:32, one launch (start us, length us, event | category | flops | bytes accessed | tf_op | source)
XLA Modules:
  0.0 105.6 jit_solution(7450806605168020504)
XLA Ops:
  0.7 3.2 %mid_partials.1 = (f32[5,128,128]{2,1,0:T(8,128)}, f32[5,128,128]{2,1,0:T(8,128)}, bf16[8,128,128]{2,1,0:T(8,128)(2,1)}) custom-call(s32[8]{0:T(128)} %bitcast.7, s32[8]{0:T(128)} %fill_ref.3, bf16[32,128,128]{2,1,0:T(8,128)(2,1)} %up_ref.1, bf16[1024,128]{1,0:T(8,128)(2,1)} %cot_ref.3, bf16[128,128]{1,0:T(8,128)(2,1)} %saved_ref.1), custom_call_target="tpu_custom_call" | custom-call | tf_op jit(solution)/shard_map/mid_sums/mid_partials/pallas_call | solution.py:70
  4.0 1.0 copy-done.6
  5.0 0.8 collective-permute-done.received_ref
  5.9 1.7 %collective-permute-start.1 = (bf16[5,128,128]{2,1,0:T(8,128)(2,1)S(1)}, bf16[5,128,128]{2,1,0:T(8,128)(2,1)S(1)}, u32[]{:S(2)}, u32[]{:S(2)}) collective-permute-start(bf16[5,128,128]{2,1,0:T(8,128)(2,1)S(1)} %get-tuple-element.36.refs_0_), channel_id=1, source_target_pairs={{0,2},{2,0},{4,6},{6,4},{1,3},{3,1},{5,7},{7,5},{8,10},{10,8},{12,... | collective-permute-start | bytes 491528 | tf_op jit(solution)/shard_map/mid_sums/ppermute | solution.py:391
  7.5 2.2 %collective-permute-start.2 = (bf16[5,128,128]{2,1,0:T(8,128)(2,1)S(1)}, bf16[5,128,128]{2,1,0:T(8,128)(2,1)S(1)}, u32[]{:S(2)}, u32[]{:S(2)}) collective-permute-start(bf16[5,128,128]{2,1,0:T(8,128)(2,1)S(1)} %get-tuple-element.37.refs_1_), channel_id=1, source_target_pairs={{0,6},{2,4},{4,2},{6,0},{1,7},{3,5},{5,3},{7,1},{8,14},{10,12},{12... | collective-permute-start | bytes 491528 | tf_op jit(solution)/shard_map/mid_sums/ppermute | solution.py:391
  9.7 2.5 %collective-permute-done.1.refs_2_ = bf16[5,128,128]{2,1,0:T(8,128)(2,1)S(1)} collective-permute-done((bf16[5,128,128]{2,1,0:T(8,128)(2,1)S(1)}, bf16[5,128,128]{2,1,0:T(8,128)(2,1)S(1)}, u32[]{:S(2)}, u32[]{:S(2)}) %collective-permute-start.1) | collective-permute-done | bytes 163872 | tf_op jit(solution)/shard_map/mid_sums/ppermute | solution.py:391
  12.2 2.5 %collective-permute-done.2.refs_3_ = bf16[5,128,128]{2,1,0:T(8,128)(2,1)S(1)} collective-permute-done((bf16[5,128,128]{2,1,0:T(8,128)(2,1)S(1)}, bf16[5,128,128]{2,1,0:T(8,128)(2,1)S(1)}, u32[]{:S(2)}, u32[]{:S(2)}) %collective-permute-start.2) | collective-permute-done | bytes 163872 | tf_op jit(solution)/shard_map/mid_sums/ppermute | solution.py:391
  14.8 2.3 %collective-permute-start.3 = (bf16[6,128,128]{2,1,0:T(8,128)(2,1)S(1)}, bf16[6,128,128]{2,1,0:T(8,128)(2,1)S(1)}, u32[]{:S(2)}, u32[]{:S(2)}) collective-permute-start(bf16[6,128,128]{2,1,0:T(8,128)(2,1)S(1)} %get-tuple-element.39.refs_0_), channel_id=1, source_target_pairs={{0,6},{2,4},{4,2},{6,0},{1,7},{3,5},{5,3},{7,1},{8,14},{10,12},{12... | collective-permute-start | bytes 589832 | tf_op jit(solution)/shard_map/mid_sums/ppermute | solution.py:393
  17.0 4.8 %collective-permute-done.3.refs_2_ = bf16[6,128,128]{2,1,0:T(8,128)(2,1)S(1)} collective-permute-done((bf16[6,128,128]{2,1,0:T(8,128)(2,1)S(1)}, bf16[6,128,128]{2,1,0:T(8,128)(2,1)S(1)}, u32[]{:S(2)}, u32[]{:S(2)}) %collective-permute-start.3) | collective-permute-done | bytes 196640 | tf_op jit(solution)/shard_map/mid_sums/ppermute | solution.py:393
  21.9 0.8 collective-permute-done.4.refs_3_
  22.9 0.8 up_products.1
  23.7 0.5 collective-permute-done.5.other_ref
  24.2 0.8 products.1
  25.0 1.4 %copy-done = bf16[8,1168,128]{2,1,0:T(8,128)(2,1)} copy-done((bf16[8,1168,128]{2,1,0:T(8,128)(2,1)}, bf16[8,1168,128]{2,1,0:T(8,128)(2,1)S(1)}, u32[]{:S(2)}) %copy-start) | copy-done | bytes 2392088
  26.4 5.9 %all-to-all-start = ((bf16[8,1168,128]{2,1,0:T(8,128)(2,1)}), bf16[8,1168,128]{2,1,0:T(8,128)(2,1)S(1)}, u32[]{:S(2)}, u32[]{:S(2)}) async-start(bf16[8,1168,128]{2,1,0:T(8,128)(2,1)} %copy-done), calls=%async_computation | async-start | bytes 4784128 | tf_op jit(solution)/shard_map/terms_over_first/all_to_all | solution.py:399
  32.4 1.6 %copy-done.2 = bf16[1024,1024]{1,0:T(8,128)(2,1)S(1)} copy-done((bf16[1024,1024]{1,0:T(8,128)(2,1)S(1)}, bf16[1024,1024]{1,0:T(8,128)(2,1)}, u32[]{:S(2)}) %copy-start.2) | copy-done | bytes 2097176
  33.9 1.6 %copy-done.4 = bf16[1024,1024]{1,0:T(8,128)(2,1)S(1)} copy-done((bf16[1024,1024]{1,0:T(8,128)(2,1)S(1)}, bf16[1024,1024]{1,0:T(8,128)(2,1)}, u32[]{:S(2)}) %copy-start.4) | copy-done | bytes 2097176
  35.5 4.5 %keys_partials.1 = (f32[4,128,1024]{2,1,0:T(8,128)S(1)}, f32[4,128,1024]{2,1,0:T(8,128)S(1)}) custom-call(s32[2]{0:T(128)S(1)} %pad_add_fusion.place_ref, bf16[1024,1024]{1,0:T(8,128)(2,1)S(1)} %copy-done.2, bf16[1024,1024]{1,0:T(8,128)(2,1)S(1)} %copy-done.4, bf16[8,128,128]{2,1,0:T(8,128)(2,1)S(1)} %get-tuple-element.42.saved_ref, ...), custom_call_target="tpu_custom_call" | custom-call | tf_op jit(solution)/shard_map/keys_core/keys_partials/pallas_call | solution.py:331
  40.1 4.1 %collective-permute-done.6.received_ref = f32[4,128,1024]{2,1,0:T(8,128)S(1)} collective-permute-done((f32[4,128,1024]{2,1,0:T(8,128)S(1)}, f32[4,128,1024]{2,1,0:T(8,128)S(1)}, u32[]{:S(2)}, u32[]{:S(2)}) %collective-permute-start.6) | collective-permute-done | bytes 2097184 | tf_op jit(solution)/shard_map/keys_core/ppermute | solution.py:25
  44.5 0.8 copy-done.11
  45.3 0.8 copy-done.13
  46.1 15.4 %all-to-all-done.terms_ref = bf16[8,1168,128]{2,1,0:T(8,128)(2,1)S(1)} async-done(((bf16[8,1168,128]{2,1,0:T(8,128)(2,1)}), bf16[8,1168,128]{2,1,0:T(8,128)(2,1)S(1)}, u32[]{:S(2)}, u32[]{:S(2)}) %all-to-all-start) | async-done | bytes 2392096 | tf_op jit(solution)/shard_map/terms_over_first/all_to_all | solution.py:399
  61.7 1.5 %slot_sums.1 = bf16[32,144,128]{2,1,0:T(8,128)(2,1)S(1)} custom-call(s32[8,8]{1,0:T(8,128)S(1)} %convert_reduce_fusion.slots_ref, bf16[8,1168,128]{2,1,0:T(8,128)(2,1)S(1)} %all-to-all-done.terms_ref), custom_call_target="tpu_custom_call" | custom-call | tf_op jit(solution)/shard_map/sums_over_adapter/slot_sums/pallas_call | solution.py:257
  63.2 1.0 copy-done.3
  64.3 10.0 %all-to-all-start.1 = ((bf16[32,144,128]{2,1,0:T(8,128)(2,1)}), bf16[32,144,128]{2,1,0:T(8,128)(2,1)S(1)}, u32[]{:S(2)}, u32[]{:S(2)}) async-start(bf16[32,144,128]{2,1,0:T(8,128)(2,1)} %copy-done.3), calls=%async_computation.1 | async-start | bytes 2359296 | tf_op jit(solution)/shard_map/sums_over_adapter/all_to_all | solution.py:413
  74.4 2.7 %collective-permute-start.8 = (f32[128,1024]{1,0:T(8,128)S(1)}, f32[128,1024]{1,0:T(8,128)S(1)}, u32[]{:S(2)}, u32[]{:S(2)}) collective-permute-start(f32[128,1024]{1,0:T(8,128)S(1)} %copy-done.12), channel_id=1, source_target_pairs={{0,4},{2,6},{4,0},{6,2},{1,5},{3,7},{5,1},{7,3},{8,12},{10,14},{12... | collective-permute-start | bytes 1572872 | tf_op jit(solution)/shard_map/keys_y/ppermute | solution.py:25
  77.1 0.5 collective-permute-start.9
  77.6 21.5 %collective-permute-done.7 = f32[128,1024]{1,0:T(8,128)S(1)} collective-permute-done((f32[128,1024]{1,0:T(8,128)S(1)}, f32[128,1024]{1,0:T(8,128)S(1)}, u32[]{:S(2)}, u32[]{:S(2)}) %collective-permute-start.7) | collective-permute-done | bytes 524320 | tf_op jit(solution)/shard_map/keys_y/ppermute | solution.py:25
  99.1 0.6 collective-permute-done.9
  99.7 0.8 add_convert_fusion
  100.6 4.1 %all-to-all-done.1 = bf16[32,144,128]{2,1,0:T(8,128)(2,1)S(1)} async-done(((bf16[32,144,128]{2,1,0:T(8,128)(2,1)}), bf16[32,144,128]{2,1,0:T(8,128)(2,1)S(1)}, u32[]{:S(2)}, u32[]{:S(2)}) %all-to-all-start.1) | async-done | bytes 1179680 | tf_op jit(solution)/shard_map/sums_over_adapter/all_to_all | solution.py:413
  104.7 0.9 finish.1
  (36 shorter events, 1.2 us)
Async XLA Ops:
  0.6 22.2 %copy-start.8 = (s32[8,1]{0,1:T(1,128)S(1)}, s32[8,1]{0,1:T(1,128)}, u32[]{:S(2)}) copy-start(s32[8,1]{0,1:T(1,128)} %param.13) | copy-start | bytes 100
  0.6 22.2 %copy-start.9 = (s32[8]{0:T(128)S(1)}, s32[8]{0:T(128)}, u32[]{:S(2)}) copy-start(s32[8]{0:T(128)} %fill_ref.3) | copy-start | bytes 100
  0.7 22.2 %copy-start.10 = (s32[32]{0:T(128)S(1)}, s32[32]{0:T(128)}, u32[]{:S(2)}) copy-start(s32[32]{0:T(128)} %slot_ref.1) | copy-start | bytes 388
  0.7 22.2 %copy-start.5 = (bf16[1024,128]{1,0:T(8,128)(2,1)S(1)}, bf16[1024,128]{1,0:T(8,128)(2,1)}, u32[]{:S(2)}) copy-start(bf16[1024,128]{1,0:T(8,128)(2,1)} %cot_ref.3) | copy-start | bytes 786436
  0.7 23.5 %copy-start.1 = (bf16[1024,1024]{1,0:T(8,128)(2,1)S(1)}, bf16[1024,1024]{1,0:T(8,128)(2,1)}, u32[]{:S(2)}) copy-start(bf16[1024,1024]{1,0:T(8,128)(2,1)} %tokens_ref.3) | copy-start | bytes 6291460
  3.9 1.9 %collective-permute-start = (f32[5,128,128]{2,1,0:T(8,128)}, f32[5,128,128]{2,1,0:T(8,128)S(1)}, u32[]{:S(2)}, u32[]{:S(2)}) collective-permute-start(f32[5,128,128]{2,1,0:T(8,128)} %get-tuple-element.34), channel_id=1, source_target_pairs={{0,1},{1,0},{2,3},{3,2},{4,5},{5,4},{6,7},{7,6},{8,9},{9,8},{10,11... | collective-permute-start | bytes 983048 | tf_op jit(solution)/shard_map/mid_sums/ppermute | solution.py:25
  4.0 1.0 copy-start.6
  5.9 6.3 %collective-permute-start.1 = (bf16[5,128,128]{2,1,0:T(8,128)(2,1)S(1)}, bf16[5,128,128]{2,1,0:T(8,128)(2,1)S(1)}, u32[]{:S(2)}, u32[]{:S(2)}) collective-permute-start(bf16[5,128,128]{2,1,0:T(8,128)(2,1)S(1)} %get-tuple-element.36.refs_0_), channel_id=1, source_target_pairs={{0,2},{2,0},{4,6},{6,4},{1,3},{3,1},{5,7},{7,5},{8,10},{10,8},{12,... | collective-permute-start | bytes 491528 | tf_op jit(solution)/shard_map/mid_sums/ppermute | solution.py:391
  7.5 7.2 %collective-permute-start.2 = (bf16[5,128,128]{2,1,0:T(8,128)(2,1)S(1)}, bf16[5,128,128]{2,1,0:T(8,128)(2,1)S(1)}, u32[]{:S(2)}, u32[]{:S(2)}) collective-permute-start(bf16[5,128,128]{2,1,0:T(8,128)(2,1)S(1)} %get-tuple-element.37.refs_1_), channel_id=1, source_target_pairs={{0,6},{2,4},{4,2},{6,0},{1,7},{3,5},{5,3},{7,1},{8,14},{10,12},{12... | collective-permute-start | bytes 491528 | tf_op jit(solution)/shard_map/mid_sums/ppermute | solution.py:391
  14.8 7.1 %collective-permute-start.3 = (bf16[6,128,128]{2,1,0:T(8,128)(2,1)S(1)}, bf16[6,128,128]{2,1,0:T(8,128)(2,1)S(1)}, u32[]{:S(2)}, u32[]{:S(2)}) collective-permute-start(bf16[6,128,128]{2,1,0:T(8,128)(2,1)S(1)} %get-tuple-element.39.refs_0_), channel_id=1, source_target_pairs={{0,6},{2,4},{4,2},{6,0},{1,7},{3,5},{5,3},{7,1},{8,14},{10,12},{12... | collective-permute-start | bytes 589832 | tf_op jit(solution)/shard_map/mid_sums/ppermute | solution.py:393
  17.0 5.7 %collective-permute-start.4 = (bf16[6,128,128]{2,1,0:T(8,128)(2,1)S(1)}, bf16[6,128,128]{2,1,0:T(8,128)(2,1)S(1)}, u32[]{:S(2)}, u32[]{:S(2)}) collective-permute-start(bf16[6,128,128]{2,1,0:T(8,128)(2,1)S(1)} %get-tuple-element.40.refs_1_), channel_id=1, source_target_pairs={{0,2},{2,0},{4,6},{6,4},{1,3},{3,1},{5,7},{7,5},{8,10},{10,8},{12,... | collective-permute-start | bytes 589832 | tf_op jit(solution)/shard_map/mid_sums/ppermute | solution.py:393
  22.8 1.4 %collective-permute-start.5 = (bf16[4,128,128]{2,1,0:T(8,128)(2,1)S(1)}, bf16[4,128,128]{2,1,0:T(8,128)(2,1)S(1)}, u32[]{:S(2)}, u32[]{:S(2)}) collective-permute-start(bf16[4,128,128]{2,1,0:T(8,128)(2,1)S(1)} %get-tuple-element.41.mids_ref), channel_id=1, source_target_pairs={{0,1},{1,0},{2,3},{3,2},{4,5},{5,4},{6,7},{7,6},{8,9},{9,8},{10,11... | collective-permute-start | bytes 393224 | tf_op jit(solution)/shard_map/mid_sums/ppermute | solution.py:25
  25.0 1.4 %copy-start = (bf16[8,1168,128]{2,1,0:T(8,128)(2,1)}, bf16[8,1168,128]{2,1,0:T(8,128)(2,1)S(1)}, u32[]{:S(2)}) copy-start(bf16[8,1168,128]{2,1,0:T(8,128)(2,1)S(1)} %products.1) | copy-start | bytes 7176196
  26.4 6.0 %copy-start.7 = (bf16[8,128,128]{2,1,0:T(8,128)(2,1)S(1)}, bf16[8,128,128]{2,1,0:T(8,128)(2,1)}, u32[]{:S(2)}) copy-start(bf16[8,128,128]{2,1,0:T(8,128)(2,1)} %get-tuple-element.45.picked_ref) | copy-start | bytes 786436
  26.4 35.1 %all-to-all-start = ((bf16[8,1168,128]{2,1,0:T(8,128)(2,1)}), bf16[8,1168,128]{2,1,0:T(8,128)(2,1)S(1)}, u32[]{:S(2)}, u32[]{:S(2)}) async-start(bf16[8,1168,128]{2,1,0:T(8,128)(2,1)} %copy-done), calls=%async_computation | async-start | bytes 4784128 | tf_op jit(solution)/shard_map/terms_over_first/all_to_all | solution.py:399
  32.4 1.6 %copy-start.2 = (bf16[1024,1024]{1,0:T(8,128)(2,1)S(1)}, bf16[1024,1024]{1,0:T(8,128)(2,1)}, u32[]{:S(2)}) copy-start(bf16[1024,1024]{1,0:T(8,128)(2,1)} %tokens_ref.3) | copy-start | bytes 6291460
  33.9 1.6 %copy-start.4 = (bf16[1024,1024]{1,0:T(8,128)(2,1)S(1)}, bf16[1024,1024]{1,0:T(8,128)(2,1)}, u32[]{:S(2)}) copy-start(bf16[1024,1024]{1,0:T(8,128)(2,1)} %weight_ref.1) | copy-start | bytes 6291460
  40.0 4.2 %collective-permute-start.6 = (f32[4,128,1024]{2,1,0:T(8,128)S(1)}, f32[4,128,1024]{2,1,0:T(8,128)S(1)}, u32[]{:S(2)}, u32[]{:S(2)}) collective-permute-start(f32[4,128,1024]{2,1,0:T(8,128)S(1)} %get-tuple-element.47), channel_id=1, source_target_pairs={{0,1},{1,0},{2,3},{3,2},{4,5},{5,4},{6,7},{7,6},{8,9},{9,8},{10,11... | collective-permute-start | bytes 6291464 | tf_op jit(solution)/shard_map/keys_core/ppermute | solution.py:25
  44.5 0.8 copy-start.11
  45.3 0.8 copy-start.13
  63.2 1.0 copy-start.3
  64.3 10.0 %copy-start.14 = (f32[128,1024]{1,0:T(8,128)S(1)}, f32[128,1024]{1,0:T(8,128)}, u32[]{:S(2)}) copy-start(f32[128,1024]{1,0:T(8,128)} %copy-done.13) | copy-start | bytes 1572868
  64.3 10.2 %copy-start.12 = (f32[128,1024]{1,0:T(8,128)S(1)}, f32[128,1024]{1,0:T(8,128)}, u32[]{:S(2)}) copy-start(f32[128,1024]{1,0:T(8,128)} %copy-done.11) | copy-start | bytes 1572868
  64.3 40.4 %all-to-all-start.1 = ((bf16[32,144,128]{2,1,0:T(8,128)(2,1)}), bf16[32,144,128]{2,1,0:T(8,128)(2,1)S(1)}, u32[]{:S(2)}, u32[]{:S(2)}) async-start(bf16[32,144,128]{2,1,0:T(8,128)(2,1)} %copy-done.3), calls=%async_computation.1 | async-start | bytes 2359296 | tf_op jit(solution)/shard_map/sums_over_adapter/all_to_all | solution.py:413
  74.2 24.9 %collective-permute-start.7 = (f32[128,1024]{1,0:T(8,128)S(1)}, f32[128,1024]{1,0:T(8,128)S(1)}, u32[]{:S(2)}, u32[]{:S(2)}) collective-permute-start(f32[128,1024]{1,0:T(8,128)S(1)} %copy-done.14), channel_id=1, source_target_pairs={{0,2},{2,4},{4,6},{6,0},{1,3},{3,5},{5,7},{7,1},{8,10},{10,12},{12... | collective-permute-start | bytes 1572872 | tf_op jit(solution)/shard_map/keys_y/ppermute | solution.py:25
  74.4 24.7 %collective-permute-start.8 = (f32[128,1024]{1,0:T(8,128)S(1)}, f32[128,1024]{1,0:T(8,128)S(1)}, u32[]{:S(2)}, u32[]{:S(2)}) collective-permute-start(f32[128,1024]{1,0:T(8,128)S(1)} %copy-done.12), channel_id=1, source_target_pairs={{0,4},{2,6},{4,0},{6,2},{1,5},{3,7},{5,1},{7,3},{8,12},{10,14},{12... | collective-permute-start | bytes 1572872 | tf_op jit(solution)/shard_map/keys_y/ppermute | solution.py:25
  77.1 22.6 %collective-permute-start.9 = (f32[128,1024]{1,0:T(8,128)S(1)}, f32[128,1024]{1,0:T(8,128)S(1)}, u32[]{:S(2)}, u32[]{:S(2)}) collective-permute-start(f32[128,1024]{1,0:T(8,128)S(1)} %get-tuple-element.55), channel_id=1, source_target_pairs={{0,6},{2,0},{4,2},{6,4},{1,7},{3,1},{5,3},{7,5},{8,14},{10,8},{12,... | collective-permute-start | bytes 1572872 | tf_op jit(solution)/shard_map/keys_y/ppermute | solution.py:25
